TPU v7x, 32 devices: a whole 2x2x4 slice. The times are simulated.
32 devices in a mesh: tile: 8 (over z, x), member: 4 (over y, core).
Axes of the slice: x: 2, y: 2, z: 4, core: 2. Of those that a mesh axis runs over, the one named last changes fastest.
Arguments:
- log_perm: float32 [128, 4, 64, 256], P('member', None, 'tile'), may hold values from -3.4 to 3.4
- start_pressure: float32 [4, 64, 256], P(None, 'tile'), may hold values from -5 to 5
- start_sat: float32 [4, 64, 256], P(None, 'tile'), may hold values from 0.1 to 0.9
- source: float32 [4, 64, 256], P(None, 'tile'), may hold values from -5 to 5
- storage: float32 [4, 64, 256], P(None, 'tile'), may hold values from 0.05 to 0.5
- well_press: float32 [256], replicated, may hold values from -4 to 4
- perf_cell: int32 [2048], P('tile'), may hold values from 0 to 8191
- perf_well: int32 [2048], P('tile'), may hold values from 0 to 255
- perf_count: int32 [8], P('tile'), may hold values from 64 to 256, as said below
- observed: float32 [256], replicated, may hold values from -8 to 8
- obs_var: float32 [256], replicated, may hold values from 0.5 to 5
- obs_noise: float32 [128, 256], P('member'), may hold values from -5 to 5
Outputs:
- new_log_perm: float32 [128, 4, 64, 256], P('member', None, 'tile')
- pressure: float32 [128, 4, 64, 256], P('member', None, 'tile')
- saturation: float32 [128, 4, 64, 256], P('member', None, 'tile')
- well_rates: float32 [128, 256], P('member', 'tile')
Inputs may be any that keep to these rules, and one draw needn't show every extreme that they name: `perf_count`: one strip has all 256 slots live.
All inputs are finite; a program needn't handle non-finite values.
Results may differ from a plain program's by a relative error of at most 0.017.
Values may be sent and summed in bfloat16 or wider, within the bound.
No kernel may reach another device: no remote copies, remote signals or barrier semaphores. Data moves between devices by JAX's collectives and lax.ppermute only.
A program may use at most 64 MiB of HBM per device.

v0:
```python
import functools

import jax
import jax.numpy as jnp
from jax import lax
from jax.experimental import pallas as pl
from jax.experimental.pallas import tpu as pltpu
from jax.sharding import PartitionSpec as P

SWEEPS = 2
RIM = SWEEPS + 1


VERTICAL = 0.5
VISCOSITY_RATIO = 2.0
STEP_COEF = 0.1
INFLATION = 4.0
PANEL = 8
GROUP = 16
LANES = 128


def fold(array):
    members, layers, width, depth = array.shape
    array = array.reshape(members, layers, width, depth // LANES, LANES)
    return array.transpose(0, 1, 3, 2, 4).reshape(-1, LANES)


def unfold(rows, shape):
    members, layers, width, depth = shape
    array = rows.reshape(members, layers, depth // LANES, width, LANES)
    return array.transpose(0, 1, 3, 2, 4).reshape(shape)


def load_rows(ref, count, layer, x, layers, width, halves):
    return jnp.concatenate(
        [
            ref[pl.ds((layer * halves + h) * width + x, count, stride=layers * width * halves), :]
            for h in range(halves)
        ],
        axis=1,
    )


def store_rows(ref, values, count, layer, x, layers, width, halves):
    for h in range(halves):
        at = pl.ds((layer * halves + h) * width + x, count, stride=layers * width * halves)
        ref[at, :] = values[:, h * LANES : (h + 1) * LANES]


def send_both(up_rows, down_rows, axis):
    count = lax.axis_size(axis)
    forward = [(i, i + 1) for i in range(count - 1)]
    backward = [(target, source) for source, target in forward]
    return lax.ppermute(up_rows, axis, forward), lax.ppermute(down_rows, axis, backward)


def reciprocal(values_in):
    guess = pl.reciprocal(values_in, approx=True)
    return guess * (2.0 - values_in * guess)


def water_frac(values_in):
    squared = values_in * values_in
    rest = 1.0 - values_in
    return squared * reciprocal(squared + VISCOSITY_RATIO * rest * rest)


def pack_kernel(dims, root, perm_ref, *refs):
    local_count, layers, width = dims
    field_refs, (up_ref, down_ref, anomaly_ref, up_rows, down_rows) = refs[:4], refs[4:]
    up_rows[...] = jnp.zeros_like(up_rows)
    down_rows[...] = jnp.zeros_like(down_rows)
    for f, field_ref in enumerate(field_refs):
        for layer in range(layers):
            at = f * GROUP + layer * RIM
            first = layer * width
            down_rows[at : at + RIM, :] = field_ref[first : first + RIM, :]
            up_rows[at : at + RIM, :] = field_ref[first + width - RIM : first + width, :]
    halves = anomaly_ref.shape[1] // LANES
    block = RIM * layers * local_count
    up_ref[block:, :] = up_rows[...].astype(jnp.bfloat16)
    down_ref[block:, :] = down_rows[...].astype(jnp.bfloat16)
    for layer in range(layers):
        for x in range(width):
            row = layer * width + x
            values = load_rows(perm_ref, local_count, layer, x, layers, width, halves)
            anomaly_ref[row * local_count : (row + 1) * local_count, :] = (values / root).astype(
                jnp.bfloat16
            )
            low_values = values.astype(jnp.bfloat16)
            if x < RIM:
                at = (x * layers + layer) * local_count
                down_ref[at : at + local_count, :] = low_values
            if x >= width - RIM:
                at = ((x - width + RIM) * layers + layer) * local_count
                up_ref[at : at + local_count, :] = low_values


def physics_kernel(dims, count_ref, rank_ref, perm_ref, low_ref, high_ref, *refs):
    local_count, layers, width, tile_count = dims
    own_refs = refs[:4]
    cell_ref, well_ref, bhp_ref, press_ref, sat_ref, rates_ref, half_inv, face_y = refs[4:12]
    face_x, face_z, inverse, first_press, last_press = refs[12:]
    depth = low_ref.shape[1]
    halves = depth // LANES
    group = pl.program_id(0)
    rim_rows = RIM * layers * local_count
    lane = lax.broadcasted_iota(jnp.int32, (1, depth), 1)
    open_y = (lane < depth - 1).astype(jnp.float32)
    has_low = (rank_ref[0] > 0).astype(jnp.float32)
    has_high = (rank_ref[0] < tile_count - 1).astype(jnp.float32)
    span = width + 2 * RIM

    def slot(r, layer):
        return (r + RIM) * layers + layer

    def ahead(values_in):
        return pltpu.roll(values_in, depth - 1, 1)

    def behind(values_in):
        return pltpu.roll(values_in, 1, 1)

    own = [ref[...] for ref in own_refs]
    rims = [
        [
            ref[rim_rows + f * GROUP : rim_rows + (f + 1) * GROUP, :].astype(jnp.float32)
            for f in range(4)
        ]
        for ref in (low_ref, high_ref)
    ]

    def with_shifts(p0, sat, source, storage):
        frac = water_frac(sat)
        return dict(
            p0=p0, sat=sat, storage=storage, base=source + storage * p0,
            ahead=ahead(p0), behind=behind(p0), frac=frac, frac_ahead=ahead(frac),
        )

    shared = [with_shifts(*fields) for fields in (own, rims[0], rims[1])]

    def field(name, r, layer):
        if 0 <= r < width:
            part, at = shared[0], layer * width + r
        elif r < 0:
            part, at = shared[1], layer * RIM + r + RIM
        else:
            part, at = shared[2], layer * RIM + r - width
        return part[name][at : at + 1, :]

    for r in range(-RIM, width + RIM):
        for layer in range(layers):
            if 0 <= r < width:
                values = load_rows(perm_ref, GROUP, layer, r, layers, width, halves)
            else:
                ref, i = (low_ref, r + RIM) if r < 0 else (high_ref, r - width)
                at = (i * layers + layer) * local_count + group * GROUP
                values = ref[pl.ds(pl.multiple_of(at, GROUP), GROUP), :].astype(jnp.float32)
            half_inv[slot(r, layer)] = 0.5 * jnp.exp(-values)

    for r in range(-RIM, width + RIM - 1):
        for layer in range(layers):
            face = reciprocal(half_inv[slot(r, layer)] + half_inv[slot(r + 1, layer)])
            if r == -1:
                face = face * has_low
            if r == width - 1:
                face = face * has_high
            face_x[slot(r, layer)] = face

    for r in range(1 - RIM, width + RIM - 1):
        for layer in range(layers):
            at = slot(r, layer)
            here = half_inv[at]
            up_y = reciprocal(here + ahead(here)) * open_y
            low_y = behind(up_y)
            face_y[at] = up_y
            low_x, up_x = face_x[slot(r - 1, layer)], face_x[at]
            flow = (
                low_x * field("p0", r - 1, layer)
                + up_x * field("p0", r + 1, layer)
                + up_y * field("ahead", r, layer)
                + low_y * field("behind", r, layer)
            )
            weight = (low_x + up_x) + (up_y + low_y)
            if layer + 1 < layers:
                up_z = VERTICAL * reciprocal(here + half_inv[slot(r, layer + 1)])
                face_z[at] = up_z
                flow = flow + up_z * field("p0", r, layer + 1)
                weight = weight + up_z
            if layer > 0:
                low_z = face_z[slot(r, layer - 1)]
                flow = flow + low_z * field("p0", r, layer - 1)
                weight = weight + low_z
            scale = reciprocal(field("storage", r, layer) + weight)
            inverse[at] = scale
            first_press[at] = (field("base", r, layer) + flow) * scale

    for r in range(-1, width + 1):
        for layer in range(layers):
            at = slot(r, layer)
            here = first_press[at]
            up_y = face_y[at]
            flow = (
                face_x[slot(r - 1, layer)] * first_press[slot(r - 1, layer)]
                + face_x[at] * first_press[slot(r + 1, layer)]
                + up_y * ahead(here)
                + behind(up_y * here)
            )
            if layer + 1 < layers:
                flow = flow + face_z[at] * first_press[slot(r, layer + 1)]
            if layer > 0:
                flow = flow + face_z[slot(r, layer - 1)] * first_press[slot(r, layer - 1)]
            last_press[at] = (field("base", r, layer) + flow) * inverse[at]

    perf_cell = cell_ref[...]
    slots = perf_cell.shape[1]
    parts = slots // LANES
    lane_at = perf_cell % LANES
    row_at = perf_cell // LANES
    lane_of = [
        jnp.broadcast_to(lane_at[:, p * LANES : (p + 1) * LANES], (GROUP, LANES))
        for p in range(parts)
    ]
    row_of = [
        jnp.broadcast_to(row_at[:, p * LANES : (p + 1) * LANES], (GROUP, LANES))
        for p in range(parts)
    ]
    zeros = jnp.zeros((GROUP, LANES), jnp.float32)
    perf_mob, perf_press = [zeros] * parts, [zeros] * parts

    def carried(face, low_press, up_press, low_frac, up_frac):
        velocity = face * (low_press - up_press)
        return velocity * jnp.where(velocity > 0, low_frac, up_frac)

    for layer in range(layers):
        low_x = carried(
            face_x[slot(-1, layer)], last_press[slot(-1, layer)], last_press[slot(0, layer)],
            field("frac", -1, layer), field("frac", 0, layer),
        )
        for r in range(width):
            at = slot(r, layer)
            here = last_press[at]
            frac = field("frac", r, layer)
            up_x = carried(
                face_x[at], here, last_press[slot(r + 1, layer)], frac, field("frac", r + 1, layer)
            )
            up_y = carried(face_y[at], here, ahead(here), frac, field("frac_ahead", r, layer))
            change = (low_x - up_x) + (behind(up_y) - up_y)
            low_x = up_x
            if layer + 1 < layers:
                up_z = carried(
                    face_z[at], here, last_press[slot(r, layer + 1)], frac,
                    field("frac", r, layer + 1),
                )
                change = change - up_z
                first_press[at] = up_z
            if layer > 0:
                change = change + first_press[slot(r, layer - 1)]
            saturation = field("sat", r, layer) + STEP_COEF * change
            row = layer * width + r
            store_rows(press_ref, here, GROUP, layer, r, layers, width, halves)
            store_rows(sat_ref, saturation, GROUP, layer, r, layers, width, halves)
            mobility = water_frac(saturation) * reciprocal(2.0 * half_inv[at])
            for half in range(halves):
                mob_part = mobility[:, half * LANES : (half + 1) * LANES]
                press_part = here[:, half * LANES : (half + 1) * LANES]
                for p in range(parts):
                    mine = row_of[p] == row * halves + half
                    perf_mob[p] = jnp.where(
                        mine, jnp.take_along_axis(mob_part, lane_of[p], axis=1, mode="promise_in_bounds"), perf_mob[p]
                    )
                    perf_press[p] = jnp.where(
                        mine,
                        jnp.take_along_axis(press_part, lane_of[p], axis=1, mode="promise_in_bounds"),
                        perf_press[p],
                    )

    wells = bhp_ref.shape[1]
    chosen = (
        lax.broadcasted_iota(jnp.int32, (wells, slots), 0) == well_ref[...]
    ).astype(jnp.float32)
    bhp = jnp.broadcast_to(bhp_ref[...], (8, wells))
    perf_bhp = jnp.dot(
        bhp, chosen, precision=lax.Precision.HIGHEST, preferred_element_type=jnp.float32
    )[:1]
    live = (lax.broadcasted_iota(jnp.int32, (1, slots), 1) < count_ref[0]).astype(jnp.float32)
    terms = (
        jnp.concatenate(perf_mob, axis=1)
        * (jnp.concatenate(perf_press, axis=1) - perf_bhp)
        * live
    )
    partial_rates = lax.dot_general(
        terms, chosen, (((1,), (1,)), ((), ())), precision=lax.Precision.HIGHEST,
        preferred_element_type=jnp.float32,
    )
    rates_ref[...] = jnp.broadcast_to(partial_rates[None], rates_ref.shape)


def invert_panel(columns):
    row = lax.broadcasted_iota(jnp.int32, columns[0].shape, 0)
    columns = list(columns)
    for k in range(PANEL):
        inverse = 1.0 / columns[k][k : k + 1]
        pivot = columns[k]
        for j in range(PANEL):
            if j != k:
                factor = columns[j][k : k + 1] * inverse
                columns[j] = jnp.where(row == k, factor, columns[j] - pivot * factor)
        columns[k] = jnp.where(row == k, inverse, -pivot * inverse)
    return columns


def solve_blocks(gram_matrix, cross_matrix):
    size = gram_matrix.shape[0]
    count = size // PANEL
    row = lax.broadcasted_iota(jnp.int32, gram_matrix.shape, 0)
    lane = lax.broadcasted_iota(jnp.int32, gram_matrix.shape, 1)
    full = gram_matrix + (row == lane).astype(jnp.float32)
    left = [full[i * PANEL : (i + 1) * PANEL] for i in range(count)]
    right = [cross_matrix[i * PANEL : (i + 1) * PANEL] for i in range(count)]
    width = cross_matrix.shape[1]
    for p in range(count):
        columns = [
            [
                jnp.broadcast_to(left[i][:, p * PANEL + j : p * PANEL + j + 1], (PANEL, size))
                for j in range(PANEL)
            ]
            for i in range(count)
        ]
        inverse = invert_panel(columns[p])
        new_left = sum(inverse[j] * left[p][j : j + 1] for j in range(PANEL))
        new_right = sum(inverse[j][:, :width] * right[p][j : j + 1] for j in range(PANEL))
        for i in range(count):
            if i != p:
                for j in range(PANEL):
                    if p + 1 < count:
                        left[i] = left[i] - columns[i][j] * new_left[j : j + 1]
                    right[i] = right[i] - columns[i][j][:, :width] * new_right[j : j + 1]
        left[p], right[p] = new_left, new_right
    return jnp.concatenate(right, axis=0)


def update_kernel(
    dims, rates_ref, own_ref, noise_ref, observed_ref, var_ref, anomaly_ref, perm_ref, out_ref,
    anomaly_buf, perm_buf, sems,
):
    local_count, layers, width = dims
    rows = layers * width
    halves = anomaly_ref.shape[1] // LANES
    copies = [
        pltpu.make_async_copy(anomaly_ref, anomaly_buf, sems.at[0]),
        pltpu.make_async_copy(perm_ref, perm_buf, sems.at[1]),
    ]
    for copy in copies:
        copy.start()
    rates = rates_ref[...]
    members = rates.shape[0]
    spread = jnp.sqrt(INFLATION * var_ref[...])
    mean_rate = jnp.sum(rates, 0, keepdims=True) / members
    scaled = (rates - mean_rate) / (spread * (members - 1) ** 0.5)
    innovation = (observed_ref[...] - own_ref[...]) / spread + noise_ref[...]
    contract = (((1,), (1,)), ((), ()))
    gram_matrix, cross_matrix = (
        lax.dot_general(
            scaled, other, contract, precision=lax.Precision.HIGHEST,
            preferred_element_type=jnp.float32,
        )
        for other in (scaled, innovation)
    )
    weights = solve_blocks(gram_matrix, cross_matrix).T.astype(jnp.bfloat16)
    for copy in copies:
        copy.wait()
    for row in range(rows):
        layer, x = row // width, row % width
        at = row * local_count
        every = jnp.concatenate(
            [
                anomaly_buf[k * rows * local_count + at : k * rows * local_count + at + local_count, :]
                for k in range(members // local_count)
            ],
            axis=0,
        )
        update = jnp.dot(weights, every, preferred_element_type=jnp.float32)
        place = (local_count, layer, x, layers, width, halves)
        store_rows(out_ref, load_rows(perm_buf, *place) + update, *place)


def per_device(
    log_perm,
    start_pressure,
    start_sat,
    source,
    storage,
    well_press,
    perf_cell,
    perf_well,
    perf_count,
    observed,
    obs_var,
    obs_noise,
):
    local_count, layers, strip_width, strip_depth = log_perm.shape
    tile_count = lax.axis_size("tile")
    members = local_count * lax.axis_size("member")
    well_count = well_press.shape[0]
    well_share = well_count // tile_count
    tile_rank = lax.axis_index("tile")
    rows = layers * strip_width
    slots = perf_cell.shape[0]
    flat_perm = fold(log_perm)
    fields = [
        array.reshape(rows, strip_depth) for array in (start_pressure, start_sat, source, storage)
    ]
    rim_shape = (RIM * layers * local_count + 4 * GROUP, strip_depth)
    field_scratch = pltpu.VMEM((4 * GROUP, strip_depth), jnp.float32)
    params = pltpu.CompilerParams(vmem_limit_bytes=40 * 2**20)
    up_rows, down_rows, anomaly = pl.pallas_call(
        functools.partial(
            pack_kernel, (local_count, layers, strip_width), (members - 1) ** 0.5
        ),
        out_shape=(
            jax.ShapeDtypeStruct(rim_shape, jnp.bfloat16),
            jax.ShapeDtypeStruct(rim_shape, jnp.bfloat16),
            jax.ShapeDtypeStruct((local_count * rows, strip_depth), jnp.bfloat16),
        ),
        scratch_shapes=[field_scratch, field_scratch],
        compiler_params=params,
        cost_estimate=pl.CostEstimate(
            flops=4 * flat_perm.size, bytes_accessed=8 * flat_perm.size, transcendentals=0
        ),
    )(flat_perm, *fields)
    low_rows, high_rows = send_both(up_rows, down_rows, "tile")
    anomaly_all = lax.all_gather(anomaly, "member", axis=0, tiled=True)

    def whole(array):
        return pl.BlockSpec(array.shape, lambda g: (0,) * array.ndim)

    block = pl.BlockSpec((GROUP * rows * (strip_depth // LANES), LANES), lambda g: (g, 0))
    smem = pl.BlockSpec(memory_space=pltpu.SMEM)
    perfs = [perf_cell[None], perf_well[None], well_press[None]]
    span = strip_width + 2 * RIM
    flat_press, flat_sat, partial_rates = pl.pallas_call(
        functools.partial(physics_kernel, (local_count, layers, strip_width, tile_count)),
        grid=(local_count // GROUP,),
        in_specs=[smem, smem, block, whole(low_rows), whole(high_rows)]
        + [whole(array) for array in fields + perfs],
        out_specs=(
            block,
            block,
            pl.BlockSpec((tile_count, GROUP, well_count), lambda g: (0, g, 0)),
        ),
        out_shape=(
            jax.ShapeDtypeStruct(flat_perm.shape, jnp.float32),
            jax.ShapeDtypeStruct(flat_perm.shape, jnp.float32),
            jax.ShapeDtypeStruct((tile_count, local_count, well_count), jnp.float32),
        ),
        scratch_shapes=[pltpu.VMEM((span * layers, GROUP, strip_depth), jnp.float32)] * 7,
        compiler_params=params,
        cost_estimate=pl.CostEstimate(
            flops=200 * flat_perm.size, bytes_accessed=16 * flat_perm.size, transcendentals=0
        ),
    )(perf_count, tile_rank[None], flat_perm, low_rows, high_rows, *fields, *perfs)
    traded = lax.all_to_all(partial_rates, "tile", 0, 0)
    own_rates = jnp.sum(traded, 0)
    well_rates = lax.dynamic_slice_in_dim(own_rates, tile_rank * well_share, well_share, 1)
    rates_all = lax.all_gather(own_rates, "member", axis=0, tiled=True)
    vmem, anywhere = pl.BlockSpec(memory_space=pltpu.VMEM), pl.BlockSpec(memory_space=pl.ANY)
    new_flat = pl.pallas_call(
        functools.partial(update_kernel, (local_count, layers, strip_width)),
        out_shape=jax.ShapeDtypeStruct(flat_perm.shape, jnp.float32),
        in_specs=[vmem] * 5 + [anywhere] * 2,
        out_specs=vmem,
        scratch_shapes=[
            pltpu.VMEM(anomaly_all.shape, jnp.bfloat16),
            pltpu.VMEM(flat_perm.shape, jnp.float32),
            pltpu.SemaphoreType.DMA((2,)),
        ],
        compiler_params=params,
        cost_estimate=pl.CostEstimate(
            flops=12 * members**3, bytes_accessed=16 * flat_perm.size, transcendentals=0
        ),
    )(rates_all, own_rates, obs_noise, observed[None], obs_var[None], anomaly_all, flat_perm)
    new_log_perm = unfold(new_flat, log_perm.shape)
    pressure = unfold(flat_press, log_perm.shape)
    saturation = unfold(flat_sat, log_perm.shape)
    return (new_log_perm, pressure, saturation, well_rates)


def solution(mesh):
    return jax.shard_map(
        per_device,
        mesh=mesh,
        in_specs=(
            P("member", None, "tile", None),
            P(None, "tile", None),
            P(None, "tile", None),
            P(None, "tile", None),
            P(None, "tile", None),
            P(),
            P("tile"),
            P("tile"),
            P("tile"),
            P(),
            P(),
            P("member", None),
        ),
        out_specs=(
            P("member", None, "tile", None),
            P("member", None, "tile", None),
            P("member", None, "tile", None),
            P("member", "tile"),
        ),
        check_vma=False,
    )
```

profile of v0, /device:TPU:0, one launch (start us, length us, event | category | flops | bytes accessed | tf_op | source)
XLA Modules:
  0.0 90.7 jit_solution(11622493501711018828)
XLA Ops:
  7.2 0.0 all-gather.2.cloned.1.call-start
  7.2 0.0 copy-start
  7.2 1.2 %copy-done = f32[32,4,8,256]{3,2,1,0:T(8,128)S(1)} copy-done((f32[32,4,8,256]{3,2,1,0:T(8,128)S(1)}, f32[32,4,8,256]{3,2,1,0:T(8,128)}, u32[]{:S(2)}) %copy-start) | copy-done | bytes 1048600
  8.4 0.0 copy-start.3
  8.4 0.8 copy-done.3
  9.2 0.0 copy-start.5
  9.2 0.8 copy-done.5
  10.0 0.0 copy-start.7
  10.0 0.8 copy-done.7
  10.7 0.0 copy-start.9
  10.7 0.8 copy-done.9
  11.5 0.0 copy-start.1
  11.5 0.0 copy-start.11
  11.5 0.0 copy-start.15
  11.5 0.0 copy-start.16
  11.5 1.5 %shard_map.147 = (bf16[448,256]{1,0:T(8,128)(2,1)S(1)}, bf16[448,256]{1,0:T(8,128)(2,1)S(1)}, bf16[1024,256]{1,0:T(8,128)(2,1)}) custom-call(f32[2048,128]{1,0:T(8,128)S(1)} %bitcast.30, f32[32,256]{1,0:T(8,128)S(1)} %bitcast.33, f32[32,256]{1,0:T(8,128)S(1)} %bitcast.35, f32[32,256]{1,0:T(8,128)S(1)} %bitcast.37, f32[32,256]{1,0:T(8,128)S(1)} %bitcast.39), custom_call_target="tpu_custom_call" | custom-call | flops 1048576 | bytes 2097152 | tf_op jit(solution)/shard_map/pallas_call | solution.py:417
  12.9 0.0 all-gather.2.cloned.1.call-update
  13.0 4.9 %collective-permute-start = (bf16[448,256]{1,0:T(8,128)(2,1)S(1)}, bf16[448,256]{1,0:T(8,128)(2,1)S(1)}, u32[]{:S(2)}, u32[]{:S(2)}) collective-permute-start(bf16[448,256]{1,0:T(8,128)(2,1)S(1)} %get-tuple-element.10), channel_id=1, source_target_pairs={{0,4},{4,8},{8,12},{12,16},{16,20},{20,24},{24,28},{1,5},{5,9},{9,... | collective-permute-start | bytes 688136 | tf_op jit(solution)/shard_map/ppermute | solution.py:55
  17.8 1.3 %collective-permute-start.1 = (bf16[448,256]{1,0:T(8,128)(2,1)S(1)}, bf16[448,256]{1,0:T(8,128)(2,1)S(1)}, u32[]{:S(2)}, u32[]{:S(2)}) collective-permute-start(bf16[448,256]{1,0:T(8,128)(2,1)S(1)} %get-tuple-element.11), channel_id=1, source_target_pairs={{4,0},{8,4},{12,8},{16,12},{20,16},{24,20},{28,24},{5,1},{9,5},{13... | collective-permute-start | bytes 688136 | tf_op jit(solution)/shard_map/ppermute | solution.py:55
  19.8 7.8 %collective-permute-done.low_ref = bf16[448,256]{1,0:T(8,128)(2,1)S(1)} collective-permute-done((bf16[448,256]{1,0:T(8,128)(2,1)S(1)}, bf16[448,256]{1,0:T(8,128)(2,1)S(1)}, u32[]{:S(2)}, u32[]{:S(2)}) %collective-permute-start) | collective-permute-done | bytes 229408 | tf_op jit(solution)/shard_map/ppermute | solution.py:55
  27.6 0.0 collective-permute-done.1.high_ref
  27.6 0.0 copy-done.1
  27.6 0.0 copy-start.4
  27.6 0.8 copy-done.4
  28.4 0.0 copy-start.6
  28.4 0.8 copy-done.6
  29.1 0.0 copy-start.8
  29.1 0.8 copy-done.8
  29.9 0.0 copy-start.10
  29.9 0.8 copy-done.10
  30.6 0.0 copy-start.12
  30.6 0.7 copy-done.12
  31.3 0.0 copy-start.13
  31.3 0.7 copy-done.13
  32.0 0.0 copy-start.14
  32.0 0.7 copy-done.14
  32.7 20.0 %shard_map.148 = (f32[2048,128]{1,0:T(8,128)}, f32[2048,128]{1,0:T(8,128)}, f32[8,32,256]{2,1,0:T(8,128)}) custom-call(s32[1]{0:T(128)S(6)} %copy.16.count_ref, s32[1]{0:T(128)} %bitcast.rank_ref, f32[2048,128]{1,0:T(8,128)S(1)} %bitcast.31, bf16[448,256]{1,0:T(8,128)(2,1)S(1)} %collective-permute-done.low_ref, ...), custom_call_target="tpu_custom_call" | custom-call | flops 52428800 | bytes 4194304 | tf_op jit(solution)/shard_map/pallas_call | solution.py:442
  52.7 6.7 %all-to-all-start = ((f32[8,32,256]{2,1,0:T(8,128)}), f32[8,32,256]{2,1,0:T(8,128)S(1)}, u32[]{:S(2)}, u32[]{:S(2)}) async-start(f32[8,32,256]{2,1,0:T(8,128)} %get-tuple-element.12), calls=%async_computation | async-start | bytes 524288 | tf_op jit(solution)/shard_map/all_to_all | solution.py:463
  59.4 9.2 %all-to-all-done = f32[8,32,256]{2,1,0:T(8,128)S(1)} async-done(((f32[8,32,256]{2,1,0:T(8,128)}), f32[8,32,256]{2,1,0:T(8,128)S(1)}, u32[]{:S(2)}, u32[]{:S(2)}) %all-to-all-start) | async-done | bytes 262176 | tf_op jit(solution)/shard_map/all_to_all | solution.py:463
  68.6 5.6 %all_gather.6.rates_ref = f32[128,256]{1,0:T(8,128)S(1)} all-gather(f32[32,256]{1,0:T(8,128)S(1)} %reduce_sum.9.own_ref), channel_id=1, replica_groups=mesh['tile'=8,'member'=4] {'member'}, dimensions={0}, use_global_device_ids=true | all-gather | bytes 163840 | tf_op jit(solution)/shard_map/all_gather | solution.py:466
  74.2 0.7 constant_dynamic-slice_fusion
  74.9 0.0 all-gather.2.cloned.1.call-done.anomaly_ref
  74.9 0.0 copy-done.11
  74.9 0.0 copy-done.15
  74.9 0.0 copy-done.16
  74.9 0.0 copy-start.2
  74.9 1.6 %copy-done.2 = bf16[4096,256]{1,0:T(8,128)(2,1)S(1)} copy-done((bf16[4096,256]{1,0:T(8,128)(2,1)S(1)}, bf16[4096,256]{1,0:T(8,128)(2,1)}, u32[]{:S(2)}) %copy-start.2) | copy-done | bytes 2097176
  76.5 7.3 %shard_map.149 = f32[2048,128]{1,0:T(8,128)} custom-call(f32[128,256]{1,0:T(8,128)S(1)} %all_gather.6.rates_ref, f32[32,256]{1,0:T(8,128)S(1)} %reduce_sum.9.own_ref, f32[32,256]{1,0:T(8,128)S(1)} %copy-done.11, f32[1,256]{1,0:T(1,128)S(1)} %bitcast.44, f32[1,256]{1,0:T(1,128)S(1)} %bitcast.45, bf16[4096,256]{1,0:T(8,128)(2,1)S(1)} %copy-done.2, ...), custom_call_target="tpu_custom_call" | custom-call | flops 25165824 | bytes 4194304 | tf_op jit(solution)/shard_map/pallas_call | solution.py:468
  (1 shorter events, 0.0 us)
Async XLA Ops:
  7.2 67.8 %all-gather.2.cloned.1.call-start = ((), (), s32[]{:S(2)}) async-start(), calls=%async_computation.1 | async-start | bytes 2621440 | tf_op jit(solution)/shard_map/all_gather | solution.py:433
  7.2 1.2 %copy-start = (f32[32,4,8,256]{3,2,1,0:T(8,128)S(1)}, f32[32,4,8,256]{3,2,1,0:T(8,128)}, u32[]{:S(2)}) copy-start(f32[32,4,8,256]{3,2,1,0:T(8,128)} %param.12) | copy-start | bytes 3145732
  8.4 0.8 copy-start.3
  9.2 0.8 copy-start.5
  10.0 0.8 copy-start.7
  10.7 0.8 copy-start.9
  11.5 16.1 %copy-start.1 = (f32[32,4,8,256]{3,2,1,0:T(8,128)S(1)}, f32[32,4,8,256]{3,2,1,0:T(8,128)}, u32[]{:S(2)}) copy-start(f32[32,4,8,256]{3,2,1,0:T(8,128)} %param.12) | copy-start | bytes 3145732
  11.5 63.5 %copy-start.11 = (f32[32,256]{1,0:T(8,128)S(1)}, f32[32,256]{1,0:T(8,128)}, u32[]{:S(2)}) copy-start(f32[32,256]{1,0:T(8,128)} %noise_ref.1) | copy-start | bytes 98308
  11.5 63.5 %copy-start.15 = (f32[256]{0:T(256)S(1)}, f32[256]{0:T(256)}, u32[]{:S(2)}) copy-start(f32[256]{0:T(256)} %param.21) | copy-start | bytes 3076
  11.5 63.5 %copy-start.16 = (f32[256]{0:T(256)S(1)}, f32[256]{0:T(256)}, u32[]{:S(2)}) copy-start(f32[256]{0:T(256)} %param.22) | copy-start | bytes 3076
  13.0 14.6 %collective-permute-start = (bf16[448,256]{1,0:T(8,128)(2,1)S(1)}, bf16[448,256]{1,0:T(8,128)(2,1)S(1)}, u32[]{:S(2)}, u32[]{:S(2)}) collective-permute-start(bf16[448,256]{1,0:T(8,128)(2,1)S(1)} %get-tuple-element.10), channel_id=1, source_target_pairs={{0,4},{4,8},{8,12},{12,16},{16,20},{20,24},{24,28},{1,5},{5,9},{9,... | collective-permute-start | bytes 688136 | tf_op jit(solution)/shard_map/ppermute | solution.py:55
  17.8 9.8 %collective-permute-start.1 = (bf16[448,256]{1,0:T(8,128)(2,1)S(1)}, bf16[448,256]{1,0:T(8,128)(2,1)S(1)}, u32[]{:S(2)}, u32[]{:S(2)}) collective-permute-start(bf16[448,256]{1,0:T(8,128)(2,1)S(1)} %get-tuple-element.11), channel_id=1, source_target_pairs={{4,0},{8,4},{12,8},{16,12},{20,16},{24,20},{28,24},{5,1},{9,5},{13... | collective-permute-start | bytes 688136 | tf_op jit(solution)/shard_map/ppermute | solution.py:55
  27.6 0.8 copy-start.4
  28.4 0.8 copy-start.6
  29.1 0.8 copy-start.8
  29.9 0.8 copy-start.10
  30.6 0.7 copy-start.12
  31.3 0.7 copy-start.13
  32.0 0.7 copy-start.14
  52.7 15.9 %all-to-all-start = ((f32[8,32,256]{2,1,0:T(8,128)}), f32[8,32,256]{2,1,0:T(8,128)S(1)}, u32[]{:S(2)}, u32[]{:S(2)}) async-start(f32[8,32,256]{2,1,0:T(8,128)} %get-tuple-element.12), calls=%async_computation | async-start | bytes 524288 | tf_op jit(solution)/shard_map/all_to_all | solution.py:463
  74.9 1.6 %copy-start.2 = (bf16[4096,256]{1,0:T(8,128)(2,1)S(1)}, bf16[4096,256]{1,0:T(8,128)(2,1)}, u32[]{:S(2)}) copy-start(bf16[4096,256]{1,0:T(8,128)(2,1)} %all-gather.2.cloned.1.call-done.anomaly_ref) | copy-start | bytes 6291460
Sparse Core Ops, SparseCore 0:
  13.1 25.2 all-gather.1
where the time goes:
time: 91.7 us; the launch traced here: 90.7 us
  Pallas kernels  28.8 us (31%)
  waiting for transfers between devices  17 us (19%)
  between operations  14.8 us (16%)
  starting transfers between devices  12.9 us (14%)
  local copies, waits for them, and re-layouts  11.6 us (13%)
  blocking collectives  5.61 us (6%)
    pallas_call x1, Pallas kernels, per_device(): pl.pallas_call(functools.partial(physics_kernel, (local_count, layers, st...  20 us
    unnamed x34, local copies, waits for them, and re-layouts  10.9 us
    all_to_all x1, waiting for transfers between devices, per_device(): traded = lax.all_to_all(partial_rates, 'tile', 0, 0)  9.21 us
    ppermute x1, waiting for transfers between devices, send_both(): lax.ppermute(up_rows, axis, forward)  7.82 us
    pallas_call x1, Pallas kernels, per_device(): pl.pallas_call(functools.partial(update_kernel, (local_count, layers, str...  7.32 us
    all_to_all x1, starting transfers between devices, per_device(): traded = lax.all_to_all(partial_rates, 'tile', 0, 0)  6.74 us
    all_gather x1, blocking collectives, per_device(): rates_all = lax.all_gather(own_rates, 'member', axis=0, tiled=True)  5.61 us
    ppermute x1, starting transfers between devices, send_both(): lax.ppermute(up_rows, axis, forward)  4.86 us
  transfers between devices with their start and end apart: 4, of which 2 were waited for; matrix products, arithmetic and copies ran while one was open for 1% of the time, Pallas kernels for 22%

commit v1 on v0

--- a/solution.py
+++ b/solution.py
@@ -55,9 +55,32 @@
     return lax.ppermute(up_rows, axis, forward), lax.ppermute(down_rows, axis, backward)
 
 
+def sum_over(array, axis):
+    count = lax.axis_size(axis)
+    stride = count
+    while stride > 1:
+        radix = 4 if stride % 4 == 0 else 2
+        stride //= radix
+        groups = [
+            [base + low + i * stride for i in range(radix)]
+            for base in range(0, count, stride * radix)
+            for low in range(stride)
+        ]
+        array = jnp.sum(lax.all_gather(array, axis, axis_index_groups=groups), 0)
+    return array
+
+
 def reciprocal(values_in):
     guess = pl.reciprocal(values_in, approx=True)
     return guess * (2.0 - values_in * guess)
+
+
+def pieces(values_in):
+    parts = []
+    for _ in range(3):
+        parts.append(values_in.astype(jnp.bfloat16))
+        values_in = values_in - parts[-1].astype(jnp.float32)
+    return jnp.concatenate(parts, axis=0)
 
 
 def water_frac(values_in):
@@ -66,17 +89,16 @@
     return squared * reciprocal(squared + VISCOSITY_RATIO * rest * rest)
 
 
-def pack_kernel(dims, root, perm_ref, *refs):
+def pack_kernel(dims, root, perm_ref, fields_ref, up_ref, down_ref, anomaly_ref, up_rows, down_rows):
     local_count, layers, width = dims
-    field_refs, (up_ref, down_ref, anomaly_ref, up_rows, down_rows) = refs[:4], refs[4:]
     up_rows[...] = jnp.zeros_like(up_rows)
     down_rows[...] = jnp.zeros_like(down_rows)
-    for f, field_ref in enumerate(field_refs):
+    for f in range(4):
         for layer in range(layers):
             at = f * GROUP + layer * RIM
-            first = layer * width
-            down_rows[at : at + RIM, :] = field_ref[first : first + RIM, :]
-            up_rows[at : at + RIM, :] = field_ref[first + width - RIM : first + width, :]
+            first = (f * layers + layer) * width
+            down_rows[at : at + RIM, :] = fields_ref[first : first + RIM, :]
+            up_rows[at : at + RIM, :] = fields_ref[first + width - RIM : first + width, :]
     halves = anomaly_ref.shape[1] // LANES
     block = RIM * layers * local_count
     up_ref[block:, :] = up_rows[...].astype(jnp.bfloat16)
@@ -99,9 +121,8 @@
 
 def physics_kernel(dims, count_ref, rank_ref, perm_ref, low_ref, high_ref, *refs):
     local_count, layers, width, tile_count = dims
-    own_refs = refs[:4]
-    cell_ref, well_ref, bhp_ref, press_ref, sat_ref, rates_ref, half_inv, face_y = refs[4:12]
-    face_x, face_z, inverse, first_press, last_press = refs[12:]
+    fields_ref, cell_ref, well_ref, bhp_ref, press_ref, sat_ref, rates_ref = refs[:7]
+    half_inv, face_y, face_x, face_z, inverse, first_press, last_press = refs[7:]
     depth = low_ref.shape[1]
     halves = depth // LANES
     group = pl.program_id(0)
@@ -121,7 +142,7 @@
     def behind(values_in):
         return pltpu.roll(values_in, 1, 1)
 
-    own = [ref[...] for ref in own_refs]
+    own = [fields_ref[f * layers * width : (f + 1) * layers * width, :] for f in range(4)]
     rims = [
         [
             ref[rim_rows + f * GROUP : rim_rows + (f + 1) * GROUP, :].astype(jnp.float32)
@@ -277,23 +298,24 @@
 
     wells = bhp_ref.shape[1]
     chosen = (
-        lax.broadcasted_iota(jnp.int32, (wells, slots), 0) == well_ref[...]
-    ).astype(jnp.float32)
-    bhp = jnp.broadcast_to(bhp_ref[...], (8, wells))
-    perf_bhp = jnp.dot(
-        bhp, chosen, precision=lax.Precision.HIGHEST, preferred_element_type=jnp.float32
-    )[:1]
+        (lax.broadcasted_iota(jnp.int32, (wells, slots), 0) == well_ref[...])
+        .astype(jnp.float32)
+        .astype(jnp.bfloat16)
+    )
+    bhp = pieces(jnp.broadcast_to(bhp_ref[...], (GROUP, wells)))
+    bhp = jnp.dot(bhp, chosen, preferred_element_type=jnp.float32)
+    perf_bhp = (bhp[:1] + bhp[GROUP : GROUP + 1]) + bhp[2 * GROUP : 2 * GROUP + 1]
     live = (lax.broadcasted_iota(jnp.int32, (1, slots), 1) < count_ref[0]).astype(jnp.float32)
     terms = (
         jnp.concatenate(perf_mob, axis=1)
         * (jnp.concatenate(perf_press, axis=1) - perf_bhp)
         * live
     )
-    partial_rates = lax.dot_general(
-        terms, chosen, (((1,), (1,)), ((), ())), precision=lax.Precision.HIGHEST,
-        preferred_element_type=jnp.float32,
+    sums = lax.dot_general(
+        pieces(terms), chosen, (((1,), (1,)), ((), ())), preferred_element_type=jnp.float32
     )
-    rates_ref[...] = jnp.broadcast_to(partial_rates[None], rates_ref.shape)
+    partial_rates = (sums[:GROUP] + sums[GROUP : 2 * GROUP]) + sums[2 * GROUP :]
+    rates_ref[...] = partial_rates
 
 
 def invert_panel(columns):
@@ -408,12 +430,10 @@
     rows = layers * strip_width
     slots = perf_cell.shape[0]
     flat_perm = fold(log_perm)
-    fields = [
-        array.reshape(rows, strip_depth) for array in (start_pressure, start_sat, source, storage)
-    ]
+    fields = jnp.stack([start_pressure, start_sat, source, storage]).reshape(-1, strip_depth)
     rim_shape = (RIM * layers * local_count + 4 * GROUP, strip_depth)
     field_scratch = pltpu.VMEM((4 * GROUP, strip_depth), jnp.float32)
-    params = pltpu.CompilerParams(vmem_limit_bytes=40 * 2**20)
+    params = pltpu.CompilerParams(vmem_limit_bytes=60 * 2**20)
     up_rows, down_rows, anomaly = pl.pallas_call(
         functools.partial(
             pack_kernel, (local_count, layers, strip_width), (members - 1) ** 0.5
@@ -428,7 +448,7 @@
         cost_estimate=pl.CostEstimate(
             flops=4 * flat_perm.size, bytes_accessed=8 * flat_perm.size, transcendentals=0
         ),
-    )(flat_perm, *fields)
+    )(flat_perm, fields)
     low_rows, high_rows = send_both(up_rows, down_rows, "tile")
     anomaly_all = lax.all_gather(anomaly, "member", axis=0, tiled=True)
 
@@ -443,25 +463,24 @@
         functools.partial(physics_kernel, (local_count, layers, strip_width, tile_count)),
         grid=(local_count // GROUP,),
         in_specs=[smem, smem, block, whole(low_rows), whole(high_rows)]
-        + [whole(array) for array in fields + perfs],
+        + [whole(array) for array in [fields] + perfs],
         out_specs=(
             block,
             block,
-            pl.BlockSpec((tile_count, GROUP, well_count), lambda g: (0, g, 0)),
+            pl.BlockSpec((GROUP, well_count), lambda g: (g, 0)),
         ),
         out_shape=(
             jax.ShapeDtypeStruct(flat_perm.shape, jnp.float32),
             jax.ShapeDtypeStruct(flat_perm.shape, jnp.float32),
-            jax.ShapeDtypeStruct((tile_count, local_count, well_count), jnp.float32),
+            jax.ShapeDtypeStruct((local_count, well_count), jnp.float32),
         ),
         scratch_shapes=[pltpu.VMEM((span * layers, GROUP, strip_depth), jnp.float32)] * 7,
         compiler_params=params,
         cost_estimate=pl.CostEstimate(
             flops=200 * flat_perm.size, bytes_accessed=16 * flat_perm.size, transcendentals=0
         ),
-    )(perf_count, tile_rank[None], flat_perm, low_rows, high_rows, *fields, *perfs)
-    traded = lax.all_to_all(partial_rates, "tile", 0, 0)
-    own_rates = jnp.sum(traded, 0)
+    )(perf_count, tile_rank[None], flat_perm, low_rows, high_rows, fields, *perfs)
+    own_rates = sum_over(partial_rates, "tile")
     well_rates = lax.dynamic_slice_in_dim(own_rates, tile_rank * well_share, well_share, 1)
     rates_all = lax.all_gather(own_rates, "member", axis=0, tiled=True)
     vmem, anywhere = pl.BlockSpec(memory_space=pltpu.VMEM), pl.BlockSpec(memory_space=pl.ANY)

time: 91.7 us -> 91.7 us (level)
  blocking collectives: 5.61 us -> 26.1 us
  local copies, waits for them, and re-layouts: 11.6 us -> 1.46 us
  waiting for transfers between devices: 17 us -> 8.15 us
  starting transfers between devices: 12.9 us -> 6.19 us
  Pallas kernels: 28.8 us -> 33.2 us
  other arithmetic: 0.02 us -> 1.48 us
    all_gather x0 -> x2, blocking collectives: none -> 20.1 us  [sum_over(): array = jnp.sum(lax.all_gather(array, axis, axis_index_groups=groups), 0)]
    unnamed x34 -> x6, local copies, waits for them, and re-layouts: 10.9 us -> 0.78 us
    all_to_all x1 -> x0, waiting for transfers between devices: 9.21 us -> none  [per_device(): traded = lax.all_to_all(partial_rates, 'tile', 0, 0)]
    all_to_all x1 -> x0, starting transfers between devices: 6.74 us -> none  [per_device(): traded = lax.all_to_all(partial_rates, 'tile', 0, 0)]
    pallas_call x1, Pallas kernels: 20 us -> 22.4 us  [per_device(): pl.pallas_call(functools.partial(physics_kernel, (local_count, layers, st...]
    another operation x0 -> x1, other arithmetic: none -> 1.46 us  [per_device(): jnp.stack([start_pressure, start_sat, source, storage])]
    pallas_call x1, Pallas kernels: 1.46 us -> 2.78 us  [per_device(): pl.pallas_call(functools.partial(pack_kernel, (local_count, layers, strip...]
  transfers between devices with their start and end apart: 4 -> 3, of which waited for: 2 -> 1; matrix products, arithmetic and copies ran while one was open for 1% -> 1% of each run, Pallas kernels for 22% -> 24%
where the time goes in v1:
time: 91.7 us; the launch traced here: 91.3 us
  Pallas kernels  33.2 us (36%)
  blocking collectives  26.1 us (28%)
  between operations  14.7 us (16%)
  waiting for transfers between devices  8.15 us (9%)
  starting transfers between devices  6.19 us (7%)
  other arithmetic  1.48 us (2%)
  local copies, waits for them, and re-layouts  1.46 us (2%)
    pallas_call x1, Pallas kernels, per_device(): pl.pallas_call(functools.partial(physics_kernel, (local_count, layers, st...  22.4 us
    all_gather x2, blocking collectives, sum_over(): array = jnp.sum(lax.all_gather(array, axis, axis_index_groups=groups), 0)  20.1 us
    ppermute x1, waiting for transfers between devices, send_both(): lax.ppermute(up_rows, axis, forward)  8.13 us
    pallas_call x1, Pallas kernels, per_device(): pl.pallas_call(functools.partial(update_kernel, (local_count, layers, str...  8.06 us
    all_gather x1, blocking collectives, per_device(): rates_all = lax.all_gather(own_rates, 'member', axis=0, tiled=True)  6.06 us
    ppermute x1, starting transfers between devices, send_both(): lax.ppermute(up_rows, axis, forward)  4.86 us
    pallas_call x1, Pallas kernels, per_device(): pl.pallas_call(functools.partial(pack_kernel, (local_count, layers, strip...  2.78 us
  transfers between devices with their start and end apart: 3, of which 1 were waited for; matrix products, arithmetic and copies ran while one was open for 1% of the time, Pallas kernels for 24%

profile of v1, /device:TPU:0, one launch (start us, length us, event | category | flops | bytes accessed | tf_op | source)
XLA Modules:
  0.0 91.3 jit_solution(17110506575195778930)
XLA Ops:
  7.2 0.0 all-gather.4.cloned.1.call-start
  7.2 1.5 %pad_maximum_fusion = f32[4,4,8,256]{3,2,1,0:T(8,128)} fusion(f32[1,4,8,256]{3,2,1,0:T(8,128)} %bitcast.41, f32[1,4,8,256]{3,2,1,0:T(8,128)} %bitcast.42, f32[1,4,8,256]{3,2,1,0:T(8,128)} %bitcast.43, f32[1,4,8,256]{3,2,1,0:T(8,128)} %bitcast.44), kind=kLoop, calls=%fused_computation | loop fusion | flops 98304 | bytes 262144 | tf_op jit(solution)/shard_map/stack | solution.py:433
  8.7 2.8 %shard_map.147 = (bf16[448,256]{1,0:T(8,128)(2,1)}, bf16[448,256]{1,0:T(8,128)(2,1)}, bf16[1024,256]{1,0:T(8,128)(2,1)}) custom-call(f32[2048,128]{1,0:T(8,128)} %bitcast.33, f32[128,256]{1,0:T(8,128)} %bitcast.36), custom_call_target="tpu_custom_call" | custom-call | flops 1048576 | bytes 2097152 | tf_op jit(solution)/shard_map/pallas_call | solution.py:437
  11.5 0.0 all-gather.4.cloned.1.call-update
  11.5 4.9 %collective-permute-start = (bf16[448,256]{1,0:T(8,128)(2,1)}, bf16[448,256]{1,0:T(8,128)(2,1)S(1)}, u32[]{:S(2)}, u32[]{:S(2)}) collective-permute-start(bf16[448,256]{1,0:T(8,128)(2,1)} %get-tuple-element.10), channel_id=1, source_target_pairs={{0,4},{4,8},{8,12},{12,16},{16,20},{20,24},{24,28},{1,5},{5,9},{9,... | collective-permute-start | bytes 688136 | tf_op jit(solution)/shard_map/ppermute | solution.py:55
  16.3 1.3 %collective-permute-start.1 = (bf16[448,256]{1,0:T(8,128)(2,1)}, bf16[448,256]{1,0:T(8,128)(2,1)S(1)}, u32[]{:S(2)}, u32[]{:S(2)}) collective-permute-start(bf16[448,256]{1,0:T(8,128)(2,1)} %get-tuple-element.11), channel_id=1, source_target_pairs={{4,0},{8,4},{12,8},{16,12},{20,16},{24,20},{28,24},{5,1},{9,5},{13... | collective-permute-start | bytes 688136 | tf_op jit(solution)/shard_map/ppermute | solution.py:55
  18.3 8.1 %collective-permute-done.low_ref = bf16[448,256]{1,0:T(8,128)(2,1)S(1)} collective-permute-done((bf16[448,256]{1,0:T(8,128)(2,1)}, bf16[448,256]{1,0:T(8,128)(2,1)S(1)}, u32[]{:S(2)}, u32[]{:S(2)}) %collective-permute-start) | collective-permute-done | bytes 229408 | tf_op jit(solution)/shard_map/ppermute | solution.py:55
  26.4 0.0 copy-start.1
  26.4 0.0 collective-permute-done.1.high_ref
  26.4 0.0 copy-start.2
  26.4 0.7 copy-done.1
  27.1 0.1 copy-done.2
  27.2 22.4 %shard_map.148 = (f32[2048,128]{1,0:T(8,128)}, f32[2048,128]{1,0:T(8,128)}, f32[32,256]{1,0:T(8,128)}) custom-call(s32[1]{0:T(128)S(6)} %copy.16.count_ref, s32[1]{0:T(128)} %bitcast.rank_ref, f32[2048,128]{1,0:T(8,128)} %bitcast.34, bf16[448,256]{1,0:T(8,128)(2,1)} %copy-done.1, bf16[448,256]{1,0:T(8,128)(2,1)} %copy-done.2, f32[128,256]{1,0:T(8,128)} %bitcast.37, ...), custom_call_target="tpu_custom_call" | custom-call | flops 52428800 | bytes 4194304 | tf_op jit(solution)/shard_map/pallas_call | solution.py:462
  49.6 15.5 %all-gather = f32[128,256]{1,0:T(8,128)S(1)} all-gather(f32[32,256]{1,0:T(8,128)} %get-tuple-element.12), channel_id=2, replica_groups={{0,8,16,24},{4,12,20,28},{1,9,17,25},{5,13,21,29},{2,10,18,26},{6,14,22..., dimensions={0}, use_global_device_ids=true | all-gather | bytes 163840 | tf_op jit(solution)/shard_map/all_gather | solution.py:69
  65.1 4.6 %all-gather.1 = f32[64,256]{1,0:T(8,128)S(1)} all-gather(f32[32,256]{1,0:T(8,128)S(1)} %reduce_sum.18), channel_id=3, replica_groups={{0,4},{8,12},{16,20},{24,28},{1,5},{9,13},{17,21},{25,29},{2,6},{10,14}..., dimensions={0}, use_global_device_ids=true | all-gather | bytes 98304 | tf_op jit(solution)/shard_map/all_gather | solution.py:69
  69.7 0.0 copy-start
  69.7 6.1 %all_gather.22.rates_ref = f32[128,256]{1,0:T(8,128)} all-gather(f32[32,256]{1,0:T(8,128)S(1)} %reduce_sum.19.own_ref), channel_id=1, replica_groups=mesh['tile'=8,'member'=4] {'member'}, dimensions={0}, use_global_device_ids=true | all-gather | bytes 163840 | tf_op jit(solution)/shard_map/all_gather | solution.py:485
  75.7 0.7 constant_dynamic-slice_fusion
  76.4 0.0 all-gather.4.cloned.1.call-done.anomaly_ref
  76.4 0.0 copy-done
  76.4 8.1 %shard_map.149 = f32[2048,128]{1,0:T(8,128)} custom-call(f32[128,256]{1,0:T(8,128)} %all_gather.22.rates_ref, f32[32,256]{1,0:T(8,128)} %copy-done, f32[32,256]{1,0:T(8,128)} %noise_ref.1, f32[1,256]{1,0:T(1,128)} %bitcast.48, f32[1,256]{1,0:T(1,128)} %bitcast.49, bf16[4096,256]{1,0:T(8,128)(2,1)} %all-gather.4.cloned.1.call-done.anomaly_ref, ...), custom_call_target="tpu_custom_call" | custom-call | flops 25165824 | bytes 4194304 | tf_op jit(solution)/shard_map/pallas_call | solution.py:487
  (2 shorter events, 0.0 us)
Async XLA Ops:
  7.2 69.2 %all-gather.4.cloned.1.call-start = ((), (), s32[]{:S(2)}) async-start(), calls=%async_computation | async-start | bytes 2621440 | tf_op jit(solution)/shard_map/all_gather | solution.py:453
  11.5 14.9 %collective-permute-start = (bf16[448,256]{1,0:T(8,128)(2,1)}, bf16[448,256]{1,0:T(8,128)(2,1)S(1)}, u32[]{:S(2)}, u32[]{:S(2)}) collective-permute-start(bf16[448,256]{1,0:T(8,128)(2,1)} %get-tuple-element.10), channel_id=1, source_target_pairs={{0,4},{4,8},{8,12},{12,16},{16,20},{20,24},{24,28},{1,5},{5,9},{9,... | collective-permute-start | bytes 688136 | tf_op jit(solution)/shard_map/ppermute | solution.py:55
  16.3 10.1 %collective-permute-start.1 = (bf16[448,256]{1,0:T(8,128)(2,1)}, bf16[448,256]{1,0:T(8,128)(2,1)S(1)}, u32[]{:S(2)}, u32[]{:S(2)}) collective-permute-start(bf16[448,256]{1,0:T(8,128)(2,1)} %get-tuple-element.11), channel_id=1, source_target_pairs={{4,0},{8,4},{12,8},{16,12},{20,16},{24,20},{28,24},{5,1},{9,5},{13... | collective-permute-start | bytes 688136 | tf_op jit(solution)/shard_map/ppermute | solution.py:55
  26.4 0.7 copy-start.1
  26.4 0.8 copy-start.2
  69.7 6.7 %copy-start = (f32[32,256]{1,0:T(8,128)}, f32[32,256]{1,0:T(8,128)S(1)}, u32[]{:S(2)}) copy-start(f32[32,256]{1,0:T(8,128)S(1)} %reduce_sum.19.own_ref) | copy-start | bytes 98308
Sparse Core Ops, SparseCore 0:
  11.6 25.3 all-gather.3

commit v2 on v1

--- a/solution.py
+++ b/solution.py
@@ -59,7 +59,7 @@
     count = lax.axis_size(axis)
     stride = count
     while stride > 1:
-        radix = 4 if stride % 4 == 0 else 2
+        radix = 2
         stride //= radix
         groups = [
             [base + low + i * stride for i in range(radix)]
@@ -119,203 +119,359 @@
                 up_ref[at : at + local_count, :] = low_values
 
 
-def physics_kernel(dims, count_ref, rank_ref, perm_ref, low_ref, high_ref, *refs):
-    local_count, layers, width, tile_count = dims
-    fields_ref, cell_ref, well_ref, bhp_ref, press_ref, sat_ref, rates_ref = refs[:7]
-    half_inv, face_y, face_x, face_z, inverse, first_press, last_press = refs[7:]
-    depth = low_ref.shape[1]
-    halves = depth // LANES
-    group = pl.program_id(0)
-    rim_rows = RIM * layers * local_count
-    lane = lax.broadcasted_iota(jnp.int32, (1, depth), 1)
-    open_y = (lane < depth - 1).astype(jnp.float32)
-    has_low = (rank_ref[0] > 0).astype(jnp.float32)
-    has_high = (rank_ref[0] < tile_count - 1).astype(jnp.float32)
-    span = width + 2 * RIM
-
-    def slot(r, layer):
-        return (r + RIM) * layers + layer
-
-    def ahead(values_in):
-        return pltpu.roll(values_in, depth - 1, 1)
-
-    def behind(values_in):
-        return pltpu.roll(values_in, 1, 1)
-
-    own = [fields_ref[f * layers * width : (f + 1) * layers * width, :] for f in range(4)]
-    rims = [
-        [
-            ref[rim_rows + f * GROUP : rim_rows + (f + 1) * GROUP, :].astype(jnp.float32)
-            for f in range(4)
-        ]
-        for ref in (low_ref, high_ref)
-    ]
-
-    def with_shifts(p0, sat, source, storage):
-        frac = water_frac(sat)
-        return dict(
-            p0=p0, sat=sat, storage=storage, base=source + storage * p0,
-            ahead=ahead(p0), behind=behind(p0), frac=frac, frac_ahead=ahead(frac),
+FIELD_NAMES = ("p0", "sat", "storage", "base", "ahead", "behind", "frac", "frac_ahead")
+
+
+def state_slots(layers, width):
+    kept, added = {}, {}
+    rim = list(range(-RIM, 0)) + list(range(width, width + RIM))
+    near = [-2, -1, width, width + 1]
+
+    def place(where, kind, rows, count=layers):
+        for r in rows:
+            for layer in range(count):
+                where[kind, r, layer] = len(where)
+
+    place(kept, "half", (0, width - 1))
+    place(kept, "face_x", range(width - 1))
+    place(kept, "face_y", range(width))
+    place(kept, "face_z", range(width), layers - 1)
+    place(kept, "inverse", range(width))
+    place(kept, "first", range(width))
+    place(kept, "last", range(2, width - 2))
+    place(kept, "sat", range(3, width - 3))
+    place(added, "half", rim)
+    place(added, "face_x", [-3, -2, -1, width - 1, width, width + 1])
+    place(added, "face_y", near)
+    place(added, "face_z", near, layers - 1)
+    place(added, "inverse", near + [0, width - 1])
+    place(added, "first", near + [0, width - 1])
+    place(added, "last", [-1, 0, 1, width - 2, width - 1, width])
+    return kept, added
+
+
+def ahead(values_in):
+    return pltpu.roll(values_in, values_in.shape[1] - 1, 1)
+
+
+def behind(values_in):
+    return pltpu.roll(values_in, 1, 1)
+
+
+def derived_fields(p0, sat, source, storage):
+    frac = water_frac(sat)
+    return dict(
+        p0=p0, sat=sat, storage=storage, base=source + storage * p0,
+        ahead=ahead(p0), behind=behind(p0), frac=frac, frac_ahead=ahead(frac),
+    )
+
+
+def cell_faces(load, store, field, r, layer, layers, sides):
+    here = load("half", r, layer)
+    lane = lax.broadcasted_iota(jnp.int32, here.shape, 1)
+    up_y = jnp.where(lane < here.shape[1] - 1, reciprocal(here + ahead(here)), 0.0)
+    low_y = behind(up_y)
+    store("face_y", r, layer, up_y)
+    flow = up_y * field("ahead", r, layer) + low_y * field("behind", r, layer)
+    weight = up_y + low_y
+    for face, towards in sides:
+        flow = flow + face * field("p0", towards, layer)
+        weight = weight + face
+    if layer + 1 < layers:
+        up_z = VERTICAL * reciprocal(here + load("half", r, layer + 1))
+        store("face_z", r, layer, up_z)
+        flow = flow + up_z * field("p0", r, layer + 1)
+        weight = weight + up_z
+    if layer > 0:
+        low_z = load("face_z", r, layer - 1)
+        flow = flow + low_z * field("p0", r, layer - 1)
+        weight = weight + low_z
+    return field("base", r, layer) + flow, field("storage", r, layer) + weight
+
+
+def second_sweep(load, store, field, r, layers):
+    for layer in range(layers):
+        here = load("first", r, layer)
+        up_y = load("face_y", r, layer)
+        flow = (
+            load("face_x", r - 1, layer) * load("first", r - 1, layer)
+            + load("face_x", r, layer) * load("first", r + 1, layer)
+            + up_y * ahead(here)
+            + behind(up_y * here)
         )
-
-    shared = [with_shifts(*fields) for fields in (own, rims[0], rims[1])]
-
-    def field(name, r, layer):
-        if 0 <= r < width:
-            part, at = shared[0], layer * width + r
-        elif r < 0:
-            part, at = shared[1], layer * RIM + r + RIM
-        else:
-            part, at = shared[2], layer * RIM + r - width
-        return part[name][at : at + 1, :]
-
-    for r in range(-RIM, width + RIM):
+        if layer + 1 < layers:
+            flow = flow + load("face_z", r, layer) * load("first", r, layer + 1)
+        if layer > 0:
+            flow = flow + load("face_z", r, layer - 1) * load("first", r, layer - 1)
+        store("last", r, layer, (field("base", r, layer) + flow) * load("inverse", r, layer))
+
+
+def carried(face, low_press, up_press, low_frac, up_frac):
+    velocity = face * (low_press - up_press)
+    return velocity * jnp.where(velocity > 0, low_frac, up_frac)
+
+
+def transported(load, field, first_row, last_row, layers):
+    def side(r, layer):
+        return carried(
+            load("face_x", r, layer), load("last", r, layer), load("last", r + 1, layer),
+            field("frac", r, layer), field("frac", r + 1, layer),
+        )
+
+    low_x = [side(first_row - 1, layer) for layer in range(layers)]
+    for r in range(first_row, last_row + 1):
+        low_z = None
         for layer in range(layers):
-            if 0 <= r < width:
-                values = load_rows(perm_ref, GROUP, layer, r, layers, width, halves)
-            else:
-                ref, i = (low_ref, r + RIM) if r < 0 else (high_ref, r - width)
-                at = (i * layers + layer) * local_count + group * GROUP
-                values = ref[pl.ds(pl.multiple_of(at, GROUP), GROUP), :].astype(jnp.float32)
-            half_inv[slot(r, layer)] = 0.5 * jnp.exp(-values)
-
-    for r in range(-RIM, width + RIM - 1):
-        for layer in range(layers):
-            face = reciprocal(half_inv[slot(r, layer)] + half_inv[slot(r + 1, layer)])
-            if r == -1:
-                face = face * has_low
-            if r == width - 1:
-                face = face * has_high
-            face_x[slot(r, layer)] = face
-
-    for r in range(1 - RIM, width + RIM - 1):
-        for layer in range(layers):
-            at = slot(r, layer)
-            here = half_inv[at]
-            up_y = reciprocal(here + ahead(here)) * open_y
-            low_y = behind(up_y)
-            face_y[at] = up_y
-            low_x, up_x = face_x[slot(r - 1, layer)], face_x[at]
-            flow = (
-                low_x * field("p0", r - 1, layer)
-                + up_x * field("p0", r + 1, layer)
-                + up_y * field("ahead", r, layer)
-                + low_y * field("behind", r, layer)
+            here = load("last", r, layer)
+            frac = field("frac", r, layer)
+            up_x = side(r, layer)
+            up_y = carried(
+                load("face_y", r, layer), here, ahead(here), frac, field("frac_ahead", r, layer)
             )
-            weight = (low_x + up_x) + (up_y + low_y)
+            change = (low_x[layer] - up_x) + (behind(up_y) - up_y)
+            low_x[layer] = up_x
+            if low_z is not None:
+                change = change + low_z
             if layer + 1 < layers:
-                up_z = VERTICAL * reciprocal(here + half_inv[slot(r, layer + 1)])
-                face_z[at] = up_z
-                flow = flow + up_z * field("p0", r, layer + 1)
-                weight = weight + up_z
-            if layer > 0:
-                low_z = face_z[slot(r, layer - 1)]
-                flow = flow + low_z * field("p0", r, layer - 1)
-                weight = weight + low_z
-            scale = reciprocal(field("storage", r, layer) + weight)
-            inverse[at] = scale
-            first_press[at] = (field("base", r, layer) + flow) * scale
-
-    for r in range(-1, width + 1):
-        for layer in range(layers):
-            at = slot(r, layer)
-            here = first_press[at]
-            up_y = face_y[at]
-            flow = (
-                face_x[slot(r - 1, layer)] * first_press[slot(r - 1, layer)]
-                + face_x[at] * first_press[slot(r + 1, layer)]
-                + up_y * ahead(here)
-                + behind(up_y * here)
-            )
-            if layer + 1 < layers:
-                flow = flow + face_z[at] * first_press[slot(r, layer + 1)]
-            if layer > 0:
-                flow = flow + face_z[slot(r, layer - 1)] * first_press[slot(r, layer - 1)]
-            last_press[at] = (field("base", r, layer) + flow) * inverse[at]
-
-    perf_cell = cell_ref[...]
-    slots = perf_cell.shape[1]
-    parts = slots // LANES
-    lane_at = perf_cell % LANES
-    row_at = perf_cell // LANES
-    lane_of = [
-        jnp.broadcast_to(lane_at[:, p * LANES : (p + 1) * LANES], (GROUP, LANES))
-        for p in range(parts)
-    ]
-    row_of = [
-        jnp.broadcast_to(row_at[:, p * LANES : (p + 1) * LANES], (GROUP, LANES))
-        for p in range(parts)
-    ]
-    zeros = jnp.zeros((GROUP, LANES), jnp.float32)
-    perf_mob, perf_press = [zeros] * parts, [zeros] * parts
-
-    def carried(face, low_press, up_press, low_frac, up_frac):
-        velocity = face * (low_press - up_press)
-        return velocity * jnp.where(velocity > 0, low_frac, up_frac)
-
-    for layer in range(layers):
-        low_x = carried(
-            face_x[slot(-1, layer)], last_press[slot(-1, layer)], last_press[slot(0, layer)],
-            field("frac", -1, layer), field("frac", 0, layer),
-        )
-        for r in range(width):
-            at = slot(r, layer)
-            here = last_press[at]
-            frac = field("frac", r, layer)
-            up_x = carried(
-                face_x[at], here, last_press[slot(r + 1, layer)], frac, field("frac", r + 1, layer)
-            )
-            up_y = carried(face_y[at], here, ahead(here), frac, field("frac_ahead", r, layer))
-            change = (low_x - up_x) + (behind(up_y) - up_y)
-            low_x = up_x
-            if layer + 1 < layers:
-                up_z = carried(
-                    face_z[at], here, last_press[slot(r, layer + 1)], frac,
+                low_z = carried(
+                    load("face_z", r, layer), here, load("last", r, layer + 1), frac,
                     field("frac", r, layer + 1),
                 )
-                change = change - up_z
-                first_press[at] = up_z
-            if layer > 0:
-                change = change + first_press[slot(r, layer - 1)]
-            saturation = field("sat", r, layer) + STEP_COEF * change
-            row = layer * width + r
-            store_rows(press_ref, here, GROUP, layer, r, layers, width, halves)
-            store_rows(sat_ref, saturation, GROUP, layer, r, layers, width, halves)
-            mobility = water_frac(saturation) * reciprocal(2.0 * half_inv[at])
-            for half in range(halves):
-                mob_part = mobility[:, half * LANES : (half + 1) * LANES]
-                press_part = here[:, half * LANES : (half + 1) * LANES]
-                for p in range(parts):
-                    mine = row_of[p] == row * halves + half
-                    perf_mob[p] = jnp.where(
-                        mine, jnp.take_along_axis(mob_part, lane_of[p], axis=1, mode="promise_in_bounds"), perf_mob[p]
-                    )
-                    perf_press[p] = jnp.where(
-                        mine,
-                        jnp.take_along_axis(press_part, lane_of[p], axis=1, mode="promise_in_bounds"),
-                        perf_press[p],
-                    )
-
+                change = change - low_z
+            yield r, layer, field("sat", r, layer) + STEP_COEF * change
+
+
+def pick(picked, values_in, row, lane_of, row_of):
+    halves = values_in.shape[1] // LANES
+    for half in range(halves):
+        part = values_in[:, half * LANES : (half + 1) * LANES]
+        for p in range(len(picked)):
+            found = jnp.take_along_axis(part, lane_of[p], axis=1, mode="promise_in_bounds")
+            picked[p] = jnp.where(row_of[p] == row * halves + half, found, picked[p])
+
+
+def slot_parts(array):
+    parts = [array[:, p * LANES : (p + 1) * LANES] for p in range(array.shape[1] // LANES)]
+    return [jnp.concatenate([part] * (GROUP // part.shape[0]), axis=0) for part in parts]
+
+
+def inner_kernel(
+    dims, count_ref, perm_ref, fields_ref, cell_ref, well_ref, bhp_ref,
+    state_ref, shared_ref, perf_ref, place_ref, chosen_ref, slot_ref, half_ref,
+):
+    local_count, layers, width = dims
+    rows = layers * width
+    depth = fields_ref.shape[1]
+    halves = depth // LANES
+    kept, _ = state_slots(layers, width)
+    fields = derived_fields(*(fields_ref[f * rows : (f + 1) * rows, :] for f in range(4)))
+    for n, name in enumerate(FIELD_NAMES):
+        for row in range(rows):
+            shared_ref[n * rows + row] = jnp.broadcast_to(
+                fields[name][row : row + 1, :], (8, depth)
+            )
+    slots = cell_ref.shape[1]
     wells = bhp_ref.shape[1]
+    cells = jnp.broadcast_to(cell_ref[...], (8, slots))
+    place_ref[:8, :] = cells % LANES
+    place_ref[8:, :] = cells // LANES
     chosen = (
         (lax.broadcasted_iota(jnp.int32, (wells, slots), 0) == well_ref[...])
         .astype(jnp.float32)
         .astype(jnp.bfloat16)
     )
+    chosen_ref[...] = chosen
     bhp = pieces(jnp.broadcast_to(bhp_ref[...], (GROUP, wells)))
     bhp = jnp.dot(bhp, chosen, preferred_element_type=jnp.float32)
-    perf_bhp = (bhp[:1] + bhp[GROUP : GROUP + 1]) + bhp[2 * GROUP : 2 * GROUP + 1]
-    live = (lax.broadcasted_iota(jnp.int32, (1, slots), 1) < count_ref[0]).astype(jnp.float32)
-    terms = (
-        jnp.concatenate(perf_mob, axis=1)
-        * (jnp.concatenate(perf_press, axis=1) - perf_bhp)
-        * live
+    live = (lax.broadcasted_iota(jnp.int32, (8, slots), 1) < count_ref[0]).astype(jnp.float32)
+    slot_ref[:8, :] = (bhp[:8] + bhp[GROUP : GROUP + 8]) + bhp[2 * GROUP : 2 * GROUP + 8]
+    slot_ref[8:, :] = live
+
+    def field(name, r, layer):
+        tile = shared_ref[FIELD_NAMES.index(name) * rows + layer * width + r]
+        return jnp.concatenate([tile] * (GROUP // 8), axis=0)
+
+    @pl.loop(0, local_count // GROUP)
+    def _(group):
+        at_group = pl.ds(pl.multiple_of(group * GROUP, GROUP), GROUP)
+        lane_of, row_of = slot_parts(place_ref[:8, :]), slot_parts(place_ref[8:, :])
+        zeros = [jnp.zeros((GROUP, LANES), jnp.float32)] * (slots // LANES)
+        picked = [list(zeros) for _ in range(3)]
+
+        def load(kind, r, layer):
+            if kind == "half":
+                return half_ref[layer * width + r]
+            return state_ref[kept[kind, r, layer], at_group, :]
+
+        def store(kind, r, layer, values_in):
+            state_ref[kept[kind, r, layer], at_group, :] = values_in
+
+        for r in range(width):
+            for layer in range(layers):
+                values = jnp.concatenate(
+                    [
+                        perm_ref[
+                            pl.ds(
+                                group * GROUP * rows * halves + (layer * halves + h) * width + r,
+                                GROUP, stride=rows * halves,
+                            ),
+                            :,
+                        ]
+                        for h in range(halves)
+                    ],
+                    axis=1,
+                )
+                half = 0.5 * jnp.exp(-values)
+                half_ref[layer * width + r] = half
+                if r in (0, width - 1):
+                    store("half", r, layer, half)
+                pick(picked[0], half, layer * width + r, lane_of, row_of)
+        for r in range(width - 1):
+            for layer in range(layers):
+                store(
+                    "face_x", r, layer,
+                    reciprocal(load("half", r, layer) + load("half", r + 1, layer)),
+                )
+        for r in range(width):
+            for layer in range(layers):
+                sides = []
+                if r > 0:
+                    sides.append((load("face_x", r - 1, layer), r - 1))
+                if r < width - 1:
+                    sides.append((load("face_x", r, layer), r + 1))
+                top, bottom = cell_faces(load, store, field, r, layer, layers, sides)
+                if 0 < r < width - 1:
+                    bottom = reciprocal(bottom)
+                    top = top * bottom
+                store("first", r, layer, top)
+                store("inverse", r, layer, bottom)
+        for r in range(2, width - 2):
+            second_sweep(load, store, field, r, layers)
+            for layer in range(layers):
+                pick(picked[1], load("last", r, layer), layer * width + r, lane_of, row_of)
+        for r, layer, saturation in transported(load, field, 3, width - 4, layers):
+            store("sat", r, layer, saturation)
+            pick(picked[2], saturation, layer * width + r, lane_of, row_of)
+        for n in range(3):
+            perf_ref[n, at_group, :] = jnp.concatenate(picked[n], axis=1)
+
+
+def edge_kernel(
+    dims, rank_ref, low_ref, high_ref, state_ref, shared_ref, perf_ref, place_ref, chosen_ref,
+    slot_ref, press_ref, sat_ref, rates_ref, added_ref, gathered_ref,
+):
+    local_count, layers, width, tile_count = dims
+    rows = layers * width
+    depth = low_ref.shape[1]
+    halves = depth // LANES
+    kept, added = state_slots(layers, width)
+    rim_rows = RIM * layers * local_count
+    has_low = (rank_ref[0] > 0).astype(jnp.float32)
+    has_high = (rank_ref[0] < tile_count - 1).astype(jnp.float32)
+    rims = [
+        derived_fields(
+            *(
+                ref[rim_rows + f * GROUP : rim_rows + (f + 1) * GROUP, :].astype(jnp.float32)
+                for f in range(4)
+            )
+        )
+        for ref in (low_ref, high_ref)
+    ]
+    slots = place_ref.shape[1]
+
+    def field(name, r, layer):
+        if 0 <= r < width:
+            tile = shared_ref[FIELD_NAMES.index(name) * rows + layer * width + r]
+            return jnp.concatenate([tile] * (GROUP // 8), axis=0)
+        part, at = (rims[0], r + RIM) if r < 0 else (rims[1], r - width)
+        at = layer * RIM + at
+        return part[name][at : at + 1, :]
+
+    @pl.loop(0, local_count // GROUP)
+    def _(group):
+        at_group = pl.ds(pl.multiple_of(group * GROUP, GROUP), GROUP)
+        lane_of, row_of = slot_parts(place_ref[:8, :]), slot_parts(place_ref[8:, :])
+        parts = slots // LANES
+        picked = [
+            [perf_ref[n, at_group, p * LANES : (p + 1) * LANES] for p in range(parts)]
+            for n in range(3)
+        ]
+
+        def load(kind, r, layer):
+            if (kind, r, layer) in added:
+                return added_ref[added[kind, r, layer]]
+            return state_ref[kept[kind, r, layer], at_group, :]
+
+        def store(kind, r, layer, values_in):
+            added_ref[added[kind, r, layer]] = values_in
+
+        for r in list(range(-RIM, 0)) + list(range(width, width + RIM)):
+            ref, i = (low_ref, r + RIM) if r < 0 else (high_ref, r - width)
+            for layer in range(layers):
+                at = (i * layers + layer) * local_count + group * GROUP
+                values = ref[pl.ds(pl.multiple_of(at, GROUP), GROUP), :].astype(jnp.float32)
+                store("half", r, layer, 0.5 * jnp.exp(-values))
+        for r in (-3, -2, -1, width - 1, width, width + 1):
+            for layer in range(layers):
+                face = reciprocal(load("half", r, layer) + load("half", r + 1, layer))
+                if r == -1:
+                    face = face * has_low
+                if r == width - 1:
+                    face = face * has_high
+                store("face_x", r, layer, face)
+        for r in (-2, -1, width, width + 1):
+            for layer in range(layers):
+                sides = [
+                    (load("face_x", r - 1, layer), r - 1), (load("face_x", r, layer), r + 1)
+                ]
+                top, bottom = cell_faces(load, store, field, r, layer, layers, sides)
+                bottom = reciprocal(bottom)
+                store("first", r, layer, top * bottom)
+                store("inverse", r, layer, bottom)
+        for r, face_row, towards in ((0, -1, -1), (width - 1, width - 1, width)):
+            for layer in range(layers):
+                face = load("face_x", face_row, layer)
+                top = state_ref[kept["first", r, layer], at_group, :]
+                bottom = state_ref[kept["inverse", r, layer], at_group, :]
+                bottom = reciprocal(bottom + face)
+                store("first", r, layer, (top + face * field("p0", towards, layer)) * bottom)
+                store("inverse", r, layer, bottom)
+        for r in (-1, 0, 1, width - 2, width - 1, width):
+            second_sweep(load, store, field, r, layers)
+
+        def put(ref, r, layer, values_in):
+            for h in range(halves):
+                at = pl.ds(
+                    group * GROUP * rows * halves + (layer * halves + h) * width + r,
+                    GROUP, stride=rows * halves,
+                )
+                ref[at, :] = values_in[:, h * LANES : (h + 1) * LANES]
+
+        for r in range(width):
+            for layer in range(layers):
+                here = load("last", r, layer)
+                put(press_ref, r, layer, here)
+                if ("last", r, layer) in added:
+                    pick(picked[1], here, layer * width + r, lane_of, row_of)
+        for first_row, last_row in ((0, 2), (width - 3, width - 1)):
+            for r, layer, saturation in transported(load, field, first_row, last_row, layers):
+                put(sat_ref, r, layer, saturation)
+                pick(picked[2], saturation, layer * width + r, lane_of, row_of)
+        for r in range(3, width - 3):
+            for layer in range(layers):
+                put(sat_ref, r, layer, load("sat", r, layer))
+        for n in range(3):
+            gathered_ref[n, at_group, :] = jnp.concatenate(picked[n], axis=1)
+
+    mobility = water_frac(gathered_ref[2]) * reciprocal(2.0 * gathered_ref[0])
+    terms = mobility * (gathered_ref[1] - slot_ref[:1, :]) * slot_ref[8:9, :]
+    sums = lax.dot_general(
+        pieces(terms), chosen_ref[...], (((1,), (1,)), ((), ())),
+        preferred_element_type=jnp.float32,
     )
-    sums = lax.dot_general(
-        pieces(terms), chosen, (((1,), (1,)), ((), ())), preferred_element_type=jnp.float32
-    )
-    partial_rates = (sums[:GROUP] + sums[GROUP : 2 * GROUP]) + sums[2 * GROUP :]
-    rates_ref[...] = partial_rates
+    rates_ref[...] = (sums[:local_count] + sums[local_count : 2 * local_count]) + sums[
+        2 * local_count :
+    ]
 
 
 def invert_panel(columns):
@@ -452,38 +608,51 @@
     low_rows, high_rows = send_both(up_rows, down_rows, "tile")
     anomaly_all = lax.all_gather(anomaly, "member", axis=0, tiled=True)
 
-    def whole(array):
-        return pl.BlockSpec(array.shape, lambda g: (0,) * array.ndim)
-
-    block = pl.BlockSpec((GROUP * rows * (strip_depth // LANES), LANES), lambda g: (g, 0))
-    smem = pl.BlockSpec(memory_space=pltpu.SMEM)
-    perfs = [perf_cell[None], perf_well[None], well_press[None]]
-    span = strip_width + 2 * RIM
+    kept, added = state_slots(layers, strip_width)
+    smem, vmem = pl.BlockSpec(memory_space=pltpu.SMEM), pl.BlockSpec(memory_space=pltpu.VMEM)
+    anywhere = pl.BlockSpec(memory_space=pl.ANY)
+    inner_params = pltpu.CompilerParams(vmem_limit_bytes=28 * 2**20)
+
+    def f32(*shape):
+        return jax.ShapeDtypeStruct(shape, jnp.float32)
+
+    handed = pl.pallas_call(
+        functools.partial(inner_kernel, (local_count, layers, strip_width)),
+        in_specs=[smem] + [vmem] * 5,
+        out_specs=(vmem,) * 6,
+        out_shape=(
+            f32(len(kept), local_count, strip_depth),
+            f32(len(FIELD_NAMES) * rows, 8, strip_depth),
+            f32(3, local_count, slots),
+            jax.ShapeDtypeStruct((16, slots), jnp.int32),
+            jax.ShapeDtypeStruct((well_count, slots), jnp.bfloat16),
+            f32(16, slots),
+        ),
+        scratch_shapes=[pltpu.VMEM((rows, GROUP, strip_depth), jnp.float32)],
+        compiler_params=inner_params,
+        cost_estimate=pl.CostEstimate(
+            flops=10**10, bytes_accessed=24 * flat_perm.size, transcendentals=0
+        ),
+    )(perf_count, flat_perm, fields, perf_cell[None], perf_well[None], well_press[None])
     flat_press, flat_sat, partial_rates = pl.pallas_call(
-        functools.partial(physics_kernel, (local_count, layers, strip_width, tile_count)),
-        grid=(local_count // GROUP,),
-        in_specs=[smem, smem, block, whole(low_rows), whole(high_rows)]
-        + [whole(array) for array in [fields] + perfs],
-        out_specs=(
-            block,
-            block,
-            pl.BlockSpec((GROUP, well_count), lambda g: (g, 0)),
-        ),
+        functools.partial(edge_kernel, (local_count, layers, strip_width, tile_count)),
+        in_specs=[smem] + [vmem] * 8,
+        out_specs=(vmem,) * 3,
         out_shape=(
-            jax.ShapeDtypeStruct(flat_perm.shape, jnp.float32),
-            jax.ShapeDtypeStruct(flat_perm.shape, jnp.float32),
-            jax.ShapeDtypeStruct((local_count, well_count), jnp.float32),
-        ),
-        scratch_shapes=[pltpu.VMEM((span * layers, GROUP, strip_depth), jnp.float32)] * 7,
-        compiler_params=params,
+            f32(*flat_perm.shape), f32(*flat_perm.shape), f32(local_count, well_count)
+        ),
+        scratch_shapes=[
+            pltpu.VMEM((len(added), GROUP, strip_depth), jnp.float32),
+            pltpu.VMEM((3, local_count, slots), jnp.float32),
+        ],
+        compiler_params=inner_params,
         cost_estimate=pl.CostEstimate(
-            flops=200 * flat_perm.size, bytes_accessed=16 * flat_perm.size, transcendentals=0
-        ),
-    )(perf_count, tile_rank[None], flat_perm, low_rows, high_rows, fields, *perfs)
+            flops=10**10, bytes_accessed=24 * flat_perm.size, transcendentals=0
+        ),
+    )(tile_rank[None], low_rows, high_rows, *handed)
     own_rates = sum_over(partial_rates, "tile")
     well_rates = lax.dynamic_slice_in_dim(own_rates, tile_rank * well_share, well_share, 1)
     rates_all = lax.all_gather(own_rates, "member", axis=0, tiled=True)
-    vmem, anywhere = pl.BlockSpec(memory_space=pltpu.VMEM), pl.BlockSpec(memory_space=pl.ANY)
     new_flat = pl.pallas_call(
         functools.partial(update_kernel, (local_count, layers, strip_width)),
         out_shape=jax.ShapeDtypeStruct(flat_perm.shape, jnp.float32),

time: 91.7 us -> 88.8 us (0.968)
  local copies, waits for them, and re-layouts: 1.46 us -> 10.1 us
  waiting for transfers between devices: 8.15 us -> 0.02 us
  blocking collectives: 26.1 us -> 22.4 us
    unnamed x6 -> x16, local copies, waits for them, and re-layouts: 0.78 us -> 9.4 us
    ppermute x1, waiting for transfers between devices: 8.13 us -> 0.01 us  [send_both(): lax.ppermute(up_rows, axis, forward)]
    all_gather x2 -> x3, blocking collectives: 20.1 us -> 16.4 us  [sum_over(): array = jnp.sum(lax.all_gather(array, axis, axis_index_groups=groups), 0)]
    pallas_call x1 -> x2, Pallas kernels: 22.4 us -> 22.5 us  [the longest x1 12.2 us: per_device(): pl.pallas_call(functools.partial(edge_kernel, (local_count, layers, strip...]
  transfers between devices with their start and end apart: 3 -> 3, of which waited for: 1 -> 0; matrix products, arithmetic and copies ran while one was open for 1% -> 1% of each run, Pallas kernels for 24% -> 26%
where the time goes in v2:
time: 88.8 us; the launch traced here: 88.3 us
  Pallas kernels  33.4 us (38%)
  blocking collectives  22.4 us (25%)
  between operations  14.8 us (17%)
  local copies, waits for them, and re-layouts  10.1 us (11%)
  starting transfers between devices  6.19 us (7%)
  other arithmetic  1.49 us (2%)
    all_gather x3, blocking collectives, sum_over(): array = jnp.sum(lax.all_gather(array, axis, axis_index_groups=groups), 0)  16.4 us
    pallas_call x1, Pallas kernels, per_device(): pl.pallas_call(functools.partial(edge_kernel, (local_count, layers, strip...  12.2 us
    pallas_call x1, Pallas kernels, per_device(): pl.pallas_call(functools.partial(inner_kernel, (local_count, layers, stri...  10.4 us
    unnamed x16, local copies, waits for them, and re-layouts  9.4 us
    pallas_call x1, Pallas kernels, per_device(): pl.pallas_call(functools.partial(update_kernel, (local_count, layers, str...  8.06 us
    all_gather x1, blocking collectives, per_device(): rates_all = lax.all_gather(own_rates, 'member', axis=0, tiled=True)  6.06 us
    ppermute x1, starting transfers between devices, send_both(): lax.ppermute(up_rows, axis, forward)  4.86 us
    pallas_call x1, Pallas kernels, per_device(): pl.pallas_call(functools.partial(pack_kernel, (local_count, layers, strip...  2.78 us
  transfers between devices with their start and end apart: 3, of which 0 were waited for; matrix products, arithmetic and copies ran while one was open for 1% of the time, Pallas kernels for 26%

profile of v2, /device:TPU:0, one launch (start us, length us, event | category | flops | bytes accessed | tf_op | source)
XLA Modules:
  0.0 88.3 jit_solution(14837429195533582326)
XLA Ops:
  7.2 0.0 all-gather.5.cloned.1.call-start
  7.2 1.5 %pad_maximum_fusion = f32[4,4,8,256]{3,2,1,0:T(8,128)} fusion(f32[1,4,8,256]{3,2,1,0:T(8,128)} %bitcast.46, f32[1,4,8,256]{3,2,1,0:T(8,128)} %bitcast.47, f32[1,4,8,256]{3,2,1,0:T(8,128)} %bitcast.48, f32[1,4,8,256]{3,2,1,0:T(8,128)} %bitcast.49), kind=kLoop, calls=%fused_computation | loop fusion | flops 98304 | bytes 262144 | tf_op jit(solution)/shard_map/stack | solution.py:589
  8.7 2.8 %shard_map.147 = (bf16[448,256]{1,0:T(8,128)(2,1)}, bf16[448,256]{1,0:T(8,128)(2,1)}, bf16[1024,256]{1,0:T(8,128)(2,1)}) custom-call(f32[2048,128]{1,0:T(8,128)} %bitcast.34, f32[128,256]{1,0:T(8,128)} %bitcast.37), custom_call_target="tpu_custom_call" | custom-call | flops 1048576 | bytes 2097152 | tf_op jit(solution)/shard_map/pallas_call | solution.py:593
  11.5 0.0 all-gather.5.cloned.1.call-update
  11.5 4.9 %collective-permute-start = (bf16[448,256]{1,0:T(8,128)(2,1)}, bf16[448,256]{1,0:T(8,128)(2,1)S(1)}, u32[]{:S(2)}, u32[]{:S(2)}) collective-permute-start(bf16[448,256]{1,0:T(8,128)(2,1)} %get-tuple-element.16), channel_id=1, source_target_pairs={{0,4},{4,8},{8,12},{12,16},{16,20},{20,24},{24,28},{1,5},{5,9},{9,... | collective-permute-start | bytes 688136 | tf_op jit(solution)/shard_map/ppermute | solution.py:55
  16.4 1.3 %collective-permute-start.1 = (bf16[448,256]{1,0:T(8,128)(2,1)}, bf16[448,256]{1,0:T(8,128)(2,1)S(1)}, u32[]{:S(2)}, u32[]{:S(2)}) collective-permute-start(bf16[448,256]{1,0:T(8,128)(2,1)} %get-tuple-element.17), channel_id=1, source_target_pairs={{4,0},{8,4},{12,8},{16,12},{20,16},{24,20},{28,24},{5,1},{9,5},{13... | collective-permute-start | bytes 688136 | tf_op jit(solution)/shard_map/ppermute | solution.py:55
  18.3 0.0 copy-start
  18.3 1.2 %copy-done = f32[32,4,8,256]{3,2,1,0:T(8,128)S(1)} copy-done((f32[32,4,8,256]{3,2,1,0:T(8,128)S(1)}, f32[32,4,8,256]{3,2,1,0:T(8,128)}, u32[]{:S(2)}) %copy-start) | copy-done | bytes 1048600
  19.5 0.0 copy-start.1
  19.5 0.9 %copy-done.1 = f32[4,4,8,256]{3,2,1,0:T(8,128)S(1)} copy-done((f32[4,4,8,256]{3,2,1,0:T(8,128)S(1)}, f32[4,4,8,256]{3,2,1,0:T(8,128)}, u32[]{:S(2)}) %copy-start.1) | copy-done | bytes 131096
  20.4 0.0 copy-start.2
  20.4 0.7 copy-done.2
  21.1 0.0 copy-start.3
  21.1 0.7 copy-done.3
  21.8 0.0 copy-start.4
  21.8 0.7 copy-done.4
  22.5 10.4 %shard_map.148 = (f32[180,32,256]{2,1,0:T(8,128)S(1)}, f32[256,8,256]{2,1,0:T(8,128)S(1)}, f32[3,32,256]{2,1,0:T(8,128)S(1)}, s32[16,256]{1,0:T(8,128)S(1)}, bf1...) custom-call(s32[1]{0:T(128)S(6)} %copy.16.count_ref, f32[2048,128]{1,0:T(8,128)S(1)} %bitcast.36, ...), custom_call_target="tpu_custom_call" | custom-call | flops 10000000000 | bytes 6291456 | tf_op jit(solution)/shard_map/pallas_call | solution.py:619
  32.9 0.0 copy-start.5
  32.9 2.5 %copy-done.5 = f32[180,32,256]{2,1,0:T(8,128)} copy-done((f32[180,32,256]{2,1,0:T(8,128)}, f32[180,32,256]{2,1,0:T(8,128)S(1)}, u32[]{:S(2)}) %copy-start.5) | copy-done | bytes 5898264
  35.4 0.0 collective-permute-done.low_ref
  35.4 0.0 collective-permute-done.1.high_ref
  35.4 0.0 copy-start.6
  35.4 2.7 %copy-done.6 = f32[180,32,256]{2,1,0:T(8,128)S(1)} copy-done((f32[180,32,256]{2,1,0:T(8,128)S(1)}, f32[180,32,256]{2,1,0:T(8,128)}, u32[]{:S(2)}) %copy-start.6) | copy-done | bytes 5898264
  38.1 12.2 %shard_map.149 = (f32[2048,128]{1,0:T(8,128)}, f32[2048,128]{1,0:T(8,128)}, f32[32,256]{1,0:T(8,128)S(1)}) custom-call(s32[1]{0:T(128)} %bitcast.rank_ref, bf16[448,256]{1,0:T(8,128)(2,1)S(1)} %collective-permute-done.low_ref, bf16[448,256]{1,0:T(8,128)(2,1)S(1)} %collective-permute-done.1.high_ref, f32[180,32,256]{2,1,0:T(8,128)S(1)} %copy-done.6, ...), custom_call_target="tpu_custom_call" | custom-call | flops 10000000000 | bytes 6291456 | tf_op jit(solution)/shard_map/pallas_call | solution.py:637
  50.3 7.2 %all-gather = f32[64,256]{1,0:T(8,128)S(1)} all-gather(f32[32,256]{1,0:T(8,128)S(1)} %get-tuple-element.24), channel_id=2, replica_groups={{0,16},{4,20},{8,24},{12,28},{1,17},{5,21},{9,25},{13,29},{2,18},{6,22}..., dimensions={0}, use_global_device_ids=true | all-gather | bytes 98304 | tf_op jit(solution)/shard_map/all_gather | solution.py:69
  57.5 4.6 %all-gather.1 = f32[64,256]{1,0:T(8,128)S(1)} all-gather(f32[32,256]{1,0:T(8,128)S(1)} %reduce_sum.27), channel_id=3, replica_groups={{0,8},{4,12},{16,24},{20,28},{1,9},{5,13},{17,25},{21,29},{2,10},{6,14}..., dimensions={0}, use_global_device_ids=true | all-gather | bytes 98304 | tf_op jit(solution)/shard_map/all_gather | solution.py:69
  62.1 4.6 %all-gather.2 = f32[64,256]{1,0:T(8,128)S(1)} all-gather(f32[32,256]{1,0:T(8,128)S(1)} %reduce_sum.28), channel_id=4, replica_groups={{0,4},{8,12},{16,20},{24,28},{1,5},{9,13},{17,21},{25,29},{2,6},{10,14}..., dimensions={0}, use_global_device_ids=true | all-gather | bytes 98304 | tf_op jit(solution)/shard_map/all_gather | solution.py:69
  66.7 0.0 copy-start.7
  66.7 6.1 %all_gather.30.rates_ref = f32[128,256]{1,0:T(8,128)} all-gather(f32[32,256]{1,0:T(8,128)S(1)} %reduce_sum.29.own_ref), channel_id=1, replica_groups=mesh['tile'=8,'member'=4] {'member'}, dimensions={0}, use_global_device_ids=true | all-gather | bytes 163840 | tf_op jit(solution)/shard_map/all_gather | solution.py:655
  72.7 0.7 constant_dynamic-slice_fusion
  73.4 0.0 all-gather.5.cloned.1.call-done.anomaly_ref
  73.4 0.0 copy-done.7
  73.4 8.1 %shard_map.150 = f32[2048,128]{1,0:T(8,128)} custom-call(f32[128,256]{1,0:T(8,128)} %all_gather.30.rates_ref, f32[32,256]{1,0:T(8,128)} %copy-done.7, f32[32,256]{1,0:T(8,128)} %noise_ref.1, f32[1,256]{1,0:T(1,128)} %bitcast.50, f32[1,256]{1,0:T(1,128)} %bitcast.51, bf16[4096,256]{1,0:T(8,128)(2,1)} %all-gather.5.cloned.1.call-done.anomaly_ref, ...), custom_call_target="tpu_custom_call" | custom-call | flops 25165824 | bytes 4194304 | tf_op jit(solution)/shard_map/pallas_call | solution.py:656
  (3 shorter events, 0.0 us)
Async XLA Ops:
  7.2 66.3 %all-gather.5.cloned.1.call-start = ((), (), s32[]{:S(2)}) async-start(), calls=%async_computation | async-start | bytes 2621440 | tf_op jit(solution)/shard_map/all_gather | solution.py:609
  11.5 23.9 %collective-permute-start = (bf16[448,256]{1,0:T(8,128)(2,1)}, bf16[448,256]{1,0:T(8,128)(2,1)S(1)}, u32[]{:S(2)}, u32[]{:S(2)}) collective-permute-start(bf16[448,256]{1,0:T(8,128)(2,1)} %get-tuple-element.16), channel_id=1, source_target_pairs={{0,4},{4,8},{8,12},{12,16},{16,20},{20,24},{24,28},{1,5},{5,9},{9,... | collective-permute-start | bytes 688136 | tf_op jit(solution)/shard_map/ppermute | solution.py:55
  16.4 19.1 %collective-permute-start.1 = (bf16[448,256]{1,0:T(8,128)(2,1)}, bf16[448,256]{1,0:T(8,128)(2,1)S(1)}, u32[]{:S(2)}, u32[]{:S(2)}) collective-permute-start(bf16[448,256]{1,0:T(8,128)(2,1)} %get-tuple-element.17), channel_id=1, source_target_pairs={{4,0},{8,4},{12,8},{16,12},{20,16},{24,20},{28,24},{5,1},{9,5},{13... | collective-permute-start | bytes 688136 | tf_op jit(solution)/shard_map/ppermute | solution.py:55
  18.3 1.2 %copy-start = (f32[32,4,8,256]{3,2,1,0:T(8,128)S(1)}, f32[32,4,8,256]{3,2,1,0:T(8,128)}, u32[]{:S(2)}) copy-start(f32[32,4,8,256]{3,2,1,0:T(8,128)} %param.12) | copy-start | bytes 3145732
  19.5 0.9 %copy-start.1 = (f32[4,4,8,256]{3,2,1,0:T(8,128)S(1)}, f32[4,4,8,256]{3,2,1,0:T(8,128)}, u32[]{:S(2)}) copy-start(f32[4,4,8,256]{3,2,1,0:T(8,128)} %pad_maximum_fusion) | copy-start | bytes 393220
  20.4 0.7 copy-start.2
  21.1 0.7 copy-start.3
  21.8 0.7 copy-start.4
  32.9 2.5 %copy-start.5 = (f32[180,32,256]{2,1,0:T(8,128)}, f32[180,32,256]{2,1,0:T(8,128)S(1)}, u32[]{:S(2)}) copy-start(f32[180,32,256]{2,1,0:T(8,128)S(1)} %get-tuple-element.18.state_ref) | copy-start | bytes 17694724
  35.4 2.7 %copy-start.6 = (f32[180,32,256]{2,1,0:T(8,128)S(1)}, f32[180,32,256]{2,1,0:T(8,128)}, u32[]{:S(2)}) copy-start(f32[180,32,256]{2,1,0:T(8,128)} %copy-done.5) | copy-start | bytes 17694724
  66.7 6.7 %copy-start.7 = (f32[32,256]{1,0:T(8,128)}, f32[32,256]{1,0:T(8,128)S(1)}, u32[]{:S(2)}) copy-start(f32[32,256]{1,0:T(8,128)S(1)} %reduce_sum.29.own_ref) | copy-start | bytes 98308
Sparse Core Ops, SparseCore 0:
  11.6 25.2 all-gather.4

commit v3 on v2

--- a/solution.py
+++ b/solution.py
@@ -57,16 +57,16 @@
 
 def sum_over(array, axis):
     count = lax.axis_size(axis)
-    stride = count
-    while stride > 1:
-        radix = 2
-        stride //= radix
+    stride = 1
+    while stride < count:
+        around = (0, 1, 3, 2) if count // stride % 4 == 0 else (0, 1)
         groups = [
-            [base + low + i * stride for i in range(radix)]
-            for base in range(0, count, stride * radix)
+            [base + low + i * stride for i in around]
+            for base in range(0, count, stride * len(around))
             for low in range(stride)
         ]
         array = jnp.sum(lax.all_gather(array, axis, axis_index_groups=groups), 0)
+        stride *= len(around)
     return array
 
 
@@ -89,7 +89,9 @@
     return squared * reciprocal(squared + VISCOSITY_RATIO * rest * rest)
 
 
-def pack_kernel(dims, root, perm_ref, fields_ref, up_ref, down_ref, anomaly_ref, up_rows, down_rows):
+def pack_kernel(
+    dims, root, perm_ref, fields_ref, up_ref, down_ref, anomaly_ref, up_rows, down_rows
+):
     local_count, layers, width = dims
     up_rows[...] = jnp.zeros_like(up_rows)
     down_rows[...] = jnp.zeros_like(down_rows)
@@ -128,9 +130,10 @@
     near = [-2, -1, width, width + 1]
 
     def place(where, kind, rows, count=layers):
+        where[kind] = {}
         for r in rows:
             for layer in range(count):
-                where[kind, r, layer] = len(where)
+                where[kind][r, layer] = len(where[kind])
 
     place(kept, "half", (0, width - 1))
     place(kept, "face_x", range(width - 1))
@@ -147,6 +150,10 @@
     place(added, "inverse", near + [0, width - 1])
     place(added, "first", near + [0, width - 1])
     place(added, "last", [-1, 0, 1, width - 2, width - 1, width])
+    first = 0
+    for places in added.values():
+        for key in places:
+            places[key], first = first, first + 1
     return kept, added
 
 
@@ -255,33 +262,42 @@
     return [jnp.concatenate([part] * (GROUP // part.shape[0]), axis=0) for part in parts]
 
 
-def inner_kernel(
-    dims, count_ref, perm_ref, fields_ref, cell_ref, well_ref, bhp_ref,
-    state_ref, shared_ref, perf_ref, place_ref, chosen_ref, slot_ref, half_ref,
-):
+def inner_kernel(dims, count_ref, *refs):
     local_count, layers, width = dims
     rows = layers * width
+    kept, _ = state_slots(layers, width)
+    perm_ref, fields_ref, refs = refs[0], refs[1], refs[2:]
+    states, refs = dict(zip(kept, refs)), refs[len(kept) :]
+    shared_ref, perf_ref, place_ref, chosen_ref, slot_ref, half_ref = refs
     depth = fields_ref.shape[1]
     halves = depth // LANES
-    kept, _ = state_slots(layers, width)
     fields = derived_fields(*(fields_ref[f * rows : (f + 1) * rows, :] for f in range(4)))
     for n, name in enumerate(FIELD_NAMES):
         for row in range(rows):
             shared_ref[n * rows + row] = jnp.broadcast_to(
                 fields[name][row : row + 1, :], (8, depth)
             )
-    slots = cell_ref.shape[1]
-    wells = bhp_ref.shape[1]
-    cells = jnp.broadcast_to(cell_ref[...], (8, slots))
+    wells, slots = chosen_ref.shape
+    cell, well, bhp = (
+        jnp.concatenate(
+            [fields_ref[i : i + 1, :] for i in range(first, first + size // depth)], axis=1
+        )
+        for first, size in (
+            (4 * rows, slots),
+            (4 * rows + slots // depth, slots),
+            (4 * rows + 2 * slots // depth, wells),
+        )
+    )
+    cells = jnp.broadcast_to(cell.astype(jnp.int32), (8, slots))
     place_ref[:8, :] = cells % LANES
     place_ref[8:, :] = cells // LANES
     chosen = (
-        (lax.broadcasted_iota(jnp.int32, (wells, slots), 0) == well_ref[...])
+        (lax.broadcasted_iota(jnp.int32, (wells, slots), 0) == well.astype(jnp.int32))
         .astype(jnp.float32)
         .astype(jnp.bfloat16)
     )
     chosen_ref[...] = chosen
-    bhp = pieces(jnp.broadcast_to(bhp_ref[...], (GROUP, wells)))
+    bhp = pieces(jnp.broadcast_to(bhp, (GROUP, wells)))
     bhp = jnp.dot(bhp, chosen, preferred_element_type=jnp.float32)
     live = (lax.broadcasted_iota(jnp.int32, (8, slots), 1) < count_ref[0]).astype(jnp.float32)
     slot_ref[:8, :] = (bhp[:8] + bhp[GROUP : GROUP + 8]) + bhp[2 * GROUP : 2 * GROUP + 8]
@@ -301,10 +317,10 @@
         def load(kind, r, layer):
             if kind == "half":
                 return half_ref[layer * width + r]
-            return state_ref[kept[kind, r, layer], at_group, :]
+            return states[kind][kept[kind][r, layer], at_group, :]
 
         def store(kind, r, layer, values_in):
-            state_ref[kept[kind, r, layer], at_group, :] = values_in
+            states[kind][kept[kind][r, layer], at_group, :] = values_in
 
         for r in range(width):
             for layer in range(layers):
@@ -356,15 +372,15 @@
             perf_ref[n, at_group, :] = jnp.concatenate(picked[n], axis=1)
 
 
-def edge_kernel(
-    dims, rank_ref, low_ref, high_ref, state_ref, shared_ref, perf_ref, place_ref, chosen_ref,
-    slot_ref, press_ref, sat_ref, rates_ref, added_ref, gathered_ref,
-):
+def edge_kernel(dims, rank_ref, low_ref, high_ref, *refs):
     local_count, layers, width, tile_count = dims
     rows = layers * width
     depth = low_ref.shape[1]
     halves = depth // LANES
     kept, added = state_slots(layers, width)
+    states, refs = dict(zip(kept, refs)), refs[len(kept) :]
+    shared_ref, perf_ref, place_ref, chosen_ref, slot_ref = refs[:5]
+    press_ref, sat_ref, rates_ref, added_ref, gathered_ref = refs[5:]
     rim_rows = RIM * layers * local_count
     has_low = (rank_ref[0] > 0).astype(jnp.float32)
     has_high = (rank_ref[0] < tile_count - 1).astype(jnp.float32)
@@ -398,12 +414,12 @@
         ]
 
         def load(kind, r, layer):
-            if (kind, r, layer) in added:
-                return added_ref[added[kind, r, layer]]
-            return state_ref[kept[kind, r, layer], at_group, :]
+            if (r, layer) in added.get(kind, {}):
+                return added_ref[added[kind][r, layer]]
+            return states[kind][kept[kind][r, layer], at_group, :]
 
         def store(kind, r, layer, values_in):
-            added_ref[added[kind, r, layer]] = values_in
+            added_ref[added[kind][r, layer]] = values_in
 
         for r in list(range(-RIM, 0)) + list(range(width, width + RIM)):
             ref, i = (low_ref, r + RIM) if r < 0 else (high_ref, r - width)
@@ -431,8 +447,8 @@
         for r, face_row, towards in ((0, -1, -1), (width - 1, width - 1, width)):
             for layer in range(layers):
                 face = load("face_x", face_row, layer)
-                top = state_ref[kept["first", r, layer], at_group, :]
-                bottom = state_ref[kept["inverse", r, layer], at_group, :]
+                top = states["first"][kept["first"][r, layer], at_group, :]
+                bottom = states["inverse"][kept["inverse"][r, layer], at_group, :]
                 bottom = reciprocal(bottom + face)
                 store("first", r, layer, (top + face * field("p0", towards, layer)) * bottom)
                 store("inverse", r, layer, bottom)
@@ -451,7 +467,7 @@
             for layer in range(layers):
                 here = load("last", r, layer)
                 put(press_ref, r, layer, here)
-                if ("last", r, layer) in added:
+                if (r, layer) in added["last"]:
                     pick(picked[1], here, layer * width + r, lane_of, row_of)
         for first_row, last_row in ((0, 2), (width - 3, width - 1)):
             for r, layer, saturation in transported(load, field, first_row, last_row, layers):
@@ -586,10 +602,18 @@
     rows = layers * strip_width
     slots = perf_cell.shape[0]
     flat_perm = fold(log_perm)
-    fields = jnp.stack([start_pressure, start_sat, source, storage]).reshape(-1, strip_depth)
+    fields = jnp.concatenate(
+        [
+            array.astype(jnp.float32).reshape(-1, strip_depth)
+            for array in (
+                start_pressure, start_sat, source, storage, perf_cell, perf_well, well_press
+            )
+        ]
+    )
+    in_hbm = pl.BlockSpec(memory_space=pltpu.HBM)
     rim_shape = (RIM * layers * local_count + 4 * GROUP, strip_depth)
     field_scratch = pltpu.VMEM((4 * GROUP, strip_depth), jnp.float32)
-    params = pltpu.CompilerParams(vmem_limit_bytes=60 * 2**20)
+    params = pltpu.CompilerParams(vmem_limit_bytes=20 * 2**20)
     up_rows, down_rows, anomaly = pl.pallas_call(
         functools.partial(
             pack_kernel, (local_count, layers, strip_width), (members - 1) ** 0.5
@@ -610,18 +634,16 @@
 
     kept, added = state_slots(layers, strip_width)
     smem, vmem = pl.BlockSpec(memory_space=pltpu.SMEM), pl.BlockSpec(memory_space=pltpu.VMEM)
-    anywhere = pl.BlockSpec(memory_space=pl.ANY)
-    inner_params = pltpu.CompilerParams(vmem_limit_bytes=28 * 2**20)
 
     def f32(*shape):
         return jax.ShapeDtypeStruct(shape, jnp.float32)
 
     handed = pl.pallas_call(
         functools.partial(inner_kernel, (local_count, layers, strip_width)),
-        in_specs=[smem] + [vmem] * 5,
-        out_specs=(vmem,) * 6,
+        in_specs=[smem] + [vmem] * 2,
+        out_specs=(vmem,) * (len(kept) + 5),
         out_shape=(
-            f32(len(kept), local_count, strip_depth),
+            *(f32(len(places), local_count, strip_depth) for places in kept.values()),
             f32(len(FIELD_NAMES) * rows, 8, strip_depth),
             f32(3, local_count, slots),
             jax.ShapeDtypeStruct((16, slots), jnp.int32),
@@ -629,23 +651,23 @@
             f32(16, slots),
         ),
         scratch_shapes=[pltpu.VMEM((rows, GROUP, strip_depth), jnp.float32)],
-        compiler_params=inner_params,
+        compiler_params=params,
         cost_estimate=pl.CostEstimate(
             flops=10**10, bytes_accessed=24 * flat_perm.size, transcendentals=0
         ),
-    )(perf_count, flat_perm, fields, perf_cell[None], perf_well[None], well_press[None])
+    )(perf_count, flat_perm, fields)
     flat_press, flat_sat, partial_rates = pl.pallas_call(
         functools.partial(edge_kernel, (local_count, layers, strip_width, tile_count)),
-        in_specs=[smem] + [vmem] * 8,
+        in_specs=[smem] + [vmem] * (len(kept) + 7),
         out_specs=(vmem,) * 3,
         out_shape=(
             f32(*flat_perm.shape), f32(*flat_perm.shape), f32(local_count, well_count)
         ),
         scratch_shapes=[
-            pltpu.VMEM((len(added), GROUP, strip_depth), jnp.float32),
+            pltpu.VMEM((sum(map(len, added.values())), GROUP, strip_depth), jnp.float32),
             pltpu.VMEM((3, local_count, slots), jnp.float32),
         ],
-        compiler_params=inner_params,
+        compiler_params=params,
         cost_estimate=pl.CostEstimate(
             flops=10**10, bytes_accessed=24 * flat_perm.size, transcendentals=0
         ),
@@ -656,14 +678,14 @@
     new_flat = pl.pallas_call(
         functools.partial(update_kernel, (local_count, layers, strip_width)),
         out_shape=jax.ShapeDtypeStruct(flat_perm.shape, jnp.float32),
-        in_specs=[vmem] * 5 + [anywhere] * 2,
+        in_specs=[vmem] * 5 + [in_hbm] * 2,
         out_specs=vmem,
         scratch_shapes=[
             pltpu.VMEM(anomaly_all.shape, jnp.bfloat16),
             pltpu.VMEM(flat_perm.shape, jnp.float32),
             pltpu.SemaphoreType.DMA((2,)),
         ],
-        compiler_params=params,
+        compiler_params=pltpu.CompilerParams(vmem_limit_bytes=60 * 2**20),
         cost_estimate=pl.CostEstimate(
             flops=12 * members**3, bytes_accessed=16 * flat_perm.size, transcendentals=0
         ),

time: 88.8 us -> 104 us (1.17)
  local copies, waits for them, and re-layouts: 10.1 us -> 25.3 us
  Pallas kernels: 33.4 us -> 32.2 us
    unnamed x16 -> x46, local copies, waits for them, and re-layouts: 9.4 us -> 20.8 us
    concatenate x0 -> x1, local copies, waits for them, and re-layouts: none -> 3.74 us  [per_device(): jnp.concatenate([array.astype(jnp.float32).reshape(-1, strip_depth) for a...]
    another operation x1 -> x0, other arithmetic: 1.47 us -> none  [per_device(): jnp.stack([start_pressure, start_sat, source, storage])]
    convert_element_type x0 -> x2, other arithmetic: none -> 1.36 us  [per_device(): array.astype(jnp.float32).reshape(-1, strip_depth)]
    pallas_call x1, Pallas kernels: 2.78 us -> 1.46 us  [per_device(): pl.pallas_call(functools.partial(pack_kernel, (local_count, layers, strip...]
    all_gather x3 -> x2, blocking collectives: 16.4 us -> 17.3 us  [sum_over(): array = jnp.sum(lax.all_gather(array, axis, axis_index_groups=groups), 0)]
  transfers between devices with their start and end apart: 3 -> 3, of which waited for: 0 -> 0; matrix products, arithmetic and copies ran while one was open for 1% -> 1% of each run, Pallas kernels for 26% -> 22%
where the time goes in v3:
time: 104 us; the launch traced here: 103 us
  Pallas kernels  32.2 us (31%)
  local copies, waits for them, and re-layouts  25.3 us (24%)
  blocking collectives  23.4 us (22%)
  between operations  14.8 us (14%)
  starting transfers between devices  6.19 us (6%)
  other arithmetic  1.38 us (1%)
    unnamed x46, local copies, waits for them, and re-layouts  20.8 us
    all_gather x2, blocking collectives, sum_over(): array = jnp.sum(lax.all_gather(array, axis, axis_index_groups=groups), 0)  17.3 us
    pallas_call x1, Pallas kernels, per_device(): pl.pallas_call(functools.partial(edge_kernel, (local_count, layers, strip...  12.3 us
    pallas_call x1, Pallas kernels, per_device(): pl.pallas_call(functools.partial(inner_kernel, (local_count, layers, stri...  10.4 us
    pallas_call x1, Pallas kernels, per_device(): pl.pallas_call(functools.partial(update_kernel, (local_count, layers, str...  8.06 us
    all_gather x1, blocking collectives, per_device(): rates_all = lax.all_gather(own_rates, 'member', axis=0, tiled=True)  6.06 us
    ppermute x1, starting transfers between devices, send_both(): lax.ppermute(up_rows, axis, forward)  4.86 us
    concatenate x1, local copies, waits for them, and re-layouts, per_device(): jnp.concatenate([array.astype(jnp.float32).reshape(-1, strip_depth) for a...  3.74 us
  transfers between devices with their start and end apart: 3, of which 0 were waited for; matrix products, arithmetic and copies ran while one was open for 1% of the time, Pallas kernels for 22%

profile of v3, /device:TPU:0, one launch (start us, length us, event | category | flops | bytes accessed | tf_op | source)
XLA Modules:
  0.0 103.1 jit_solution(13986629604915234190)
XLA Ops:
  7.2 0.0 all-gather.4.cloned.1.call-start
  7.2 0.7 convert_element_type.6
  7.9 0.7 convert_element_type.7
  8.6 3.7 %concatenate.3.fields_ref.refs_1_ = f32[131,256]{1,0:T(8,128)S(1)} concatenate(f32[32,256]{1,0:T(8,128)} %bitcast.38, f32[32,256]{1,0:T(8,128)} %bitcast.39, f32[32,256]{1,0:T(8,128)} %bitcast.40, f32[32,256]{1,0:T(8,128)} %bitcast.41, f32[1,256]{1,0:T(1,128)S(1)} %bitcast.42, f32[1,256]{1,0:T(1,128)S(1)} %bitcast.43, f32[1,256]{1,0:T(1,128)} %bitcast.44), dimensions={0} | concatenate | bytes 268288 | tf_op jit(solution)/shard_map/concatenate | solution.py:605
  12.3 0.0 copy-start
  12.3 1.2 %copy-done = f32[32,4,8,256]{3,2,1,0:T(8,128)S(1)} copy-done((f32[32,4,8,256]{3,2,1,0:T(8,128)S(1)}, f32[32,4,8,256]{3,2,1,0:T(8,128)}, u32[]{:S(2)}) %copy-start) | copy-done | bytes 1048600
  13.5 1.5 %shard_map.147 = (bf16[448,256]{1,0:T(8,128)(2,1)S(1)}, bf16[448,256]{1,0:T(8,128)(2,1)S(1)}, bf16[1024,256]{1,0:T(8,128)(2,1)}) custom-call(f32[2048,128]{1,0:T(8,128)S(1)} %bitcast.33, f32[131,256]{1,0:T(8,128)S(1)} %concatenate.3.fields_ref.refs_1_), custom_call_target="tpu_custom_call" | custom-call | flops 1048576 | bytes 2097152 | tf_op jit(solution)/shard_map/pallas_call | solution.py:617
  15.0 0.0 all-gather.4.cloned.1.call-update
  15.0 4.9 %collective-permute-start = (bf16[448,256]{1,0:T(8,128)(2,1)S(1)}, bf16[448,256]{1,0:T(8,128)(2,1)S(1)}, u32[]{:S(2)}, u32[]{:S(2)}) collective-permute-start(bf16[448,256]{1,0:T(8,128)(2,1)S(1)} %get-tuple-element.23), channel_id=1, source_target_pairs={{0,4},{4,8},{8,12},{12,16},{16,20},{20,24},{24,28},{1,5},{5,9},{9,... | collective-permute-start | bytes 688136 | tf_op jit(solution)/shard_map/ppermute | solution.py:55
  19.9 1.3 %collective-permute-start.1 = (bf16[448,256]{1,0:T(8,128)(2,1)S(1)}, bf16[448,256]{1,0:T(8,128)(2,1)S(1)}, u32[]{:S(2)}, u32[]{:S(2)}) collective-permute-start(bf16[448,256]{1,0:T(8,128)(2,1)S(1)} %get-tuple-element.24), channel_id=1, source_target_pairs={{4,0},{8,4},{12,8},{16,12},{20,16},{24,20},{28,24},{5,1},{9,5},{13... | collective-permute-start | bytes 688136 | tf_op jit(solution)/shard_map/ppermute | solution.py:55
  21.8 0.0 copy-start.1
  21.8 1.2 %copy-done.1 = f32[32,4,8,256]{3,2,1,0:T(8,128)S(1)} copy-done((f32[32,4,8,256]{3,2,1,0:T(8,128)S(1)}, f32[32,4,8,256]{3,2,1,0:T(8,128)}, u32[]{:S(2)}) %copy-start.1) | copy-done | bytes 1048600
  23.1 10.4 %shard_map.148 = (f32[8,32,256]{2,1,0:T(8,128)S(1)}, f32[28,32,256]{2,1,0:T(8,128)S(1)}, f32[32,32,256]{2,1,0:T(8,128)S(1)}, f32[24,32,256]{2,1,0:T(8,128)S(1)},...) custom-call(s32[1]{0:T(128)S(6)} %copy.16.count_ref, ...), custom_call_target="tpu_custom_call" | custom-call | flops 10000000000 | bytes 6291456 | tf_op jit(solution)/shard_map/pallas_call | solution.py:641
  33.4 0.0 copy-start.2
  33.4 1.0 copy-done.2
  34.4 0.0 copy-start.4
  34.4 1.0 copy-done.4
  35.4 0.0 copy-start.6
  35.4 1.0 copy-done.6
  36.3 0.0 copy-start.8
  36.4 0.9 copy-done.8
  37.3 0.0 copy-start.10
  37.3 0.9 copy-done.10
  38.2 0.0 copy-start.12
  38.2 0.8 copy-done.12
  39.0 0.0 copy-start.14
  39.0 0.7 copy-done.14
  39.7 0.0 copy-start.16
  39.7 0.7 copy-done.16
  40.3 0.0 copy-start.18
  40.3 0.6 copy-done.18
  40.9 0.0 copy-start.20
  40.9 0.6 copy-done.20
  41.6 0.0 collective-permute-done.low_ref
  41.6 0.0 collective-permute-done.1.high_ref
  41.6 0.0 copy-start.3
  41.6 1.2 %copy-done.3 = f32[32,32,256]{2,1,0:T(8,128)S(1)} copy-done((f32[32,32,256]{2,1,0:T(8,128)S(1)}, f32[32,32,256]{2,1,0:T(8,128)}, u32[]{:S(2)}) %copy-start.3) | copy-done | bytes 1048600
  42.8 0.0 copy-start.5
  42.8 1.2 %copy-done.5 = f32[32,32,256]{2,1,0:T(8,128)S(1)} copy-done((f32[32,32,256]{2,1,0:T(8,128)S(1)}, f32[32,32,256]{2,1,0:T(8,128)}, u32[]{:S(2)}) %copy-start.5) | copy-done | bytes 1048600
  44.0 0.0 copy-start.7
  44.0 1.2 %copy-done.7 = f32[32,32,256]{2,1,0:T(8,128)S(1)} copy-done((f32[32,32,256]{2,1,0:T(8,128)S(1)}, f32[32,32,256]{2,1,0:T(8,128)}, u32[]{:S(2)}) %copy-start.7) | copy-done | bytes 1048600
  45.2 0.0 copy-start.9
  45.2 1.2 %copy-done.9 = f32[28,32,256]{2,1,0:T(8,128)S(1)} copy-done((f32[28,32,256]{2,1,0:T(8,128)S(1)}, f32[28,32,256]{2,1,0:T(8,128)}, u32[]{:S(2)}) %copy-start.9) | copy-done | bytes 917528
  46.4 0.0 copy-start.11
  46.4 1.1 %copy-done.11 = f32[24,32,256]{2,1,0:T(8,128)S(1)} copy-done((f32[24,32,256]{2,1,0:T(8,128)S(1)}, f32[24,32,256]{2,1,0:T(8,128)}, u32[]{:S(2)}) %copy-start.11) | copy-done | bytes 786456
  47.6 0.0 copy-start.13
  47.6 1.0 %copy-done.13 = f32[16,32,256]{2,1,0:T(8,128)S(1)} copy-done((f32[16,32,256]{2,1,0:T(8,128)S(1)}, f32[16,32,256]{2,1,0:T(8,128)}, u32[]{:S(2)}) %copy-start.13) | copy-done | bytes 524312
  48.6 0.0 copy-start.15
  48.6 0.9 copy-done.15
  49.5 0.0 copy-start.17
  49.5 0.9 copy-done.17
  50.4 0.0 copy-start.19
  50.4 0.7 copy-done.19
  51.2 0.0 copy-start.21
  51.2 0.7 copy-done.21
  51.9 12.3 %shard_map.149 = (f32[2048,128]{1,0:T(8,128)}, f32[2048,128]{1,0:T(8,128)}, f32[32,256]{1,0:T(8,128)S(1)}) custom-call(s32[1]{0:T(128)} %bitcast.rank_ref, bf16[448,256]{1,0:T(8,128)(2,1)S(1)} %collective-permute-done.low_ref, bf16[448,256]{1,0:T(8,128)(2,1)S(1)} %collective-permute-done.1.high_ref, f32[8,32,256]{2,1,0:T(8,128)S(1)} %get-tuple-element.25.refs_0_, ...), custom_call_target="tpu_custom_call" | custom-call | flops 10000000000 | bytes 6291456 | tf_op jit(solution)/shard_map/pallas_call | solution.py:659
  64.2 11.8 %all-gather = f32[128,256]{1,0:T(8,128)S(1)} all-gather(f32[32,256]{1,0:T(8,128)S(1)} %get-tuple-element.38), channel_id=2, replica_groups={{0,4,12,8},{16,20,28,24},{1,5,13,9},{17,21,29,25},{2,6,14,10},{18,22,30..., dimensions={0}, use_global_device_ids=true | all-gather | bytes 163840 | tf_op jit(solution)/shard_map/all_gather | solution.py:68
  76.0 5.5 %all-gather.1 = f32[64,256]{1,0:T(8,128)S(1)} all-gather(f32[32,256]{1,0:T(8,128)S(1)} %reduce_sum.18), channel_id=3, replica_groups={{0,16},{4,20},{8,24},{12,28},{1,17},{5,21},{9,25},{13,29},{2,18},{6,22}..., dimensions={0}, use_global_device_ids=true | all-gather | bytes 98304 | tf_op jit(solution)/shard_map/all_gather | solution.py:68
  81.5 0.0 copy-start.22
  81.5 6.1 %all_gather.22.rates_ref = f32[128,256]{1,0:T(8,128)} all-gather(f32[32,256]{1,0:T(8,128)S(1)} %reduce_sum.19.own_ref), channel_id=1, replica_groups=mesh['tile'=8,'member'=4] {'member'}, dimensions={0}, use_global_device_ids=true | all-gather | bytes 163840 | tf_op jit(solution)/shard_map/all_gather | solution.py:677
  87.5 0.7 constant_dynamic-slice_fusion
  88.2 0.0 all-gather.4.cloned.1.call-done.anomaly_ref
  88.2 0.0 copy-done.22
  88.2 8.1 %shard_map.150 = f32[2048,128]{1,0:T(8,128)} custom-call(f32[128,256]{1,0:T(8,128)} %all_gather.22.rates_ref, f32[32,256]{1,0:T(8,128)} %copy-done.22, f32[32,256]{1,0:T(8,128)} %noise_ref.1, f32[1,256]{1,0:T(1,128)} %bitcast.45, f32[1,256]{1,0:T(1,128)} %bitcast.46, bf16[4096,256]{1,0:T(8,128)(2,1)} %all-gather.4.cloned.1.call-done.anomaly_ref, ...), custom_call_target="tpu_custom_call" | custom-call | flops 25165824 | bytes 4194304 | tf_op jit(solution)/shard_map/pallas_call | solution.py:678
  (2 shorter events, 0.0 us)
Async XLA Ops:
  7.2 81.1 %all-gather.4.cloned.1.call-start = ((), (), s32[]{:S(2)}) async-start(), calls=%async_computation | async-start | bytes 2621440 | tf_op jit(solution)/shard_map/all_gather | solution.py:633
  12.3 1.2 %copy-start = (f32[32,4,8,256]{3,2,1,0:T(8,128)S(1)}, f32[32,4,8,256]{3,2,1,0:T(8,128)}, u32[]{:S(2)}) copy-start(f32[32,4,8,256]{3,2,1,0:T(8,128)} %param.12) | copy-start | bytes 3145732
  15.0 26.5 %collective-permute-start = (bf16[448,256]{1,0:T(8,128)(2,1)S(1)}, bf16[448,256]{1,0:T(8,128)(2,1)S(1)}, u32[]{:S(2)}, u32[]{:S(2)}) collective-permute-start(bf16[448,256]{1,0:T(8,128)(2,1)S(1)} %get-tuple-element.23), channel_id=1, source_target_pairs={{0,4},{4,8},{8,12},{12,16},{16,20},{20,24},{24,28},{1,5},{5,9},{9,... | collective-permute-start | bytes 688136 | tf_op jit(solution)/shard_map/ppermute | solution.py:55
  19.9 21.7 %collective-permute-start.1 = (bf16[448,256]{1,0:T(8,128)(2,1)S(1)}, bf16[448,256]{1,0:T(8,128)(2,1)S(1)}, u32[]{:S(2)}, u32[]{:S(2)}) collective-permute-start(bf16[448,256]{1,0:T(8,128)(2,1)S(1)} %get-tuple-element.24), channel_id=1, source_target_pairs={{4,0},{8,4},{12,8},{16,12},{20,16},{24,20},{28,24},{5,1},{9,5},{13... | collective-permute-start | bytes 688136 | tf_op jit(solution)/shard_map/ppermute | solution.py:55
  21.8 1.2 %copy-start.1 = (f32[32,4,8,256]{3,2,1,0:T(8,128)S(1)}, f32[32,4,8,256]{3,2,1,0:T(8,128)}, u32[]{:S(2)}) copy-start(f32[32,4,8,256]{3,2,1,0:T(8,128)} %param.12) | copy-start | bytes 3145732
  33.4 1.0 copy-start.2
  34.4 1.0 copy-start.4
  35.4 1.0 copy-start.6
  36.3 0.9 copy-start.8
  37.3 0.9 copy-start.10
  38.2 0.8 copy-start.12
  39.0 0.7 copy-start.14
  39.7 0.7 copy-start.16
  40.3 0.6 copy-start.18
  40.9 0.6 copy-start.20
  41.6 1.2 %copy-start.3 = (f32[32,32,256]{2,1,0:T(8,128)S(1)}, f32[32,32,256]{2,1,0:T(8,128)}, u32[]{:S(2)}) copy-start(f32[32,32,256]{2,1,0:T(8,128)} %copy-done.2) | copy-start | bytes 3145732
  42.8 1.2 %copy-start.5 = (f32[32,32,256]{2,1,0:T(8,128)S(1)}, f32[32,32,256]{2,1,0:T(8,128)}, u32[]{:S(2)}) copy-start(f32[32,32,256]{2,1,0:T(8,128)} %copy-done.4) | copy-start | bytes 3145732
  44.0 1.2 %copy-start.7 = (f32[32,32,256]{2,1,0:T(8,128)S(1)}, f32[32,32,256]{2,1,0:T(8,128)}, u32[]{:S(2)}) copy-start(f32[32,32,256]{2,1,0:T(8,128)} %copy-done.6) | copy-start | bytes 3145732
  45.2 1.2 %copy-start.9 = (f32[28,32,256]{2,1,0:T(8,128)S(1)}, f32[28,32,256]{2,1,0:T(8,128)}, u32[]{:S(2)}) copy-start(f32[28,32,256]{2,1,0:T(8,128)} %copy-done.8) | copy-start | bytes 2752516
  46.4 1.1 %copy-start.11 = (f32[24,32,256]{2,1,0:T(8,128)S(1)}, f32[24,32,256]{2,1,0:T(8,128)}, u32[]{:S(2)}) copy-start(f32[24,32,256]{2,1,0:T(8,128)} %copy-done.10) | copy-start | bytes 2359300
  47.6 1.0 %copy-start.13 = (f32[16,32,256]{2,1,0:T(8,128)S(1)}, f32[16,32,256]{2,1,0:T(8,128)}, u32[]{:S(2)}) copy-start(f32[16,32,256]{2,1,0:T(8,128)} %copy-done.12) | copy-start | bytes 1572868
  48.6 0.9 copy-start.15
  49.5 0.9 copy-start.17
  50.4 0.7 copy-start.19
  51.2 0.7 copy-start.21
  81.5 6.7 %copy-start.22 = (f32[32,256]{1,0:T(8,128)}, f32[32,256]{1,0:T(8,128)S(1)}, u32[]{:S(2)}) copy-start(f32[32,256]{1,0:T(8,128)S(1)} %reduce_sum.19.own_ref) | copy-start | bytes 98308
Sparse Core Ops, SparseCore 0:
  15.1 25.2 all-gather.3

commit v4 on v2

--- a/solution.py
+++ b/solution.py
@@ -89,14 +89,17 @@
     return squared * reciprocal(squared + VISCOSITY_RATIO * rest * rest)
 
 
-def pack_kernel(dims, root, perm_ref, fields_ref, up_ref, down_ref, anomaly_ref, up_rows, down_rows):
+def pack_kernel(
+    dims, root, perm_ref, p0_ref, sat_ref, source_ref, storage_ref, up_ref, down_ref, anomaly_ref,
+    up_rows, down_rows,
+):
     local_count, layers, width = dims
     up_rows[...] = jnp.zeros_like(up_rows)
     down_rows[...] = jnp.zeros_like(down_rows)
-    for f in range(4):
+    for f, fields_ref in enumerate((p0_ref, sat_ref, source_ref, storage_ref)):
         for layer in range(layers):
             at = f * GROUP + layer * RIM
-            first = (f * layers + layer) * width
+            first = layer * width
             down_rows[at : at + RIM, :] = fields_ref[first : first + RIM, :]
             up_rows[at : at + RIM, :] = fields_ref[first + width - RIM : first + width, :]
     halves = anomaly_ref.shape[1] // LANES
@@ -119,6 +122,7 @@
                 up_ref[at : at + local_count, :] = low_values
 
 
+WORK = ("half", "face_x", "face_y", "face_z", "inverse", "first", "last")
 FIELD_NAMES = ("p0", "sat", "storage", "base", "ahead", "behind", "frac", "frac_ahead")
 
 
@@ -128,16 +132,18 @@
     near = [-2, -1, width, width + 1]
 
     def place(where, kind, rows, count=layers):
+        where[kind] = {}
         for r in rows:
             for layer in range(count):
-                where[kind, r, layer] = len(where)
+                where[kind][r, layer] = len(where[kind])
 
     place(kept, "half", (0, width - 1))
-    place(kept, "face_x", range(width - 1))
-    place(kept, "face_y", range(width))
-    place(kept, "face_z", range(width), layers - 1)
-    place(kept, "inverse", range(width))
-    place(kept, "first", range(width))
+    place(kept, "face_x", [0, 1, 2, width - 4, width - 3, width - 2])
+    outer = [0, 1, 2, width - 3, width - 2, width - 1]
+    place(kept, "face_y", outer)
+    place(kept, "face_z", outer, layers - 1)
+    place(kept, "inverse", [0, 1, width - 2, width - 1])
+    place(kept, "first", outer)
     place(kept, "last", range(2, width - 2))
     place(kept, "sat", range(3, width - 3))
     place(added, "half", rim)
@@ -147,6 +153,10 @@
     place(added, "inverse", near + [0, width - 1])
     place(added, "first", near + [0, width - 1])
     place(added, "last", [-1, 0, 1, width - 2, width - 1, width])
+    first = 0
+    for places in added.values():
+        for key in places:
+            places[key], first = first, first + 1
     return kept, added
 
 
@@ -255,116 +265,98 @@
     return [jnp.concatenate([part] * (GROUP // part.shape[0]), axis=0) for part in parts]
 
 
-def inner_kernel(
-    dims, count_ref, perm_ref, fields_ref, cell_ref, well_ref, bhp_ref,
-    state_ref, shared_ref, perf_ref, place_ref, chosen_ref, slot_ref, half_ref,
-):
-    local_count, layers, width = dims
-    rows = layers * width
-    depth = fields_ref.shape[1]
-    halves = depth // LANES
-    kept, _ = state_slots(layers, width)
-    fields = derived_fields(*(fields_ref[f * rows : (f + 1) * rows, :] for f in range(4)))
+def put_fields(dest_ref, field_refs):
+    fields = derived_fields(*(ref[...] for ref in field_refs))
+    rows, depth = field_refs[0].shape
     for n, name in enumerate(FIELD_NAMES):
         for row in range(rows):
-            shared_ref[n * rows + row] = jnp.broadcast_to(
-                fields[name][row : row + 1, :], (8, depth)
-            )
+            dest_ref[n * rows + row] = jnp.broadcast_to(fields[name][row : row + 1, :], (8, depth))
+
+
+def cell_places(cell_ref):
+    cells = jnp.broadcast_to(cell_ref[...], (GROUP, cell_ref.shape[1]))
+    return slot_parts(cells % LANES), slot_parts(cells // LANES)
+
+
+def inner_kernel(dims, perm_ref, *refs):
+    layers, width = dims
+    rows = layers * width
+    kept, _ = state_slots(layers, width)
+    field_refs, cell_ref, refs = refs[:4], refs[4], refs[5:]
+    states, refs = dict(zip(kept, refs)), refs[len(kept) :]
+    perf_ref, shared_ref, work_refs = refs[0], refs[1], dict(zip(WORK, refs[2:]))
     slots = cell_ref.shape[1]
-    wells = bhp_ref.shape[1]
-    cells = jnp.broadcast_to(cell_ref[...], (8, slots))
-    place_ref[:8, :] = cells % LANES
-    place_ref[8:, :] = cells // LANES
-    chosen = (
-        (lax.broadcasted_iota(jnp.int32, (wells, slots), 0) == well_ref[...])
-        .astype(jnp.float32)
-        .astype(jnp.bfloat16)
-    )
-    chosen_ref[...] = chosen
-    bhp = pieces(jnp.broadcast_to(bhp_ref[...], (GROUP, wells)))
-    bhp = jnp.dot(bhp, chosen, preferred_element_type=jnp.float32)
-    live = (lax.broadcasted_iota(jnp.int32, (8, slots), 1) < count_ref[0]).astype(jnp.float32)
-    slot_ref[:8, :] = (bhp[:8] + bhp[GROUP : GROUP + 8]) + bhp[2 * GROUP : 2 * GROUP + 8]
-    slot_ref[8:, :] = live
+    depth = field_refs[0].shape[1]
+    halves = depth // LANES
+
+    @pl.when(pl.program_id(0) == 0)
+    def _():
+        put_fields(shared_ref, field_refs)
 
     def field(name, r, layer):
         tile = shared_ref[FIELD_NAMES.index(name) * rows + layer * width + r]
         return jnp.concatenate([tile] * (GROUP // 8), axis=0)
 
-    @pl.loop(0, local_count // GROUP)
-    def _(group):
-        at_group = pl.ds(pl.multiple_of(group * GROUP, GROUP), GROUP)
-        lane_of, row_of = slot_parts(place_ref[:8, :]), slot_parts(place_ref[8:, :])
-        zeros = [jnp.zeros((GROUP, LANES), jnp.float32)] * (slots // LANES)
-        picked = [list(zeros) for _ in range(3)]
-
-        def load(kind, r, layer):
-            if kind == "half":
-                return half_ref[layer * width + r]
-            return state_ref[kept[kind, r, layer], at_group, :]
-
-        def store(kind, r, layer, values_in):
-            state_ref[kept[kind, r, layer], at_group, :] = values_in
-
-        for r in range(width):
-            for layer in range(layers):
-                values = jnp.concatenate(
-                    [
-                        perm_ref[
-                            pl.ds(
-                                group * GROUP * rows * halves + (layer * halves + h) * width + r,
-                                GROUP, stride=rows * halves,
-                            ),
-                            :,
-                        ]
-                        for h in range(halves)
-                    ],
-                    axis=1,
-                )
-                half = 0.5 * jnp.exp(-values)
-                half_ref[layer * width + r] = half
-                if r in (0, width - 1):
-                    store("half", r, layer, half)
-                pick(picked[0], half, layer * width + r, lane_of, row_of)
-        for r in range(width - 1):
-            for layer in range(layers):
-                store(
-                    "face_x", r, layer,
-                    reciprocal(load("half", r, layer) + load("half", r + 1, layer)),
-                )
-        for r in range(width):
-            for layer in range(layers):
-                sides = []
-                if r > 0:
-                    sides.append((load("face_x", r - 1, layer), r - 1))
-                if r < width - 1:
-                    sides.append((load("face_x", r, layer), r + 1))
-                top, bottom = cell_faces(load, store, field, r, layer, layers, sides)
-                if 0 < r < width - 1:
-                    bottom = reciprocal(bottom)
-                    top = top * bottom
-                store("first", r, layer, top)
-                store("inverse", r, layer, bottom)
-        for r in range(2, width - 2):
-            second_sweep(load, store, field, r, layers)
-            for layer in range(layers):
-                pick(picked[1], load("last", r, layer), layer * width + r, lane_of, row_of)
-        for r, layer, saturation in transported(load, field, 3, width - 4, layers):
-            store("sat", r, layer, saturation)
-            pick(picked[2], saturation, layer * width + r, lane_of, row_of)
-        for n in range(3):
-            perf_ref[n, at_group, :] = jnp.concatenate(picked[n], axis=1)
-
-
-def edge_kernel(
-    dims, rank_ref, low_ref, high_ref, state_ref, shared_ref, perf_ref, place_ref, chosen_ref,
-    slot_ref, press_ref, sat_ref, rates_ref, added_ref, gathered_ref,
-):
+    lane_of, row_of = cell_places(cell_ref)
+    zeros = [jnp.zeros((GROUP, LANES), jnp.float32)] * (slots // LANES)
+    picked = [list(zeros) for _ in range(3)]
+
+    def load(kind, r, layer):
+        return work_refs[kind][layer * width + r]
+
+    def store(kind, r, layer, values_in):
+        if kind in work_refs:
+            work_refs[kind][layer * width + r] = values_in
+        if (r, layer) in kept[kind]:
+            states[kind][kept[kind][r, layer]] = values_in
+
+    for r in range(width):
+        for layer in range(layers):
+            values = load_rows(perm_ref, GROUP, layer, r, layers, width, halves)
+            half = 0.5 * jnp.exp(-values)
+            store("half", r, layer, half)
+            pick(picked[0], half, layer * width + r, lane_of, row_of)
+    for r in range(width - 1):
+        for layer in range(layers):
+            store(
+                "face_x", r, layer,
+                reciprocal(load("half", r, layer) + load("half", r + 1, layer)),
+            )
+    for r in range(width):
+        for layer in range(layers):
+            sides = []
+            if r > 0:
+                sides.append((load("face_x", r - 1, layer), r - 1))
+            if r < width - 1:
+                sides.append((load("face_x", r, layer), r + 1))
+            top, bottom = cell_faces(load, store, field, r, layer, layers, sides)
+            if 0 < r < width - 1:
+                bottom = reciprocal(bottom)
+                top = top * bottom
+            store("first", r, layer, top)
+            store("inverse", r, layer, bottom)
+    for r in range(2, width - 2):
+        second_sweep(load, store, field, r, layers)
+        for layer in range(layers):
+            pick(picked[1], load("last", r, layer), layer * width + r, lane_of, row_of)
+    for r, layer, saturation in transported(load, field, 3, width - 4, layers):
+        store("sat", r, layer, saturation)
+        pick(picked[2], saturation, layer * width + r, lane_of, row_of)
+    for n in range(3):
+        perf_ref[n] = jnp.concatenate(picked[n], axis=1)
+
+
+def edge_kernel(dims, rank_ref, low_ref, high_ref, *refs):
     local_count, layers, width, tile_count = dims
     rows = layers * width
     depth = low_ref.shape[1]
     halves = depth // LANES
+    group = pl.program_id(0)
     kept, added = state_slots(layers, width)
+    field_refs, count_ref, cell_ref, well_ref, bhp_ref = refs[:4], refs[4], refs[5], refs[6], refs[7]
+    refs = refs[8:]
+    states, refs = dict(zip(kept, refs)), refs[len(kept) :]
+    perf_ref, press_ref, sat_ref, rates_ref, added_ref, gathered_ref, shared_ref = refs
     rim_rows = RIM * layers * local_count
     has_low = (rank_ref[0] > 0).astype(jnp.float32)
     has_high = (rank_ref[0] < tile_count - 1).astype(jnp.float32)
@@ -377,7 +369,11 @@
         )
         for ref in (low_ref, high_ref)
     ]
-    slots = place_ref.shape[1]
+    slots, wells = cell_ref.shape[1], bhp_ref.shape[1]
+
+    @pl.when(group == 0)
+    def _():
+        put_fields(shared_ref, field_refs)
 
     def field(name, r, layer):
         if 0 <= r < width:
@@ -387,91 +383,93 @@
         at = layer * RIM + at
         return part[name][at : at + 1, :]
 
-    @pl.loop(0, local_count // GROUP)
-    def _(group):
-        at_group = pl.ds(pl.multiple_of(group * GROUP, GROUP), GROUP)
-        lane_of, row_of = slot_parts(place_ref[:8, :]), slot_parts(place_ref[8:, :])
-        parts = slots // LANES
-        picked = [
-            [perf_ref[n, at_group, p * LANES : (p + 1) * LANES] for p in range(parts)]
-            for n in range(3)
+    lane_of, row_of = cell_places(cell_ref)
+    parts = slots // LANES
+    picked = [
+        [perf_ref[n, :, p * LANES : (p + 1) * LANES] for p in range(parts)]
+        for n in range(3)
+    ]
+
+    def load(kind, r, layer):
+        if (r, layer) in added.get(kind, {}):
+            return added_ref[added[kind][r, layer]]
+        return states[kind][kept[kind][r, layer]]
+
+    def store(kind, r, layer, values_in):
+        added_ref[added[kind][r, layer]] = values_in
+
+    for r in list(range(-RIM, 0)) + list(range(width, width + RIM)):
+        ref, i = (low_ref, r + RIM) if r < 0 else (high_ref, r - width)
+        for layer in range(layers):
+            at = (i * layers + layer) * local_count + group * GROUP
+            values = ref[pl.ds(pl.multiple_of(at, GROUP), GROUP), :].astype(jnp.float32)
+            store("half", r, layer, 0.5 * jnp.exp(-values))
+    for r in (-3, -2, -1, width - 1, width, width + 1):
+        for layer in range(layers):
+            face = reciprocal(load("half", r, layer) + load("half", r + 1, layer))
+            if r == -1:
+                face = face * has_low
+            if r == width - 1:
+                face = face * has_high
+            store("face_x", r, layer, face)
+    for r in (-2, -1, width, width + 1):
+        for layer in range(layers):
+            sides = [
+                (load("face_x", r - 1, layer), r - 1), (load("face_x", r, layer), r + 1)
+            ]
+            top, bottom = cell_faces(load, store, field, r, layer, layers, sides)
+            bottom = reciprocal(bottom)
+            store("first", r, layer, top * bottom)
+            store("inverse", r, layer, bottom)
+    for r, face_row, towards in ((0, -1, -1), (width - 1, width - 1, width)):
+        for layer in range(layers):
+            face = load("face_x", face_row, layer)
+            top = states["first"][kept["first"][r, layer]]
+            bottom = states["inverse"][kept["inverse"][r, layer]]
+            bottom = reciprocal(bottom + face)
+            store("first", r, layer, (top + face * field("p0", towards, layer)) * bottom)
+            store("inverse", r, layer, bottom)
+    for r in (-1, 0, 1, width - 2, width - 1, width):
+        second_sweep(load, store, field, r, layers)
+
+    def put(ref, r, layer, values_in):
+        store_rows(ref, values_in, GROUP, layer, r, layers, width, halves)
+
+    for r in range(width):
+        for layer in range(layers):
+            here = load("last", r, layer)
+            put(press_ref, r, layer, here)
+            if (r, layer) in added["last"]:
+                pick(picked[1], here, layer * width + r, lane_of, row_of)
+    for first_row, last_row in ((0, 2), (width - 3, width - 1)):
+        for r, layer, saturation in transported(load, field, first_row, last_row, layers):
+            put(sat_ref, r, layer, saturation)
+            pick(picked[2], saturation, layer * width + r, lane_of, row_of)
+    for r in range(3, width - 3):
+        for layer in range(layers):
+            put(sat_ref, r, layer, load("sat", r, layer))
+    for n in range(3):
+        gathered_ref[n, pl.ds(pl.multiple_of(group * GROUP, GROUP), GROUP), :] = jnp.concatenate(picked[n], axis=1)
+
+    @pl.when(group == local_count // GROUP - 1)
+    def _():
+        chosen = (
+            (lax.broadcasted_iota(jnp.int32, (wells, slots), 0) == well_ref[...])
+            .astype(jnp.float32)
+            .astype(jnp.bfloat16)
+        )
+        bhp = pieces(jnp.broadcast_to(bhp_ref[...], (GROUP, wells)))
+        bhp = jnp.dot(bhp, chosen, preferred_element_type=jnp.float32)
+        perf_bhp = (bhp[:1] + bhp[GROUP : GROUP + 1]) + bhp[2 * GROUP : 2 * GROUP + 1]
+        live = (lax.broadcasted_iota(jnp.int32, (1, slots), 1) < count_ref[0]).astype(jnp.float32)
+        mobility = water_frac(gathered_ref[2]) * reciprocal(2.0 * gathered_ref[0])
+        terms = mobility * (gathered_ref[1] - perf_bhp) * live
+        sums = lax.dot_general(
+            pieces(terms), chosen, (((1,), (1,)), ((), ())), preferred_element_type=jnp.float32
+        )
+        rates_ref[...] = (sums[:local_count] + sums[local_count : 2 * local_count]) + sums[
+            2 * local_count :
         ]
-
-        def load(kind, r, layer):
-            if (kind, r, layer) in added:
-                return added_ref[added[kind, r, layer]]
-            return state_ref[kept[kind, r, layer], at_group, :]
-
-        def store(kind, r, layer, values_in):
-            added_ref[added[kind, r, layer]] = values_in
-
-        for r in list(range(-RIM, 0)) + list(range(width, width + RIM)):
-            ref, i = (low_ref, r + RIM) if r < 0 else (high_ref, r - width)
-            for layer in range(layers):
-                at = (i * layers + layer) * local_count + group * GROUP
-                values = ref[pl.ds(pl.multiple_of(at, GROUP), GROUP), :].astype(jnp.float32)
-                store("half", r, layer, 0.5 * jnp.exp(-values))
-        for r in (-3, -2, -1, width - 1, width, width + 1):
-            for layer in range(layers):
-                face = reciprocal(load("half", r, layer) + load("half", r + 1, layer))
-                if r == -1:
-                    face = face * has_low
-                if r == width - 1:
-                    face = face * has_high
-                store("face_x", r, layer, face)
-        for r in (-2, -1, width, width + 1):
-            for layer in range(layers):
-                sides = [
-                    (load("face_x", r - 1, layer), r - 1), (load("face_x", r, layer), r + 1)
-                ]
-                top, bottom = cell_faces(load, store, field, r, layer, layers, sides)
-                bottom = reciprocal(bottom)
-                store("first", r, layer, top * bottom)
-                store("inverse", r, layer, bottom)
-        for r, face_row, towards in ((0, -1, -1), (width - 1, width - 1, width)):
-            for layer in range(layers):
-                face = load("face_x", face_row, layer)
-                top = state_ref[kept["first", r, layer], at_group, :]
-                bottom = state_ref[kept["inverse", r, layer], at_group, :]
-                bottom = reciprocal(bottom + face)
-                store("first", r, layer, (top + face * field("p0", towards, layer)) * bottom)
-                store("inverse", r, layer, bottom)
-        for r in (-1, 0, 1, width - 2, width - 1, width):
-            second_sweep(load, store, field, r, layers)
-
-        def put(ref, r, layer, values_in):
-            for h in range(halves):
-                at = pl.ds(
-                    group * GROUP * rows * halves + (layer * halves + h) * width + r,
-                    GROUP, stride=rows * halves,
-                )
-                ref[at, :] = values_in[:, h * LANES : (h + 1) * LANES]
-
-        for r in range(width):
-            for layer in range(layers):
-                here = load("last", r, layer)
-                put(press_ref, r, layer, here)
-                if ("last", r, layer) in added:
-                    pick(picked[1], here, layer * width + r, lane_of, row_of)
-        for first_row, last_row in ((0, 2), (width - 3, width - 1)):
-            for r, layer, saturation in transported(load, field, first_row, last_row, layers):
-                put(sat_ref, r, layer, saturation)
-                pick(picked[2], saturation, layer * width + r, lane_of, row_of)
-        for r in range(3, width - 3):
-            for layer in range(layers):
-                put(sat_ref, r, layer, load("sat", r, layer))
-        for n in range(3):
-            gathered_ref[n, at_group, :] = jnp.concatenate(picked[n], axis=1)
-
-    mobility = water_frac(gathered_ref[2]) * reciprocal(2.0 * gathered_ref[0])
-    terms = mobility * (gathered_ref[1] - slot_ref[:1, :]) * slot_ref[8:9, :]
-    sums = lax.dot_general(
-        pieces(terms), chosen_ref[...], (((1,), (1,)), ((), ())),
-        preferred_element_type=jnp.float32,
-    )
-    rates_ref[...] = (sums[:local_count] + sums[local_count : 2 * local_count]) + sums[
-        2 * local_count :
-    ]
 
 
 def invert_panel(columns):
@@ -586,7 +584,10 @@
     rows = layers * strip_width
     slots = perf_cell.shape[0]
     flat_perm = fold(log_perm)
-    fields = jnp.stack([start_pressure, start_sat, source, storage]).reshape(-1, strip_depth)
+    fields = [
+        array.reshape(rows, strip_depth) for array in (start_pressure, start_sat, source, storage)
+    ]
+    in_hbm = pl.BlockSpec(memory_space=pltpu.HBM)
     rim_shape = (RIM * layers * local_count + 4 * GROUP, strip_depth)
     field_scratch = pltpu.VMEM((4 * GROUP, strip_depth), jnp.float32)
     params = pltpu.CompilerParams(vmem_limit_bytes=60 * 2**20)
@@ -604,66 +605,78 @@
         cost_estimate=pl.CostEstimate(
             flops=4 * flat_perm.size, bytes_accessed=8 * flat_perm.size, transcendentals=0
         ),
-    )(flat_perm, fields)
+    )(flat_perm, *fields)
     low_rows, high_rows = send_both(up_rows, down_rows, "tile")
     anomaly_all = lax.all_gather(anomaly, "member", axis=0, tiled=True)
 
     kept, added = state_slots(layers, strip_width)
     smem, vmem = pl.BlockSpec(memory_space=pltpu.SMEM), pl.BlockSpec(memory_space=pltpu.VMEM)
-    anywhere = pl.BlockSpec(memory_space=pl.ANY)
-    inner_params = pltpu.CompilerParams(vmem_limit_bytes=28 * 2**20)
 
     def f32(*shape):
         return jax.ShapeDtypeStruct(shape, jnp.float32)
 
-    handed = pl.pallas_call(
-        functools.partial(inner_kernel, (local_count, layers, strip_width)),
-        in_specs=[smem] + [vmem] * 5,
-        out_specs=(vmem,) * 6,
-        out_shape=(
-            f32(len(kept), local_count, strip_depth),
-            f32(len(FIELD_NAMES) * rows, 8, strip_depth),
-            f32(3, local_count, slots),
-            jax.ShapeDtypeStruct((16, slots), jnp.int32),
-            jax.ShapeDtypeStruct((well_count, slots), jnp.bfloat16),
-            f32(16, slots),
-        ),
-        scratch_shapes=[pltpu.VMEM((rows, GROUP, strip_depth), jnp.float32)],
-        compiler_params=inner_params,
-        cost_estimate=pl.CostEstimate(
-            flops=10**10, bytes_accessed=24 * flat_perm.size, transcendentals=0
-        ),
-    )(perf_count, flat_perm, fields, perf_cell[None], perf_well[None], well_press[None])
+    def whole(array):
+        return pl.BlockSpec(array.shape, lambda g: (0,) * array.ndim)
+
+    block = pl.BlockSpec((GROUP * rows * (strip_depth // LANES), LANES), lambda g: (g, 0))
+    state_specs = [
+        pl.BlockSpec((count, GROUP, strip_depth), lambda g: (0, g, 0))
+        for count in [*map(len, kept.values()), 3]
+    ]
+    shared_scratch = pltpu.VMEM((len(FIELD_NAMES) * rows, 8, strip_depth), jnp.float32)
+    cells, wells, press = perf_cell[None], perf_well[None], well_press[None]
+    cost = pl.CostEstimate(flops=10**10, bytes_accessed=24 * flat_perm.size, transcendentals=0)
+    state = pl.pallas_call(
+        functools.partial(inner_kernel, (layers, strip_width)),
+        grid=(local_count // GROUP,),
+        in_specs=[block] + [whole(array) for array in fields] + [whole(cells)],
+        out_specs=state_specs,
+        out_shape=[
+            f32(count, local_count, strip_depth) for count in map(len, kept.values())
+        ]
+        + [f32(3, local_count, slots)],
+        scratch_shapes=[shared_scratch]
+        + [pltpu.VMEM((rows, GROUP, strip_depth), jnp.float32)] * len(WORK),
+        compiler_params=params,
+        cost_estimate=cost,
+    )(flat_perm, *fields, cells)
     flat_press, flat_sat, partial_rates = pl.pallas_call(
         functools.partial(edge_kernel, (local_count, layers, strip_width, tile_count)),
-        in_specs=[smem] + [vmem] * 8,
-        out_specs=(vmem,) * 3,
-        out_shape=(
+        grid=(local_count // GROUP,),
+        in_specs=[smem, whole(low_rows), whole(high_rows)]
+        + [whole(array) for array in fields]
+        + [smem, whole(cells), whole(wells), whole(press)]
+        + state_specs,
+        out_specs=[
+            block, block, pl.BlockSpec((local_count, well_count), lambda g: (0, 0))
+        ],
+        out_shape=[
             f32(*flat_perm.shape), f32(*flat_perm.shape), f32(local_count, well_count)
-        ),
+        ],
         scratch_shapes=[
-            pltpu.VMEM((len(added), GROUP, strip_depth), jnp.float32),
+            pltpu.VMEM((sum(map(len, added.values())), GROUP, strip_depth), jnp.float32),
             pltpu.VMEM((3, local_count, slots), jnp.float32),
+            shared_scratch,
         ],
-        compiler_params=inner_params,
-        cost_estimate=pl.CostEstimate(
-            flops=10**10, bytes_accessed=24 * flat_perm.size, transcendentals=0
-        ),
-    )(tile_rank[None], low_rows, high_rows, *handed)
+        compiler_params=params,
+        cost_estimate=cost,
+    )(
+        tile_rank[None], low_rows, high_rows, *fields, perf_count, cells, wells, press, *state
+    )
     own_rates = sum_over(partial_rates, "tile")
     well_rates = lax.dynamic_slice_in_dim(own_rates, tile_rank * well_share, well_share, 1)
     rates_all = lax.all_gather(own_rates, "member", axis=0, tiled=True)
     new_flat = pl.pallas_call(
         functools.partial(update_kernel, (local_count, layers, strip_width)),
         out_shape=jax.ShapeDtypeStruct(flat_perm.shape, jnp.float32),
-        in_specs=[vmem] * 5 + [anywhere] * 2,
+        in_specs=[vmem] * 5 + [in_hbm] * 2,
         out_specs=vmem,
         scratch_shapes=[
             pltpu.VMEM(anomaly_all.shape, jnp.bfloat16),
             pltpu.VMEM(flat_perm.shape, jnp.float32),
             pltpu.SemaphoreType.DMA((2,)),
         ],
-        compiler_params=params,
+        compiler_params=pltpu.CompilerParams(vmem_limit_bytes=60 * 2**20),
         cost_estimate=pl.CostEstimate(
             flops=12 * members**3, bytes_accessed=16 * flat_perm.size, transcendentals=0
         ),

time: 88.8 us -> 83.4 us (0.939)
  local copies, waits for them, and re-layouts: 10.1 us -> 1.44 us
  Pallas kernels: 33.4 us -> 38 us
  other arithmetic: 1.49 us -> 0.02 us
    unnamed x16 -> x6, local copies, waits for them, and re-layouts: 9.4 us -> 0.76 us
    pallas_call x1, Pallas kernels: 10.4 us -> 12.9 us  [per_device(): pl.pallas_call(functools.partial(inner_kernel, (layers, strip_width)), gr...]
    pallas_call x1, Pallas kernels: 12.2 us -> 14.2 us  [per_device(): pl.pallas_call(functools.partial(edge_kernel, (local_count, layers, strip...]
    another operation x1 -> x0, other arithmetic: 1.47 us -> none  [per_device(): jnp.stack([start_pressure, start_sat, source, storage])]
  transfers between devices with their start and end apart: 3 -> 3, of which waited for: 0 -> 0; matrix products, arithmetic and copies ran while one was open for 1% -> 1% of each run, Pallas kernels for 26% -> 33%
where the time goes in v4:
time: 83.4 us; the launch traced here: 83.2 us
  Pallas kernels  38 us (46%)
  blocking collectives  22.7 us (27%)
  between operations  14.8 us (18%)
  starting transfers between devices  6.19 us (7%)
  local copies, waits for them, and re-layouts  1.44 us (2%)
    all_gather x3, blocking collectives, sum_over(): array = jnp.sum(lax.all_gather(array, axis, axis_index_groups=groups), 0)  16.7 us
    pallas_call x1, Pallas kernels, per_device(): pl.pallas_call(functools.partial(edge_kernel, (local_count, layers, strip...  14.2 us
    pallas_call x1, Pallas kernels, per_device(): pl.pallas_call(functools.partial(inner_kernel, (layers, strip_width)), gr...  12.9 us
    pallas_call x1, Pallas kernels, per_device(): pl.pallas_call(functools.partial(update_kernel, (local_count, layers, str...  8.06 us
    all_gather x1, blocking collectives, per_device(): rates_all = lax.all_gather(own_rates, 'member', axis=0, tiled=True)  6.06 us
    ppermute x1, starting transfers between devices, send_both(): lax.ppermute(up_rows, axis, forward)  4.86 us
    pallas_call x1, Pallas kernels, per_device(): pl.pallas_call(functools.partial(pack_kernel, (local_count, layers, strip...  2.84 us
  transfers between devices with their start and end apart: 3, of which 0 were waited for; matrix products, arithmetic and copies ran while one was open for 1% of the time, Pallas kernels for 33%

profile of v4, /device:TPU:0, one launch (start us, length us, event | category | flops | bytes accessed | tf_op | source)
XLA Modules:
  0.0 83.2 jit_solution(7735152479649149356)
XLA Ops:
  7.2 0.0 all-gather.5.cloned.1.call-start
  7.2 2.8 %shard_map.147 = (bf16[448,256]{1,0:T(8,128)(2,1)}, bf16[448,256]{1,0:T(8,128)(2,1)}, bf16[1024,256]{1,0:T(8,128)(2,1)}) custom-call(f32[2048,128]{1,0:T(8,128)} %bitcast.33, f32[32,256]{1,0:T(8,128)} %bitcast.40, f32[32,256]{1,0:T(8,128)} %bitcast.43, f32[32,256]{1,0:T(8,128)} %bitcast.46, f32[32,256]{1,0:T(8,128)} %bitcast.49), custom_call_target="tpu_custom_call" | custom-call | flops 1048576 | bytes 2097152 | tf_op jit(solution)/shard_map/pallas_call | solution.py:594
  10.0 0.0 all-gather.5.cloned.1.call-update
  10.1 4.9 %collective-permute-start = (bf16[448,256]{1,0:T(8,128)(2,1)}, bf16[448,256]{1,0:T(8,128)(2,1)S(1)}, u32[]{:S(2)}, u32[]{:S(2)}) collective-permute-start(bf16[448,256]{1,0:T(8,128)(2,1)} %get-tuple-element.19), channel_id=1, source_target_pairs={{0,4},{4,8},{8,12},{12,16},{16,20},{20,24},{24,28},{1,5},{5,9},{9,... | collective-permute-start | bytes 688136 | tf_op jit(solution)/shard_map/ppermute | solution.py:55
  14.9 1.3 %collective-permute-start.1 = (bf16[448,256]{1,0:T(8,128)(2,1)}, bf16[448,256]{1,0:T(8,128)(2,1)S(1)}, u32[]{:S(2)}, u32[]{:S(2)}) collective-permute-start(bf16[448,256]{1,0:T(8,128)(2,1)} %get-tuple-element.20), channel_id=1, source_target_pairs={{4,0},{8,4},{12,8},{16,12},{20,16},{24,20},{28,24},{5,1},{9,5},{13... | collective-permute-start | bytes 688136 | tf_op jit(solution)/shard_map/ppermute | solution.py:55
  16.2 12.9 %shard_map.148 = (f32[8,32,256]{2,1,0:T(8,128)}, f32[24,32,256]{2,1,0:T(8,128)}, f32[24,32,256]{2,1,0:T(8,128)}, f32[18,32,256]{2,1,0:T(8,128)}, f32[16,32,256]{...) custom-call(f32[2048,128]{1,0:T(8,128)} %bitcast.34, ...), custom_call_target="tpu_custom_call" | custom-call | flops 10000000000 | bytes 6291456 | tf_op jit(solution)/shard_map/pallas_call | solution.py:629
  29.8 0.0 collective-permute-done.low_ref
  29.8 0.0 copy-start.1
  29.8 0.0 collective-permute-done.1.high_ref
  29.8 0.0 copy-start.2
  29.8 0.7 copy-done.1
  30.5 0.1 copy-done.2
  30.6 14.2 %shard_map.149 = (f32[2048,128]{1,0:T(8,128)}, f32[2048,128]{1,0:T(8,128)}, f32[32,256]{1,0:T(8,128)}) custom-call(s32[1]{0:T(128)} %bitcast.rank_ref, bf16[448,256]{1,0:T(8,128)(2,1)} %copy-done.1, bf16[448,256]{1,0:T(8,128)(2,1)} %copy-done.2, f32[32,256]{1,0:T(8,128)} %bitcast.42, f32[32,256]{1,0:T(8,128)} %bitcast.45, f32[32,256]{1,0:T(8,128)} %bitcast.48, ...), custom_call_target="tpu_custom_call" | custom-call | flops 10000000000 | bytes 6291456 | tf_op jit(solution)/shard_map/pallas_call | solution.py:643
  44.8 7.5 %all-gather = f32[64,256]{1,0:T(8,128)S(1)} all-gather(f32[32,256]{1,0:T(8,128)} %get-tuple-element.30), channel_id=2, replica_groups={{0,16},{4,20},{8,24},{12,28},{1,17},{5,21},{9,25},{13,29},{2,18},{6,22}..., dimensions={0}, use_global_device_ids=true | all-gather | bytes 98304 | tf_op jit(solution)/shard_map/all_gather | solution.py:69
  52.3 4.6 %all-gather.1 = f32[64,256]{1,0:T(8,128)S(1)} all-gather(f32[32,256]{1,0:T(8,128)S(1)} %reduce_sum.27), channel_id=3, replica_groups={{0,8},{4,12},{16,24},{20,28},{1,9},{5,13},{17,25},{21,29},{2,10},{6,14}..., dimensions={0}, use_global_device_ids=true | all-gather | bytes 98304 | tf_op jit(solution)/shard_map/all_gather | solution.py:69
  56.9 4.6 %all-gather.2 = f32[64,256]{1,0:T(8,128)S(1)} all-gather(f32[32,256]{1,0:T(8,128)S(1)} %reduce_sum.28), channel_id=4, replica_groups={{0,4},{8,12},{16,20},{24,28},{1,5},{9,13},{17,21},{25,29},{2,6},{10,14}..., dimensions={0}, use_global_device_ids=true | all-gather | bytes 98304 | tf_op jit(solution)/shard_map/all_gather | solution.py:69
  61.5 0.0 copy-start
  61.5 6.1 %all_gather.30.rates_ref = f32[128,256]{1,0:T(8,128)} all-gather(f32[32,256]{1,0:T(8,128)S(1)} %reduce_sum.29.own_ref), channel_id=1, replica_groups=mesh['tile'=8,'member'=4] {'member'}, dimensions={0}, use_global_device_ids=true | all-gather | bytes 163840 | tf_op jit(solution)/shard_map/all_gather | solution.py:668
  67.6 0.7 constant_dynamic-slice_fusion
  68.2 0.0 all-gather.5.cloned.1.call-done.anomaly_ref
  68.2 0.0 copy-done
  68.2 8.1 %shard_map.150 = f32[2048,128]{1,0:T(8,128)} custom-call(f32[128,256]{1,0:T(8,128)} %all_gather.30.rates_ref, f32[32,256]{1,0:T(8,128)} %copy-done, f32[32,256]{1,0:T(8,128)} %noise_ref.1, f32[1,256]{1,0:T(1,128)} %bitcast.52, f32[1,256]{1,0:T(1,128)} %bitcast.53, bf16[4096,256]{1,0:T(8,128)(2,1)} %all-gather.5.cloned.1.call-done.anomaly_ref, ...), custom_call_target="tpu_custom_call" | custom-call | flops 25165824 | bytes 4194304 | tf_op jit(solution)/shard_map/pallas_call | solution.py:669
  (3 shorter events, 0.0 us)
Async XLA Ops:
  7.2 61.1 %all-gather.5.cloned.1.call-start = ((), (), s32[]{:S(2)}) async-start(), calls=%async_computation | async-start | bytes 2621440 | tf_op jit(solution)/shard_map/all_gather | solution.py:610
  10.1 19.7 %collective-permute-start = (bf16[448,256]{1,0:T(8,128)(2,1)}, bf16[448,256]{1,0:T(8,128)(2,1)S(1)}, u32[]{:S(2)}, u32[]{:S(2)}) collective-permute-start(bf16[448,256]{1,0:T(8,128)(2,1)} %get-tuple-element.19), channel_id=1, source_target_pairs={{0,4},{4,8},{8,12},{12,16},{16,20},{20,24},{24,28},{1,5},{5,9},{9,... | collective-permute-start | bytes 688136 | tf_op jit(solution)/shard_map/ppermute | solution.py:55
  14.9 14.9 %collective-permute-start.1 = (bf16[448,256]{1,0:T(8,128)(2,1)}, bf16[448,256]{1,0:T(8,128)(2,1)S(1)}, u32[]{:S(2)}, u32[]{:S(2)}) collective-permute-start(bf16[448,256]{1,0:T(8,128)(2,1)} %get-tuple-element.20), channel_id=1, source_target_pairs={{4,0},{8,4},{12,8},{16,12},{20,16},{24,20},{28,24},{5,1},{9,5},{13... | collective-permute-start | bytes 688136 | tf_op jit(solution)/shard_map/ppermute | solution.py:55
  29.8 0.7 copy-start.1
  29.8 0.8 copy-start.2
  61.5 6.7 %copy-start = (f32[32,256]{1,0:T(8,128)}, f32[32,256]{1,0:T(8,128)S(1)}, u32[]{:S(2)}) copy-start(f32[32,256]{1,0:T(8,128)S(1)} %reduce_sum.29.own_ref) | copy-start | bytes 98308
Sparse Core Ops, SparseCore 0:
  10.2 25.3 all-gather.4

commit v5 on v4

--- a/solution.py
+++ b/solution.py
@@ -32,20 +32,36 @@
     return array.transpose(0, 1, 3, 2, 4).reshape(shape)
 
 
-def load_rows(ref, count, layer, x, layers, width, halves):
-    return jnp.concatenate(
-        [
-            ref[pl.ds((layer * halves + h) * width + x, count, stride=layers * width * halves), :]
-            for h in range(halves)
-        ],
-        axis=1,
-    )
-
-
-def store_rows(ref, values, count, layer, x, layers, width, halves):
-    for h in range(halves):
-        at = pl.ds((layer * halves + h) * width + x, count, stride=layers * width * halves)
-        ref[at, :] = values[:, h * LANES : (h + 1) * LANES]
+def turn(tiles):
+    row = lax.broadcasted_iota(jnp.int32, tiles[0].shape, 0)
+    for step in (4, 2, 1):
+        stays = (row & step) == 0
+        turned = list(tiles)
+        for i in range(8):
+            if i & step == 0:
+                first, second = tiles[i], tiles[i + step]
+                turned[i] = jnp.where(stays, first, pltpu.roll(second, step, 0))
+                turned[i + step] = jnp.where(stays, pltpu.roll(first, 8 - step, 0), second)
+        tiles = turned
+    return tiles
+
+
+def tile_rows(member, layer, half, layers, halves):
+    return pl.ds(((member * layers + layer) * halves + half) * 8, 8)
+
+
+def members_down(ref, layer, half, first, count, layers, halves):
+    octets = [
+        turn([ref[tile_rows(m + i, layer, half, layers, halves), :] for i in range(8)])
+        for m in range(first, first + count, 8)
+    ]
+    return [jnp.concatenate([octet[x] for octet in octets], axis=0) for x in range(8)]
+
+
+def members_apart(rows_of_x, layer, half, layers, halves):
+    for m in range(0, rows_of_x[0].shape[0], 8):
+        for i, tile in enumerate(turn([rows[m : m + 8] for rows in rows_of_x])):
+            yield tile_rows(m + i, layer, half, layers, halves), tile
 
 
 def send_both(up_rows, down_rows, axis):
@@ -107,19 +123,20 @@
     up_ref[block:, :] = up_rows[...].astype(jnp.bfloat16)
     down_ref[block:, :] = down_rows[...].astype(jnp.bfloat16)
     for layer in range(layers):
-        for x in range(width):
-            row = layer * width + x
-            values = load_rows(perm_ref, local_count, layer, x, layers, width, halves)
-            anomaly_ref[row * local_count : (row + 1) * local_count, :] = (values / root).astype(
-                jnp.bfloat16
-            )
-            low_values = values.astype(jnp.bfloat16)
-            if x < RIM:
-                at = (x * layers + layer) * local_count
-                down_ref[at : at + local_count, :] = low_values
-            if x >= width - RIM:
-                at = ((x - width + RIM) * layers + layer) * local_count
-                up_ref[at : at + local_count, :] = low_values
+        for half in range(halves):
+            lanes = slice(half * LANES, (half + 1) * LANES)
+            for m in range(0, local_count, GROUP):
+                values_of_x = members_down(perm_ref, layer, half, m, GROUP, layers, halves)
+                for x, values in enumerate(values_of_x):
+                    at = (layer * width + x) * local_count + m
+                    anomaly_ref[at : at + GROUP, lanes] = (values / root).astype(jnp.bfloat16)
+                    low_values = values.astype(jnp.bfloat16)
+                    if x < RIM:
+                        at = (x * layers + layer) * local_count + m
+                        down_ref[at : at + GROUP, lanes] = low_values
+                    if x >= width - RIM:
+                        at = ((x - width + RIM) * layers + layer) * local_count + m
+                        up_ref[at : at + GROUP, lanes] = low_values
 
 
 WORK = ("half", "face_x", "face_y", "face_z", "inverse", "first", "last")
@@ -310,9 +327,12 @@
         if (r, layer) in kept[kind]:
             states[kind][kept[kind][r, layer]] = values_in
 
-    for r in range(width):
-        for layer in range(layers):
-            values = load_rows(perm_ref, GROUP, layer, r, layers, width, halves)
+    for layer in range(layers):
+        lane_tiles = [
+            members_down(perm_ref, layer, h, 0, GROUP, layers, halves) for h in range(halves)
+        ]
+        for r in range(width):
+            values = jnp.concatenate([tiles[r] for tiles in lane_tiles], axis=1)
             half = 0.5 * jnp.exp(-values)
             store("half", r, layer, half)
             pick(picked[0], half, layer * width + r, lane_of, row_of)
@@ -356,7 +376,8 @@
     field_refs, count_ref, cell_ref, well_ref, bhp_ref = refs[:4], refs[4], refs[5], refs[6], refs[7]
     refs = refs[8:]
     states, refs = dict(zip(kept, refs)), refs[len(kept) :]
-    perf_ref, press_ref, sat_ref, rates_ref, added_ref, gathered_ref, shared_ref = refs
+    perf_ref, press_ref, sat_ref, rates_ref = refs[:4]
+    added_ref, gathered_ref, shared_ref, moved_ref = refs[4:]
     rim_rows = RIM * layers * local_count
     has_low = (rank_ref[0] > 0).astype(jnp.float32)
     has_high = (rank_ref[0] < tile_count - 1).astype(jnp.float32)
@@ -432,22 +453,28 @@
     for r in (-1, 0, 1, width - 2, width - 1, width):
         second_sweep(load, store, field, r, layers)
 
-    def put(ref, r, layer, values_in):
-        store_rows(ref, values_in, GROUP, layer, r, layers, width, halves)
-
-    for r in range(width):
-        for layer in range(layers):
-            here = load("last", r, layer)
-            put(press_ref, r, layer, here)
-            if (r, layer) in added["last"]:
-                pick(picked[1], here, layer * width + r, lane_of, row_of)
+    def put(ref, rows_of, layer):
+        for h in range(halves):
+            rows_of_x = [rows_of(r)[:, h * LANES : (h + 1) * LANES] for r in range(width)]
+            for where_tile, tile in members_apart(rows_of_x, layer, h, layers, halves):
+                ref[where_tile, :] = tile
+
+    for r in (0, 1, width - 2, width - 1):
+        for layer in range(layers):
+            pick(picked[1], load("last", r, layer), layer * width + r, lane_of, row_of)
     for first_row, last_row in ((0, 2), (width - 3, width - 1)):
         for r, layer, saturation in transported(load, field, first_row, last_row, layers):
-            put(sat_ref, r, layer, saturation)
+            moved_ref[layer * width + r] = saturation
             pick(picked[2], saturation, layer * width + r, lane_of, row_of)
-    for r in range(3, width - 3):
-        for layer in range(layers):
-            put(sat_ref, r, layer, load("sat", r, layer))
+
+    def saturation_of(r, layer):
+        if (r, layer) in kept["sat"]:
+            return load("sat", r, layer)
+        return moved_ref[layer * width + r]
+
+    for layer in range(layers):
+        put(press_ref, lambda r: load("last", r, layer), layer)
+        put(sat_ref, lambda r: saturation_of(r, layer), layer)
     for n in range(3):
         gathered_ref[n, pl.ds(pl.multiple_of(group * GROUP, GROUP), GROUP), :] = jnp.concatenate(picked[n], axis=1)
 
@@ -546,19 +573,22 @@
     weights = solve_blocks(gram_matrix, cross_matrix).T.astype(jnp.bfloat16)
     for copy in copies:
         copy.wait()
-    for row in range(rows):
-        layer, x = row // width, row % width
-        at = row * local_count
-        every = jnp.concatenate(
-            [
-                anomaly_buf[k * rows * local_count + at : k * rows * local_count + at + local_count, :]
-                for k in range(members // local_count)
-            ],
-            axis=0,
-        )
-        update = jnp.dot(weights, every, preferred_element_type=jnp.float32)
-        place = (local_count, layer, x, layers, width, halves)
-        store_rows(out_ref, load_rows(perm_buf, *place) + update, *place)
+    for layer in range(layers):
+        updates = []
+        for x in range(width):
+            at = (layer * width + x) * local_count
+            every = jnp.concatenate(
+                [
+                    anomaly_buf[first + at : first + at + local_count, :]
+                    for first in range(0, members * rows, rows * local_count)
+                ],
+                axis=0,
+            )
+            updates.append(jnp.dot(weights, every, preferred_element_type=jnp.float32))
+        for h in range(halves):
+            rows_of_x = [update[:, h * LANES : (h + 1) * LANES] for update in updates]
+            for where_tile, tile in members_apart(rows_of_x, layer, h, layers, halves):
+                out_ref[where_tile, :] = perm_buf[where_tile, :] + tile
 
 
 def per_device(
@@ -657,6 +687,7 @@
             pltpu.VMEM((sum(map(len, added.values())), GROUP, strip_depth), jnp.float32),
             pltpu.VMEM((3, local_count, slots), jnp.float32),
             shared_scratch,
+            pltpu.VMEM((rows, GROUP, strip_depth), jnp.float32),
         ],
         compiler_params=params,
         cost_estimate=cost,

time: 83.4 us -> 81.4 us (0.976)
  Pallas kernels: 38 us -> 36 us
    pallas_call x1, Pallas kernels: 8.06 us -> 7.16 us  [per_device(): pl.pallas_call(functools.partial(update_kernel, (local_count, layers, str...]
  transfers between devices with their start and end apart: 3 -> 3, of which waited for: 0 -> 0; matrix products, arithmetic and copies ran while one was open for 1% -> 1% of each run, Pallas kernels for 33% -> 32%
where the time goes in v5:
time: 81.4 us; the launch traced here: 81.1 us
  Pallas kernels  36 us (44%)
  blocking collectives  22.7 us (28%)
  between operations  14.8 us (18%)
  starting transfers between devices  6.19 us (8%)
  local copies, waits for them, and re-layouts  1.44 us (2%)
    all_gather x3, blocking collectives, sum_over(): array = jnp.sum(lax.all_gather(array, axis, axis_index_groups=groups), 0)  16.7 us
    pallas_call x1, Pallas kernels, per_device(): pl.pallas_call(functools.partial(edge_kernel, (local_count, layers, strip...  13.5 us
    pallas_call x1, Pallas kernels, per_device(): pl.pallas_call(functools.partial(inner_kernel, (layers, strip_width)), gr...  12.7 us
    pallas_call x1, Pallas kernels, per_device(): pl.pallas_call(functools.partial(update_kernel, (local_count, layers, str...  7.16 us
    all_gather x1, blocking collectives, per_device(): rates_all = lax.all_gather(own_rates, 'member', axis=0, tiled=True)  6.06 us
    ppermute x1, starting transfers between devices, send_both(): lax.ppermute(up_rows, axis, forward)  4.86 us
    pallas_call x1, Pallas kernels, per_device(): pl.pallas_call(functools.partial(pack_kernel, (local_count, layers, strip...  2.54 us
  transfers between devices with their start and end apart: 3, of which 0 were waited for; matrix products, arithmetic and copies ran while one was open for 1% of the time, Pallas kernels for 32%

profile of v5, /device:TPU:0, one launch (start us, length us, event | category | flops | bytes accessed | tf_op | source)
XLA Modules:
  0.0 81.1 jit_solution(10915724109610566432)
XLA Ops:
  7.2 0.0 all-gather.5.cloned.1.call-start
  7.2 2.5 %shard_map.147 = (bf16[448,256]{1,0:T(8,128)(2,1)}, bf16[448,256]{1,0:T(8,128)(2,1)}, bf16[1024,256]{1,0:T(8,128)(2,1)}) custom-call(f32[2048,128]{1,0:T(8,128)} %bitcast.33, f32[32,256]{1,0:T(8,128)} %bitcast.40, f32[32,256]{1,0:T(8,128)} %bitcast.43, f32[32,256]{1,0:T(8,128)} %bitcast.46, f32[32,256]{1,0:T(8,128)} %bitcast.49), custom_call_target="tpu_custom_call" | custom-call | flops 1048576 | bytes 2097152 | tf_op jit(solution)/shard_map/pallas_call | solution.py:624
  9.7 0.0 all-gather.5.cloned.1.call-update
  9.8 4.9 %collective-permute-start = (bf16[448,256]{1,0:T(8,128)(2,1)}, bf16[448,256]{1,0:T(8,128)(2,1)S(1)}, u32[]{:S(2)}, u32[]{:S(2)}) collective-permute-start(bf16[448,256]{1,0:T(8,128)(2,1)} %get-tuple-element.19), channel_id=1, source_target_pairs={{0,4},{4,8},{8,12},{12,16},{16,20},{20,24},{24,28},{1,5},{5,9},{9,... | collective-permute-start | bytes 688136 | tf_op jit(solution)/shard_map/ppermute | solution.py:71
  14.6 1.3 %collective-permute-start.1 = (bf16[448,256]{1,0:T(8,128)(2,1)}, bf16[448,256]{1,0:T(8,128)(2,1)S(1)}, u32[]{:S(2)}, u32[]{:S(2)}) collective-permute-start(bf16[448,256]{1,0:T(8,128)(2,1)} %get-tuple-element.20), channel_id=1, source_target_pairs={{4,0},{8,4},{12,8},{16,12},{20,16},{24,20},{28,24},{5,1},{9,5},{13... | collective-permute-start | bytes 688136 | tf_op jit(solution)/shard_map/ppermute | solution.py:71
  15.9 12.7 %shard_map.148 = (f32[8,32,256]{2,1,0:T(8,128)}, f32[24,32,256]{2,1,0:T(8,128)}, f32[24,32,256]{2,1,0:T(8,128)}, f32[18,32,256]{2,1,0:T(8,128)}, f32[16,32,256]{...) custom-call(f32[2048,128]{1,0:T(8,128)} %bitcast.34, ...), custom_call_target="tpu_custom_call" | custom-call | flops 10000000000 | bytes 6291456 | tf_op jit(solution)/shard_map/pallas_call | solution.py:659
  29.3 0.0 collective-permute-done.low_ref
  29.3 0.0 copy-start.1
  29.3 0.0 collective-permute-done.1.high_ref
  29.3 0.0 copy-start.2
  29.3 0.7 copy-done.1
  30.0 0.1 copy-done.2
  30.1 13.5 %shard_map.149 = (f32[2048,128]{1,0:T(8,128)}, f32[2048,128]{1,0:T(8,128)}, f32[32,256]{1,0:T(8,128)}) custom-call(s32[1]{0:T(128)} %bitcast.rank_ref, bf16[448,256]{1,0:T(8,128)(2,1)} %copy-done.1, bf16[448,256]{1,0:T(8,128)(2,1)} %copy-done.2, f32[32,256]{1,0:T(8,128)} %bitcast.42, f32[32,256]{1,0:T(8,128)} %bitcast.45, f32[32,256]{1,0:T(8,128)} %bitcast.48, ...), custom_call_target="tpu_custom_call" | custom-call | flops 10000000000 | bytes 6291456 | tf_op jit(solution)/shard_map/pallas_call | solution.py:673
  43.6 7.5 %all-gather = f32[64,256]{1,0:T(8,128)S(1)} all-gather(f32[32,256]{1,0:T(8,128)} %get-tuple-element.30), channel_id=2, replica_groups={{0,16},{4,20},{8,24},{12,28},{1,17},{5,21},{9,25},{13,29},{2,18},{6,22}..., dimensions={0}, use_global_device_ids=true | all-gather | bytes 98304 | tf_op jit(solution)/shard_map/all_gather | solution.py:85
  51.1 4.6 %all-gather.1 = f32[64,256]{1,0:T(8,128)S(1)} all-gather(f32[32,256]{1,0:T(8,128)S(1)} %reduce_sum.27), channel_id=3, replica_groups={{0,8},{4,12},{16,24},{20,28},{1,9},{5,13},{17,25},{21,29},{2,10},{6,14}..., dimensions={0}, use_global_device_ids=true | all-gather | bytes 98304 | tf_op jit(solution)/shard_map/all_gather | solution.py:85
  55.7 4.6 %all-gather.2 = f32[64,256]{1,0:T(8,128)S(1)} all-gather(f32[32,256]{1,0:T(8,128)S(1)} %reduce_sum.28), channel_id=4, replica_groups={{0,4},{8,12},{16,20},{24,28},{1,5},{9,13},{17,21},{25,29},{2,6},{10,14}..., dimensions={0}, use_global_device_ids=true | all-gather | bytes 98304 | tf_op jit(solution)/shard_map/all_gather | solution.py:85
  60.3 0.0 copy-start
  60.3 6.1 %all_gather.30.rates_ref = f32[128,256]{1,0:T(8,128)} all-gather(f32[32,256]{1,0:T(8,128)S(1)} %reduce_sum.29.own_ref), channel_id=1, replica_groups=mesh['tile'=8,'member'=4] {'member'}, dimensions={0}, use_global_device_ids=true | all-gather | bytes 163840 | tf_op jit(solution)/shard_map/all_gather | solution.py:699
  66.4 0.7 constant_dynamic-slice_fusion
  67.1 0.0 all-gather.5.cloned.1.call-done.anomaly_ref
  67.1 0.0 copy-done
  67.1 7.2 %shard_map.150 = f32[2048,128]{1,0:T(8,128)} custom-call(f32[128,256]{1,0:T(8,128)} %all_gather.30.rates_ref, f32[32,256]{1,0:T(8,128)} %copy-done, f32[32,256]{1,0:T(8,128)} %noise_ref.1, f32[1,256]{1,0:T(1,128)} %bitcast.52, f32[1,256]{1,0:T(1,128)} %bitcast.53, bf16[4096,256]{1,0:T(8,128)(2,1)} %all-gather.5.cloned.1.call-done.anomaly_ref, ...), custom_call_target="tpu_custom_call" | custom-call | flops 25165824 | bytes 4194304 | tf_op jit(solution)/shard_map/pallas_call | solution.py:700
  (3 shorter events, 0.0 us)
Async XLA Ops:
  7.2 59.9 %all-gather.5.cloned.1.call-start = ((), (), s32[]{:S(2)}) async-start(), calls=%async_computation | async-start | bytes 2621440 | tf_op jit(solution)/shard_map/all_gather | solution.py:640
  9.8 19.5 %collective-permute-start = (bf16[448,256]{1,0:T(8,128)(2,1)}, bf16[448,256]{1,0:T(8,128)(2,1)S(1)}, u32[]{:S(2)}, u32[]{:S(2)}) collective-permute-start(bf16[448,256]{1,0:T(8,128)(2,1)} %get-tuple-element.19), channel_id=1, source_target_pairs={{0,4},{4,8},{8,12},{12,16},{16,20},{20,24},{24,28},{1,5},{5,9},{9,... | collective-permute-start | bytes 688136 | tf_op jit(solution)/shard_map/ppermute | solution.py:71
  14.6 14.7 %collective-permute-start.1 = (bf16[448,256]{1,0:T(8,128)(2,1)}, bf16[448,256]{1,0:T(8,128)(2,1)S(1)}, u32[]{:S(2)}, u32[]{:S(2)}) collective-permute-start(bf16[448,256]{1,0:T(8,128)(2,1)} %get-tuple-element.20), channel_id=1, source_target_pairs={{4,0},{8,4},{12,8},{16,12},{20,16},{24,20},{28,24},{5,1},{9,5},{13... | collective-permute-start | bytes 688136 | tf_op jit(solution)/shard_map/ppermute | solution.py:71
  29.3 0.7 copy-start.1
  29.3 0.8 copy-start.2
  60.3 6.7 %copy-start = (f32[32,256]{1,0:T(8,128)}, f32[32,256]{1,0:T(8,128)S(1)}, u32[]{:S(2)}) copy-start(f32[32,256]{1,0:T(8,128)S(1)} %reduce_sum.29.own_ref) | copy-start | bytes 98308
Sparse Core Ops, SparseCore 0:
  9.9 25.3 all-gather.4

commit v6 on v5

--- a/solution.py
+++ b/solution.py
@@ -268,18 +268,23 @@
             yield r, layer, field("sat", r, layer) + STEP_COEF * change
 
 
-def pick(picked, values_in, row, lane_of, row_of):
-    halves = values_in.shape[1] // LANES
-    for half in range(halves):
-        part = values_in[:, half * LANES : (half + 1) * LANES]
-        for p in range(len(picked)):
-            found = jnp.take_along_axis(part, lane_of[p], axis=1, mode="promise_in_bounds")
-            picked[p] = jnp.where(row_of[p] == row * halves + half, found, picked[p])
-
-
-def slot_parts(array):
-    parts = [array[:, p * LANES : (p + 1) * LANES] for p in range(array.shape[1] // LANES)]
-    return [jnp.concatenate([part] * (GROUP // part.shape[0]), axis=0) for part in parts]
+def put_places(dest_ref, cell_ref, cell_rows, depth):
+    at = lax.broadcasted_iota(jnp.int32, (depth, cell_ref.shape[1]), 0)
+    for i, row in enumerate(cell_rows):
+        found = at + row * depth == cell_ref[...]
+        dest_ref[i * depth : (i + 1) * depth, :] = found.astype(jnp.float32).astype(jnp.bfloat16)
+
+
+def find(found, values_of, place):
+    every = jnp.concatenate([pieces(values) for _, values in values_of], axis=0)
+    sums = jnp.dot(every, place, preferred_element_type=jnp.float32)
+    for i, (n, _) in enumerate(values_of):
+        part = sums[i * 3 * GROUP : (i + 1) * 3 * GROUP]
+        found[n] = part if found[n] is None else found[n] + part
+
+
+def joined(part):
+    return (part[:GROUP] + part[GROUP : 2 * GROUP]) + part[2 * GROUP :]
 
 
 def put_fields(dest_ref, field_refs):
@@ -290,33 +295,27 @@
             dest_ref[n * rows + row] = jnp.broadcast_to(fields[name][row : row + 1, :], (8, depth))
 
 
-def cell_places(cell_ref):
-    cells = jnp.broadcast_to(cell_ref[...], (GROUP, cell_ref.shape[1]))
-    return slot_parts(cells % LANES), slot_parts(cells // LANES)
-
-
 def inner_kernel(dims, perm_ref, *refs):
     layers, width = dims
     rows = layers * width
     kept, _ = state_slots(layers, width)
     field_refs, cell_ref, refs = refs[:4], refs[4], refs[5:]
     states, refs = dict(zip(kept, refs)), refs[len(kept) :]
-    perf_ref, shared_ref, work_refs = refs[0], refs[1], dict(zip(WORK, refs[2:]))
-    slots = cell_ref.shape[1]
+    perf_ref, shared_ref, place_ref = refs[:3]
+    work_refs = dict(zip(WORK, refs[3:]))
     depth = field_refs[0].shape[1]
     halves = depth // LANES
 
     @pl.when(pl.program_id(0) == 0)
     def _():
         put_fields(shared_ref, field_refs)
+        put_places(place_ref, cell_ref, range(rows), depth)
 
     def field(name, r, layer):
         tile = shared_ref[FIELD_NAMES.index(name) * rows + layer * width + r]
         return jnp.concatenate([tile] * (GROUP // 8), axis=0)
 
-    lane_of, row_of = cell_places(cell_ref)
-    zeros = [jnp.zeros((GROUP, LANES), jnp.float32)] * (slots // LANES)
-    picked = [list(zeros) for _ in range(3)]
+    found = [None] * 3
 
     def load(kind, r, layer):
         return work_refs[kind][layer * width + r]
@@ -335,7 +334,6 @@
             values = jnp.concatenate([tiles[r] for tiles in lane_tiles], axis=1)
             half = 0.5 * jnp.exp(-values)
             store("half", r, layer, half)
-            pick(picked[0], half, layer * width + r, lane_of, row_of)
     for r in range(width - 1):
         for layer in range(layers):
             store(
@@ -357,13 +355,19 @@
             store("inverse", r, layer, bottom)
     for r in range(2, width - 2):
         second_sweep(load, store, field, r, layers)
-        for layer in range(layers):
-            pick(picked[1], load("last", r, layer), layer * width + r, lane_of, row_of)
     for r, layer, saturation in transported(load, field, 3, width - 4, layers):
         store("sat", r, layer, saturation)
-        pick(picked[2], saturation, layer * width + r, lane_of, row_of)
+    for r in range(width):
+        for layer in range(layers):
+            values_of = [(0, load("half", r, layer))]
+            if (r, layer) in kept["last"]:
+                values_of.append((1, load("last", r, layer)))
+            if (r, layer) in kept["sat"]:
+                values_of.append((2, states["sat"][kept["sat"][r, layer]]))
+            first = (layer * width + r) * depth
+            find(found, values_of, place_ref[first : first + depth, :])
     for n in range(3):
-        perf_ref[n] = jnp.concatenate(picked[n], axis=1)
+        perf_ref[n] = joined(found[n])
 
 
 def edge_kernel(dims, rank_ref, low_ref, high_ref, *refs):
@@ -377,7 +381,7 @@
     refs = refs[8:]
     states, refs = dict(zip(kept, refs)), refs[len(kept) :]
     perf_ref, press_ref, sat_ref, rates_ref = refs[:4]
-    added_ref, gathered_ref, shared_ref, moved_ref = refs[4:]
+    added_ref, gathered_ref, shared_ref, moved_ref, place_ref = refs[4:]
     rim_rows = RIM * layers * local_count
     has_low = (rank_ref[0] > 0).astype(jnp.float32)
     has_high = (rank_ref[0] < tile_count - 1).astype(jnp.float32)
@@ -392,9 +396,13 @@
     ]
     slots, wells = cell_ref.shape[1], bhp_ref.shape[1]
 
+    moved = [layer * width + r for layer in range(layers) for r in range(width)]
+    moved = [row for row in moved if (row % width, row // width) not in kept["sat"]]
+
     @pl.when(group == 0)
     def _():
         put_fields(shared_ref, field_refs)
+        put_places(place_ref, cell_ref, moved, depth)
 
     def field(name, r, layer):
         if 0 <= r < width:
@@ -404,12 +412,7 @@
         at = layer * RIM + at
         return part[name][at : at + 1, :]
 
-    lane_of, row_of = cell_places(cell_ref)
-    parts = slots // LANES
-    picked = [
-        [perf_ref[n, :, p * LANES : (p + 1) * LANES] for p in range(parts)]
-        for n in range(3)
-    ]
+    found = [None] * 3
 
     def load(kind, r, layer):
         if (r, layer) in added.get(kind, {}):
@@ -459,13 +462,9 @@
             for where_tile, tile in members_apart(rows_of_x, layer, h, layers, halves):
                 ref[where_tile, :] = tile
 
-    for r in (0, 1, width - 2, width - 1):
-        for layer in range(layers):
-            pick(picked[1], load("last", r, layer), layer * width + r, lane_of, row_of)
     for first_row, last_row in ((0, 2), (width - 3, width - 1)):
         for r, layer, saturation in transported(load, field, first_row, last_row, layers):
             moved_ref[layer * width + r] = saturation
-            pick(picked[2], saturation, layer * width + r, lane_of, row_of)
 
     def saturation_of(r, layer):
         if (r, layer) in kept["sat"]:
@@ -475,8 +474,15 @@
     for layer in range(layers):
         put(press_ref, lambda r: load("last", r, layer), layer)
         put(sat_ref, lambda r: saturation_of(r, layer), layer)
+    for i, row in enumerate(moved):
+        r, layer = row % width, row // width
+        values_of = [(2, moved_ref[row])]
+        if (r, layer) in added["last"]:
+            values_of.append((1, load("last", r, layer)))
+        find(found, values_of, place_ref[i * depth : (i + 1) * depth, :])
     for n in range(3):
-        gathered_ref[n, pl.ds(pl.multiple_of(group * GROUP, GROUP), GROUP), :] = jnp.concatenate(picked[n], axis=1)
+        total = perf_ref[n] if found[n] is None else perf_ref[n] + joined(found[n])
+        gathered_ref[n, pl.ds(pl.multiple_of(group * GROUP, GROUP), GROUP), :] = total
 
     @pl.when(group == local_count // GROUP - 1)
     def _():
@@ -544,8 +550,8 @@
 
 
 def update_kernel(
-    dims, rates_ref, own_ref, noise_ref, observed_ref, var_ref, anomaly_ref, perm_ref, out_ref,
-    anomaly_buf, perm_buf, sems,
+    dims, rank_ref, rates_ref, own_ref, noise_ref, observed_ref, var_ref, anomaly_ref, perm_ref,
+    out_ref, held_ref, anomaly_buf, perm_buf, sems,
 ):
     local_count, layers, width = dims
     rows = layers * width
@@ -556,6 +562,10 @@
     ]
     for copy in copies:
         copy.start()
+    wells, share = own_ref.shape[1], held_ref.shape[1]
+    held_ref[...] = pltpu.roll(
+        own_ref[...], lax.rem(wells - rank_ref[0] * share, wells), 1
+    )[:, :share]
     rates = rates_ref[...]
     members = rates.shape[0]
     spread = jnp.sqrt(INFLATION * var_ref[...])
@@ -654,6 +664,7 @@
         for count in [*map(len, kept.values()), 3]
     ]
     shared_scratch = pltpu.VMEM((len(FIELD_NAMES) * rows, 8, strip_depth), jnp.float32)
+    place_scratch = pltpu.VMEM((rows * strip_depth, slots), jnp.bfloat16)
     cells, wells, press = perf_cell[None], perf_well[None], well_press[None]
     cost = pl.CostEstimate(flops=10**10, bytes_accessed=24 * flat_perm.size, transcendentals=0)
     state = pl.pallas_call(
@@ -665,7 +676,7 @@
             f32(count, local_count, strip_depth) for count in map(len, kept.values())
         ]
         + [f32(3, local_count, slots)],
-        scratch_shapes=[shared_scratch]
+        scratch_shapes=[shared_scratch, place_scratch]
         + [pltpu.VMEM((rows, GROUP, strip_depth), jnp.float32)] * len(WORK),
         compiler_params=params,
         cost_estimate=cost,
@@ -688,6 +699,7 @@
             pltpu.VMEM((3, local_count, slots), jnp.float32),
             shared_scratch,
             pltpu.VMEM((rows, GROUP, strip_depth), jnp.float32),
+            place_scratch,
         ],
         compiler_params=params,
         cost_estimate=cost,
@@ -695,13 +707,12 @@
         tile_rank[None], low_rows, high_rows, *fields, perf_count, cells, wells, press, *state
     )
     own_rates = sum_over(partial_rates, "tile")
-    well_rates = lax.dynamic_slice_in_dim(own_rates, tile_rank * well_share, well_share, 1)
     rates_all = lax.all_gather(own_rates, "member", axis=0, tiled=True)
-    new_flat = pl.pallas_call(
+    new_flat, well_rates = pl.pallas_call(
         functools.partial(update_kernel, (local_count, layers, strip_width)),
-        out_shape=jax.ShapeDtypeStruct(flat_perm.shape, jnp.float32),
-        in_specs=[vmem] * 5 + [in_hbm] * 2,
-        out_specs=vmem,
+        out_shape=(f32(*flat_perm.shape), f32(local_count, well_share)),
+        in_specs=[smem] + [vmem] * 5 + [in_hbm] * 2,
+        out_specs=(vmem, vmem),
         scratch_shapes=[
             pltpu.VMEM(anomaly_all.shape, jnp.bfloat16),
             pltpu.VMEM(flat_perm.shape, jnp.float32),
@@ -711,7 +722,7 @@
         cost_estimate=pl.CostEstimate(
             flops=12 * members**3, bytes_accessed=16 * flat_perm.size, transcendentals=0
         ),
-    )(rates_all, own_rates, obs_noise, observed[None], obs_var[None], anomaly_all, flat_perm)
+    )(tile_rank[None], rates_all, own_rates, obs_noise, observed[None], obs_var[None], anomaly_all, flat_perm)
     new_log_perm = unfold(new_flat, log_perm.shape)
     pressure = unfold(flat_press, log_perm.shape)
     saturation = unfold(flat_sat, log_perm.shape)

time: 81.4 us -> 69.5 us (0.85)
  Pallas kernels: 36 us -> 24.2 us
  waiting for transfers between devices: 0.02 us -> 1.24 us
    pallas_call x1, Pallas kernels: 13.5 us -> 7.59 us  [per_device(): pl.pallas_call(functools.partial(edge_kernel, (local_count, layers, strip...]
    pallas_call x1, Pallas kernels: 12.7 us -> 6.91 us  [per_device(): pl.pallas_call(functools.partial(inner_kernel, (layers, strip_width)), gr...]
    ppermute x1, waiting for transfers between devices: 0.01 us -> 1.21 us  [send_both(): lax.ppermute(up_rows, axis, forward)]
  transfers between devices with their start and end apart: 3 -> 3, of which waited for: 0 -> 1; matrix products, arithmetic and copies ran while one was open for 1% -> 0% of each run, Pallas kernels for 32% -> 21%
where the time goes in v6:
time: 69.5 us; the launch traced here: 69.3 us
  Pallas kernels  24.2 us (35%)
  blocking collectives  22.1 us (32%)
  between operations  14.7 us (21%)
  starting transfers between devices  6.19 us (9%)
  waiting for transfers between devices  1.24 us (2%)
  local copies, waits for them, and re-layouts  0.78 us (1%)
    all_gather x3, blocking collectives, sum_over(): array = jnp.sum(lax.all_gather(array, axis, axis_index_groups=groups), 0)  16.2 us
    pallas_call x1, Pallas kernels, per_device(): pl.pallas_call(functools.partial(edge_kernel, (local_count, layers, strip...  7.59 us
    pallas_call x1, Pallas kernels, per_device(): pl.pallas_call(functools.partial(update_kernel, (local_count, layers, str...  7.18 us
    pallas_call x1, Pallas kernels, per_device(): pl.pallas_call(functools.partial(inner_kernel, (layers, strip_width)), gr...  6.91 us
    all_gather x1, blocking collectives, per_device(): rates_all = lax.all_gather(own_rates, 'member', axis=0, tiled=True)  5.87 us
    ppermute x1, starting transfers between devices, send_both(): lax.ppermute(up_rows, axis, forward)  4.86 us
    pallas_call x1, Pallas kernels, per_device(): pl.pallas_call(functools.partial(pack_kernel, (local_count, layers, strip...  2.54 us
  transfers between devices with their start and end apart: 3, of which 1 were waited for; matrix products, arithmetic and copies ran while one was open for 0% of the time, Pallas kernels for 21%

profile of v6, /device:TPU:0, one launch (start us, length us, event | category | flops | bytes accessed | tf_op | source)
XLA Modules:
  0.0 69.3 jit_solution(1743099108847485877)
XLA Ops:
  7.2 0.0 all-gather.5.cloned.1.call-start
  7.2 2.5 %shard_map.147 = (bf16[448,256]{1,0:T(8,128)(2,1)}, bf16[448,256]{1,0:T(8,128)(2,1)}, bf16[1024,256]{1,0:T(8,128)(2,1)}) custom-call(f32[2048,128]{1,0:T(8,128)} %bitcast.33, f32[32,256]{1,0:T(8,128)} %bitcast.39, f32[32,256]{1,0:T(8,128)} %bitcast.42, f32[32,256]{1,0:T(8,128)} %bitcast.45, f32[32,256]{1,0:T(8,128)} %bitcast.48), custom_call_target="tpu_custom_call" | custom-call | flops 1048576 | bytes 2097152 | tf_op jit(solution)/shard_map/pallas_call | solution.py:634
  9.7 0.0 all-gather.5.cloned.1.call-update
  9.8 4.9 %collective-permute-start = (bf16[448,256]{1,0:T(8,128)(2,1)}, bf16[448,256]{1,0:T(8,128)(2,1)S(1)}, u32[]{:S(2)}, u32[]{:S(2)}) collective-permute-start(bf16[448,256]{1,0:T(8,128)(2,1)} %get-tuple-element.21), channel_id=1, source_target_pairs={{0,4},{4,8},{8,12},{12,16},{16,20},{20,24},{24,28},{1,5},{5,9},{9,... | collective-permute-start | bytes 688136 | tf_op jit(solution)/shard_map/ppermute | solution.py:71
  14.6 1.3 %collective-permute-start.1 = (bf16[448,256]{1,0:T(8,128)(2,1)}, bf16[448,256]{1,0:T(8,128)(2,1)S(1)}, u32[]{:S(2)}, u32[]{:S(2)}) collective-permute-start(bf16[448,256]{1,0:T(8,128)(2,1)} %get-tuple-element.22), channel_id=1, source_target_pairs={{4,0},{8,4},{12,8},{16,12},{20,16},{24,20},{28,24},{5,1},{9,5},{13... | collective-permute-start | bytes 688136 | tf_op jit(solution)/shard_map/ppermute | solution.py:71
  15.9 6.9 %shard_map.148 = (f32[8,32,256]{2,1,0:T(8,128)}, f32[24,32,256]{2,1,0:T(8,128)}, f32[24,32,256]{2,1,0:T(8,128)}, f32[18,32,256]{2,1,0:T(8,128)}, f32[16,32,256]{...) custom-call(f32[2048,128]{1,0:T(8,128)} %bitcast.34, ...), custom_call_target="tpu_custom_call" | custom-call | flops 10000000000 | bytes 6291456 | tf_op jit(solution)/shard_map/pallas_call | solution.py:670
  23.5 1.2 %collective-permute-done.low_ref = bf16[448,256]{1,0:T(8,128)(2,1)S(1)} collective-permute-done((bf16[448,256]{1,0:T(8,128)(2,1)}, bf16[448,256]{1,0:T(8,128)(2,1)S(1)}, u32[]{:S(2)}, u32[]{:S(2)}) %collective-permute-start) | collective-permute-done | bytes 229408 | tf_op jit(solution)/shard_map/ppermute | solution.py:71
  24.7 0.0 copy-start.1
  24.7 0.0 collective-permute-done.1.high_ref
  24.7 0.0 copy-start.2
  24.7 0.7 copy-done.1
  25.4 0.1 copy-done.2
  25.5 7.6 %shard_map.149 = (f32[2048,128]{1,0:T(8,128)}, f32[2048,128]{1,0:T(8,128)}, f32[32,256]{1,0:T(8,128)}) custom-call(s32[1]{0:T(128)} %bitcast.rank_ref, bf16[448,256]{1,0:T(8,128)(2,1)} %copy-done.1, bf16[448,256]{1,0:T(8,128)(2,1)} %copy-done.2, f32[32,256]{1,0:T(8,128)} %bitcast.41, f32[32,256]{1,0:T(8,128)} %bitcast.44, f32[32,256]{1,0:T(8,128)} %bitcast.47, ...), custom_call_target="tpu_custom_call" | custom-call | flops 10000000000 | bytes 6291456 | tf_op jit(solution)/shard_map/pallas_call | solution.py:684
  33.1 7.1 %all-gather = f32[64,256]{1,0:T(8,128)S(1)} all-gather(f32[32,256]{1,0:T(8,128)} %get-tuple-element.32), channel_id=2, replica_groups={{0,16},{4,20},{8,24},{12,28},{1,17},{5,21},{9,25},{13,29},{2,18},{6,22}..., dimensions={0}, use_global_device_ids=true | all-gather | bytes 98304 | tf_op jit(solution)/shard_map/all_gather | solution.py:85
  40.2 4.6 %all-gather.1 = f32[64,256]{1,0:T(8,128)S(1)} all-gather(f32[32,256]{1,0:T(8,128)S(1)} %reduce_sum.27), channel_id=3, replica_groups={{0,8},{4,12},{16,24},{20,28},{1,9},{5,13},{17,25},{21,29},{2,10},{6,14}..., dimensions={0}, use_global_device_ids=true | all-gather | bytes 98304 | tf_op jit(solution)/shard_map/all_gather | solution.py:85
  44.8 4.6 %all-gather.2 = f32[64,256]{1,0:T(8,128)S(1)} all-gather(f32[32,256]{1,0:T(8,128)S(1)} %reduce_sum.28), channel_id=4, replica_groups={{0,4},{8,12},{16,20},{24,28},{1,5},{9,13},{17,21},{25,29},{2,6},{10,14}..., dimensions={0}, use_global_device_ids=true | all-gather | bytes 98304 | tf_op jit(solution)/shard_map/all_gather | solution.py:85
  49.3 0.0 copy-start
  49.4 5.9 %all_gather.30.rates_ref = f32[128,256]{1,0:T(8,128)} all-gather(f32[32,256]{1,0:T(8,128)S(1)} %reduce_sum.29.own_ref), channel_id=1, replica_groups=mesh['tile'=8,'member'=4] {'member'}, dimensions={0}, use_global_device_ids=true | all-gather | bytes 163840 | tf_op jit(solution)/shard_map/all_gather | solution.py:710
  55.2 0.0 all-gather.5.cloned.1.call-done.anomaly_ref
  55.2 0.0 copy-done
  55.2 7.2 %shard_map.150 = (f32[2048,128]{1,0:T(8,128)}, f32[32,32]{1,0:T(8,128)}) custom-call(s32[1]{0:T(128)} %bitcast.rank_ref, f32[128,256]{1,0:T(8,128)} %all_gather.30.rates_ref, f32[32,256]{1,0:T(8,128)} %copy-done, f32[32,256]{1,0:T(8,128)} %noise_ref.1, f32[1,256]{1,0:T(1,128)} %bitcast.51, f32[1,256]{1,0:T(1,128)} %bitcast.52, ...), custom_call_target="tpu_custom_call" | custom-call | flops 25165824 | bytes 4194304 | tf_op jit(solution)/shard_map/pallas_call | solution.py:711
  (3 shorter events, 0.0 us)
Async XLA Ops:
  7.2 48.1 %all-gather.5.cloned.1.call-start = ((), (), s32[]{:S(2)}) async-start(), calls=%async_computation | async-start | bytes 2621440 | tf_op jit(solution)/shard_map/all_gather | solution.py:650
  9.8 14.9 %collective-permute-start = (bf16[448,256]{1,0:T(8,128)(2,1)}, bf16[448,256]{1,0:T(8,128)(2,1)S(1)}, u32[]{:S(2)}, u32[]{:S(2)}) collective-permute-start(bf16[448,256]{1,0:T(8,128)(2,1)} %get-tuple-element.21), channel_id=1, source_target_pairs={{0,4},{4,8},{8,12},{12,16},{16,20},{20,24},{24,28},{1,5},{5,9},{9,... | collective-permute-start | bytes 688136 | tf_op jit(solution)/shard_map/ppermute | solution.py:71
  14.6 10.1 %collective-permute-start.1 = (bf16[448,256]{1,0:T(8,128)(2,1)}, bf16[448,256]{1,0:T(8,128)(2,1)S(1)}, u32[]{:S(2)}, u32[]{:S(2)}) collective-permute-start(bf16[448,256]{1,0:T(8,128)(2,1)} %get-tuple-element.22), channel_id=1, source_target_pairs={{4,0},{8,4},{12,8},{16,12},{20,16},{24,20},{28,24},{5,1},{9,5},{13... | collective-permute-start | bytes 688136 | tf_op jit(solution)/shard_map/ppermute | solution.py:71
  24.7 0.7 copy-start.1
  24.7 0.8 %copy-start.2 = (bf16[448,256]{1,0:T(8,128)(2,1)}, bf16[448,256]{1,0:T(8,128)(2,1)S(1)}, u32[]{:S(2)}) copy-start(bf16[448,256]{1,0:T(8,128)(2,1)S(1)} %collective-permute-done.1.high_ref) | copy-start | bytes 688132
  49.3 5.9 %copy-start = (f32[32,256]{1,0:T(8,128)}, f32[32,256]{1,0:T(8,128)S(1)}, u32[]{:S(2)}) copy-start(f32[32,256]{1,0:T(8,128)S(1)} %reduce_sum.29.own_ref) | copy-start | bytes 98308
Sparse Core Ops, SparseCore 0:
  9.9 25.2 all-gather.4

commit v7 on v6

--- a/solution.py
+++ b/solution.py
@@ -17,6 +17,8 @@
 INFLATION = 4.0
 PANEL = 8
 GROUP = 16
+INNER_GRANT = 121 * 2**19
+UPDATE_GRANT = 598 * 2**20 // 10
 LANES = 128
 
 
@@ -106,37 +108,39 @@
 
 
 def pack_kernel(
-    dims, root, perm_ref, p0_ref, sat_ref, source_ref, storage_ref, up_ref, down_ref, anomaly_ref,
+    dims, scale, perm_ref, p0_ref, sat_ref, source_ref, storage_ref, up_ref, down_ref, anomaly_ref,
     up_rows, down_rows,
 ):
-    local_count, layers, width = dims
-    up_rows[...] = jnp.zeros_like(up_rows)
-    down_rows[...] = jnp.zeros_like(down_rows)
-    for f, fields_ref in enumerate((p0_ref, sat_ref, source_ref, storage_ref)):
-        for layer in range(layers):
-            at = f * GROUP + layer * RIM
-            first = layer * width
-            down_rows[at : at + RIM, :] = fields_ref[first : first + RIM, :]
-            up_rows[at : at + RIM, :] = fields_ref[first + width - RIM : first + width, :]
-    halves = anomaly_ref.shape[1] // LANES
-    block = RIM * layers * local_count
-    up_ref[block:, :] = up_rows[...].astype(jnp.bfloat16)
-    down_ref[block:, :] = down_rows[...].astype(jnp.bfloat16)
+    layers, width = dims
+    halves = anomaly_ref.shape[2] // LANES
+    block = RIM * layers
+
+    @pl.when(pl.program_id(0) == 0)
+    def _():
+        up_rows[...] = jnp.zeros_like(up_rows)
+        down_rows[...] = jnp.zeros_like(down_rows)
+        for f, fields_ref in enumerate((p0_ref, sat_ref, source_ref, storage_ref)):
+            for layer in range(layers):
+                at = layer * RIM
+                first = layer * width
+                down_rows[f, at : at + RIM, :] = fields_ref[first : first + RIM, :]
+                up_rows[f, at : at + RIM, :] = fields_ref[first + width - RIM : first + width, :]
+
+    for i in range(2):
+        f = 2 * i + pl.program_id(0)
+        up_ref[block + i] = up_rows[f].astype(jnp.bfloat16)
+        down_ref[block + i] = down_rows[f].astype(jnp.bfloat16)
     for layer in range(layers):
         for half in range(halves):
             lanes = slice(half * LANES, (half + 1) * LANES)
-            for m in range(0, local_count, GROUP):
-                values_of_x = members_down(perm_ref, layer, half, m, GROUP, layers, halves)
-                for x, values in enumerate(values_of_x):
-                    at = (layer * width + x) * local_count + m
-                    anomaly_ref[at : at + GROUP, lanes] = (values / root).astype(jnp.bfloat16)
-                    low_values = values.astype(jnp.bfloat16)
-                    if x < RIM:
-                        at = (x * layers + layer) * local_count + m
-                        down_ref[at : at + GROUP, lanes] = low_values
-                    if x >= width - RIM:
-                        at = ((x - width + RIM) * layers + layer) * local_count + m
-                        up_ref[at : at + GROUP, lanes] = low_values
+            values_of_x = members_down(perm_ref, layer, half, 0, GROUP, layers, halves)
+            for x, values in enumerate(values_of_x):
+                anomaly_ref[layer * width + x, :, lanes] = (values * scale).astype(jnp.bfloat16)
+                low_values = values.astype(jnp.bfloat16)
+                if x < RIM:
+                    down_ref[x * layers + layer, :, lanes] = low_values
+                if x >= width - RIM:
+                    up_ref[(x - width + RIM) * layers + layer, :, lanes] = low_values
 
 
 WORK = ("half", "face_x", "face_y", "face_z", "inverse", "first", "last")
@@ -295,7 +299,7 @@
             dest_ref[n * rows + row] = jnp.broadcast_to(fields[name][row : row + 1, :], (8, depth))
 
 
-def inner_kernel(dims, perm_ref, *refs):
+def inner_kernel(dims, rank_ref, count_ref, perm_ref, *refs):
     layers, width = dims
     rows = layers * width
     kept, _ = state_slots(layers, width)
@@ -509,7 +513,7 @@
     row = lax.broadcasted_iota(jnp.int32, columns[0].shape, 0)
     columns = list(columns)
     for k in range(PANEL):
-        inverse = 1.0 / columns[k][k : k + 1]
+        inverse = reciprocal(columns[k][k : k + 1])
         pivot = columns[k]
         for j in range(PANEL):
             if j != k:
@@ -628,24 +632,35 @@
         array.reshape(rows, strip_depth) for array in (start_pressure, start_sat, source, storage)
     ]
     in_hbm = pl.BlockSpec(memory_space=pltpu.HBM)
-    rim_shape = (RIM * layers * local_count + 4 * GROUP, strip_depth)
-    field_scratch = pltpu.VMEM((4 * GROUP, strip_depth), jnp.float32)
-    params = pltpu.CompilerParams(vmem_limit_bytes=60 * 2**20)
-    up_rows, down_rows, anomaly = pl.pallas_call(
-        functools.partial(
-            pack_kernel, (local_count, layers, strip_width), (members - 1) ** 0.5
-        ),
-        out_shape=(
-            jax.ShapeDtypeStruct(rim_shape, jnp.bfloat16),
-            jax.ShapeDtypeStruct(rim_shape, jnp.bfloat16),
-            jax.ShapeDtypeStruct((local_count * rows, strip_depth), jnp.bfloat16),
-        ),
-        scratch_shapes=[field_scratch, field_scratch],
-        compiler_params=params,
-        cost_estimate=pl.CostEstimate(
-            flops=4 * flat_perm.size, bytes_accessed=8 * flat_perm.size, transcendentals=0
-        ),
-    )(flat_perm, *fields)
+    rim_blocks = RIM * layers + 2
+    field_scratch = pltpu.VMEM((4, GROUP, strip_depth), jnp.float32)
+    params = pltpu.CompilerParams(vmem_limit_bytes=INNER_GRANT)
+
+    def whole(array):
+        return pl.BlockSpec(array.shape, lambda g: (0,) * array.ndim)
+
+    def stacked(count):
+        return pl.BlockSpec((count, GROUP, strip_depth), lambda g: (0, g, 0))
+
+    block = pl.BlockSpec((GROUP * rows * (strip_depth // LANES), LANES), lambda g: (g, 0))
+    up_rows, down_rows, anomaly = (
+        array.reshape(-1, strip_depth)
+        for array in pl.pallas_call(
+            functools.partial(pack_kernel, (layers, strip_width), (members - 1) ** -0.5),
+            grid=(local_count // GROUP,),
+            in_specs=[block] + [whole(array) for array in fields],
+            out_specs=[stacked(rim_blocks), stacked(rim_blocks), stacked(rows)],
+            out_shape=[
+                jax.ShapeDtypeStruct((count, local_count, strip_depth), jnp.bfloat16)
+                for count in (rim_blocks, rim_blocks, rows)
+            ],
+            scratch_shapes=[field_scratch, field_scratch],
+            compiler_params=params,
+            cost_estimate=pl.CostEstimate(
+                flops=4 * flat_perm.size, bytes_accessed=8 * flat_perm.size, transcendentals=0
+            ),
+        )(flat_perm, *fields)
+    )
     low_rows, high_rows = send_both(up_rows, down_rows, "tile")
     anomaly_all = lax.all_gather(anomaly, "member", axis=0, tiled=True)
 
@@ -655,14 +670,7 @@
     def f32(*shape):
         return jax.ShapeDtypeStruct(shape, jnp.float32)
 
-    def whole(array):
-        return pl.BlockSpec(array.shape, lambda g: (0,) * array.ndim)
-
-    block = pl.BlockSpec((GROUP * rows * (strip_depth // LANES), LANES), lambda g: (g, 0))
-    state_specs = [
-        pl.BlockSpec((count, GROUP, strip_depth), lambda g: (0, g, 0))
-        for count in [*map(len, kept.values()), 3]
-    ]
+    state_specs = [stacked(count) for count in [*map(len, kept.values()), 3]]
     shared_scratch = pltpu.VMEM((len(FIELD_NAMES) * rows, 8, strip_depth), jnp.float32)
     place_scratch = pltpu.VMEM((rows * strip_depth, slots), jnp.bfloat16)
     cells, wells, press = perf_cell[None], perf_well[None], well_press[None]
@@ -670,7 +678,7 @@
     state = pl.pallas_call(
         functools.partial(inner_kernel, (layers, strip_width)),
         grid=(local_count // GROUP,),
-        in_specs=[block] + [whole(array) for array in fields] + [whole(cells)],
+        in_specs=[smem, smem, block] + [whole(array) for array in fields] + [whole(cells)],
         out_specs=state_specs,
         out_shape=[
             f32(count, local_count, strip_depth) for count in map(len, kept.values())
@@ -680,7 +688,7 @@
         + [pltpu.VMEM((rows, GROUP, strip_depth), jnp.float32)] * len(WORK),
         compiler_params=params,
         cost_estimate=cost,
-    )(flat_perm, *fields, cells)
+    )(tile_rank[None], perf_count, flat_perm, *fields, cells)
     flat_press, flat_sat, partial_rates = pl.pallas_call(
         functools.partial(edge_kernel, (local_count, layers, strip_width, tile_count)),
         grid=(local_count // GROUP,),
@@ -718,7 +726,7 @@
             pltpu.VMEM(flat_perm.shape, jnp.float32),
             pltpu.SemaphoreType.DMA((2,)),
         ],
-        compiler_params=pltpu.CompilerParams(vmem_limit_bytes=60 * 2**20),
+        compiler_params=pltpu.CompilerParams(vmem_limit_bytes=UPDATE_GRANT),
         cost_estimate=pl.CostEstimate(
             flops=12 * members**3, bytes_accessed=16 * flat_perm.size, transcendentals=0
         ),

time: 69.5 us -> 69.8 us (level)
  no operation moved by 1% of the time
where the time goes in v7:
time: 69.8 us; the launch traced here: 69.5 us
  Pallas kernels  24.3 us (35%)
  blocking collectives  22.3 us (32%)
  between operations  14.7 us (21%)
  starting transfers between devices  6.19 us (9%)
  waiting for transfers between devices  1.23 us (2%)
  local copies, waits for them, and re-layouts  0.78 us (1%)
    all_gather x3, blocking collectives, sum_over(): array = jnp.sum(lax.all_gather(array, axis, axis_index_groups=groups), 0)  16.2 us
    pallas_call x1, Pallas kernels, per_device(): pl.pallas_call(functools.partial(edge_kernel, (local_count, layers, strip...  7.58 us
    pallas_call x1, Pallas kernels, per_device(): pl.pallas_call(functools.partial(update_kernel, (local_count, layers, str...  7.45 us
    pallas_call x1, Pallas kernels, per_device(): pl.pallas_call(functools.partial(inner_kernel, (layers, strip_width)), gr...  6.91 us
    all_gather x1, blocking collectives, per_device(): rates_all = lax.all_gather(own_rates, 'member', axis=0, tiled=True)  6.06 us
    ppermute x1, starting transfers between devices, send_both(): lax.ppermute(up_rows, axis, forward)  4.86 us
    pallas_call x1, Pallas kernels, per_device(): pl.pallas_call(functools.partial(pack_kernel, (layers, strip_width), (mem...  2.3 us
  transfers between devices with their start and end apart: 3, of which 1 were waited for; matrix products, arithmetic and copies ran while one was open for 0% of the time, Pallas kernels for 21%

profile of v7, /device:TPU:0, one launch (start us, length us, event | category | flops | bytes accessed | tf_op | source)
XLA Modules:
  0.0 69.5 jit_solution(1048113218627757088)
XLA Ops:
  7.2 0.0 all-gather.5.cloned.1.call-start
  7.2 2.3 %shard_map.147 = (bf16[14,32,256]{2,1,0:T(8,128)(2,1)}, bf16[14,32,256]{2,1,0:T(8,128)(2,1)}, bf16[32,32,256]{2,1,0:T(8,128)(2,1)}) custom-call(f32[2048,128]{1,0:T(8,128)} %bitcast.36, f32[32,256]{1,0:T(8,128)} %bitcast.43, f32[32,256]{1,0:T(8,128)} %bitcast.46, f32[32,256]{1,0:T(8,128)} %bitcast.49, f32[32,256]{1,0:T(8,128)} %bitcast.52), custom_call_target="tpu_custom_call" | custom-call | flops 1048576 | bytes 2097152 | tf_op jit(solution)/shard_map/pallas_call | solution.py:648
  9.5 0.0 all-gather.5.cloned.1.call-update
  9.5 4.9 %collective-permute-start = (bf16[448,256]{1,0:T(8,128)(2,1)}, bf16[448,256]{1,0:T(8,128)(2,1)S(1)}, u32[]{:S(2)}, u32[]{:S(2)}) collective-permute-start(bf16[448,256]{1,0:T(8,128)(2,1)} %bitcast.59), channel_id=1, source_target_pairs={{0,4},{4,8},{8,12},{12,16},{16,20},{20,24},{24,28},{1,5},{5,9},{9,... | collective-permute-start | bytes 688136 | tf_op jit(solution)/shard_map/ppermute | solution.py:73
  14.4 1.3 %collective-permute-start.1 = (bf16[448,256]{1,0:T(8,128)(2,1)}, bf16[448,256]{1,0:T(8,128)(2,1)S(1)}, u32[]{:S(2)}, u32[]{:S(2)}) collective-permute-start(bf16[448,256]{1,0:T(8,128)(2,1)} %bitcast.58), channel_id=1, source_target_pairs={{4,0},{8,4},{12,8},{16,12},{20,16},{24,20},{28,24},{5,1},{9,5},{13... | collective-permute-start | bytes 688136 | tf_op jit(solution)/shard_map/ppermute | solution.py:73
  16.4 6.9 %shard_map.148 = (f32[8,32,256]{2,1,0:T(8,128)}, f32[24,32,256]{2,1,0:T(8,128)}, f32[24,32,256]{2,1,0:T(8,128)}, f32[18,32,256]{2,1,0:T(8,128)}, f32[16,32,256]{...) custom-call(s32[1]{0:T(128)} %bitcast.rank_ref, ...), custom_call_target="tpu_custom_call" | custom-call | flops 10000000000 | bytes 6291456 | tf_op jit(solution)/shard_map/pallas_call | solution.py:678
  23.3 1.2 %collective-permute-done.low_ref = bf16[448,256]{1,0:T(8,128)(2,1)S(1)} collective-permute-done((bf16[448,256]{1,0:T(8,128)(2,1)}, bf16[448,256]{1,0:T(8,128)(2,1)S(1)}, u32[]{:S(2)}, u32[]{:S(2)}) %collective-permute-start) | collective-permute-done | bytes 229408 | tf_op jit(solution)/shard_map/ppermute | solution.py:73
  24.5 0.0 copy-start.1
  24.5 0.0 collective-permute-done.1.high_ref
  24.5 0.0 copy-start.2
  24.5 0.7 copy-done.1
  25.2 0.1 copy-done.2
  25.3 7.6 %shard_map.149 = (f32[2048,128]{1,0:T(8,128)}, f32[2048,128]{1,0:T(8,128)}, f32[32,256]{1,0:T(8,128)}) custom-call(s32[1]{0:T(128)} %bitcast.rank_ref, bf16[448,256]{1,0:T(8,128)(2,1)} %copy-done.1, bf16[448,256]{1,0:T(8,128)(2,1)} %copy-done.2, f32[32,256]{1,0:T(8,128)} %bitcast.45, f32[32,256]{1,0:T(8,128)} %bitcast.48, f32[32,256]{1,0:T(8,128)} %bitcast.51, ...), custom_call_target="tpu_custom_call" | custom-call | flops 10000000000 | bytes 6291456 | tf_op jit(solution)/shard_map/pallas_call | solution.py:692
  32.8 7.1 %all-gather = f32[64,256]{1,0:T(8,128)S(1)} all-gather(f32[32,256]{1,0:T(8,128)} %get-tuple-element.32), channel_id=2, replica_groups={{0,16},{4,20},{8,24},{12,28},{1,17},{5,21},{9,25},{13,29},{2,18},{6,22}..., dimensions={0}, use_global_device_ids=true | all-gather | bytes 98304 | tf_op jit(solution)/shard_map/all_gather | solution.py:87
  39.9 4.6 %all-gather.1 = f32[64,256]{1,0:T(8,128)S(1)} all-gather(f32[32,256]{1,0:T(8,128)S(1)} %reduce_sum.27), channel_id=3, replica_groups={{0,8},{4,12},{16,24},{20,28},{1,9},{5,13},{17,25},{21,29},{2,10},{6,14}..., dimensions={0}, use_global_device_ids=true | all-gather | bytes 98304 | tf_op jit(solution)/shard_map/all_gather | solution.py:87
  44.5 4.6 %all-gather.2 = f32[64,256]{1,0:T(8,128)S(1)} all-gather(f32[32,256]{1,0:T(8,128)S(1)} %reduce_sum.28), channel_id=4, replica_groups={{0,4},{8,12},{16,20},{24,28},{1,5},{9,13},{17,21},{25,29},{2,6},{10,14}..., dimensions={0}, use_global_device_ids=true | all-gather | bytes 98304 | tf_op jit(solution)/shard_map/all_gather | solution.py:87
  49.1 0.0 copy-start
  49.1 6.1 %all_gather.30.rates_ref = f32[128,256]{1,0:T(8,128)} all-gather(f32[32,256]{1,0:T(8,128)S(1)} %reduce_sum.29.own_ref), channel_id=1, replica_groups=mesh['tile'=8,'member'=4] {'member'}, dimensions={0}, use_global_device_ids=true | all-gather | bytes 163840 | tf_op jit(solution)/shard_map/all_gather | solution.py:718
  55.2 0.0 all-gather.5.cloned.1.call-done.anomaly_ref
  55.2 0.0 copy-done
  55.2 7.5 %shard_map.150 = (f32[2048,128]{1,0:T(8,128)}, f32[32,32]{1,0:T(8,128)}) custom-call(s32[1]{0:T(128)} %bitcast.rank_ref, f32[128,256]{1,0:T(8,128)} %all_gather.30.rates_ref, f32[32,256]{1,0:T(8,128)} %copy-done, f32[32,256]{1,0:T(8,128)} %noise_ref.1, f32[1,256]{1,0:T(1,128)} %bitcast.55, f32[1,256]{1,0:T(1,128)} %bitcast.56, ...), custom_call_target="tpu_custom_call" | custom-call | flops 25165824 | bytes 4194304 | tf_op jit(solution)/shard_map/pallas_call | solution.py:719
  (3 shorter events, 0.0 us)
Async XLA Ops:
  7.2 48.0 %all-gather.5.cloned.1.call-start = ((), (), s32[]{:S(2)}) async-start(), calls=%async_computation | async-start | bytes 2621440 | tf_op jit(solution)/shard_map/all_gather | solution.py:665
  9.5 14.9 %collective-permute-start = (bf16[448,256]{1,0:T(8,128)(2,1)}, bf16[448,256]{1,0:T(8,128)(2,1)S(1)}, u32[]{:S(2)}, u32[]{:S(2)}) collective-permute-start(bf16[448,256]{1,0:T(8,128)(2,1)} %bitcast.59), channel_id=1, source_target_pairs={{0,4},{4,8},{8,12},{12,16},{16,20},{20,24},{24,28},{1,5},{5,9},{9,... | collective-permute-start | bytes 688136 | tf_op jit(solution)/shard_map/ppermute | solution.py:73
  14.4 10.1 %collective-permute-start.1 = (bf16[448,256]{1,0:T(8,128)(2,1)}, bf16[448,256]{1,0:T(8,128)(2,1)S(1)}, u32[]{:S(2)}, u32[]{:S(2)}) collective-permute-start(bf16[448,256]{1,0:T(8,128)(2,1)} %bitcast.58), channel_id=1, source_target_pairs={{4,0},{8,4},{12,8},{16,12},{20,16},{24,20},{28,24},{5,1},{9,5},{13... | collective-permute-start | bytes 688136 | tf_op jit(solution)/shard_map/ppermute | solution.py:73
  24.5 0.7 copy-start.1
  24.5 0.8 %copy-start.2 = (bf16[448,256]{1,0:T(8,128)(2,1)}, bf16[448,256]{1,0:T(8,128)(2,1)S(1)}, u32[]{:S(2)}) copy-start(bf16[448,256]{1,0:T(8,128)(2,1)S(1)} %collective-permute-done.1.high_ref) | copy-start | bytes 688132
  49.1 6.1 %copy-start = (f32[32,256]{1,0:T(8,128)}, f32[32,256]{1,0:T(8,128)S(1)}, u32[]{:S(2)}) copy-start(f32[32,256]{1,0:T(8,128)S(1)} %reduce_sum.29.own_ref) | copy-start | bytes 98308
Sparse Core Ops, SparseCore 0:
  9.7 25.2 all-gather.4

commit v8 on v7

--- a/solution.py
+++ b/solution.py
@@ -17,8 +17,6 @@
 INFLATION = 4.0
 PANEL = 8
 GROUP = 16
-INNER_GRANT = 121 * 2**19
-UPDATE_GRANT = 598 * 2**20 // 10
 LANES = 128
 
 
@@ -71,21 +69,6 @@
     forward = [(i, i + 1) for i in range(count - 1)]
     backward = [(target, source) for source, target in forward]
     return lax.ppermute(up_rows, axis, forward), lax.ppermute(down_rows, axis, backward)
-
-
-def sum_over(array, axis):
-    count = lax.axis_size(axis)
-    stride = count
-    while stride > 1:
-        radix = 2
-        stride //= radix
-        groups = [
-            [base + low + i * stride for i in range(radix)]
-            for base in range(0, count, stride * radix)
-            for low in range(stride)
-        ]
-        array = jnp.sum(lax.all_gather(array, axis, axis_index_groups=groups), 0)
-    return array
 
 
 def reciprocal(values_in):
@@ -384,8 +367,8 @@
     field_refs, count_ref, cell_ref, well_ref, bhp_ref = refs[:4], refs[4], refs[5], refs[6], refs[7]
     refs = refs[8:]
     states, refs = dict(zip(kept, refs)), refs[len(kept) :]
-    perf_ref, press_ref, sat_ref, rates_ref = refs[:4]
-    added_ref, gathered_ref, shared_ref, moved_ref, place_ref = refs[4:]
+    perf_ref, press_ref, moved_ref, rates_ref = refs[:4]
+    added_ref, gathered_ref, shared_ref, place_ref = refs[4:]
     rim_rows = RIM * layers * local_count
     has_low = (rank_ref[0] > 0).astype(jnp.float32)
     has_high = (rank_ref[0] < tile_count - 1).astype(jnp.float32)
@@ -460,24 +443,16 @@
     for r in (-1, 0, 1, width - 2, width - 1, width):
         second_sweep(load, store, field, r, layers)
 
-    def put(ref, rows_of, layer):
-        for h in range(halves):
-            rows_of_x = [rows_of(r)[:, h * LANES : (h + 1) * LANES] for r in range(width)]
-            for where_tile, tile in members_apart(rows_of_x, layer, h, layers, halves):
-                ref[where_tile, :] = tile
-
     for first_row, last_row in ((0, 2), (width - 3, width - 1)):
         for r, layer, saturation in transported(load, field, first_row, last_row, layers):
             moved_ref[layer * width + r] = saturation
 
-    def saturation_of(r, layer):
-        if (r, layer) in kept["sat"]:
-            return load("sat", r, layer)
-        return moved_ref[layer * width + r]
-
     for layer in range(layers):
-        put(press_ref, lambda r: load("last", r, layer), layer)
-        put(sat_ref, lambda r: saturation_of(r, layer), layer)
+        for r in range(width):
+            press_ref[layer * width + r] = load("last", r, layer)
+            if (r, layer) in kept["sat"]:
+                moved_ref[layer * width + r] = load("sat", r, layer)
+
     for i, row in enumerate(moved):
         r, layer = row % width, row // width
         values_of = [(2, moved_ref[row])]
@@ -504,16 +479,30 @@
         sums = lax.dot_general(
             pieces(terms), chosen, (((1,), (1,)), ((), ())), preferred_element_type=jnp.float32
         )
-        rates_ref[...] = (sums[:local_count] + sums[local_count : 2 * local_count]) + sums[
+        partial_rates = (sums[:local_count] + sums[local_count : 2 * local_count]) + sums[
             2 * local_count :
         ]
+        rates_ref[...] = jnp.broadcast_to(partial_rates[None], rates_ref.shape)
+
+
+def output_kernel(layers, width, *refs):
+    halves = refs[0].shape[2] // LANES
+    for source_ref, out_ref in zip(refs[:2], refs[2:]):
+        for layer in range(layers):
+            for h in range(halves):
+                rows_of_x = [
+                    source_ref[layer * width + x, :, h * LANES : (h + 1) * LANES]
+                    for x in range(width)
+                ]
+                for where_tile, tile in members_apart(rows_of_x, layer, h, layers, halves):
+                    out_ref[where_tile, :] = tile
 
 
 def invert_panel(columns):
     row = lax.broadcasted_iota(jnp.int32, columns[0].shape, 0)
     columns = list(columns)
     for k in range(PANEL):
-        inverse = reciprocal(columns[k][k : k + 1])
+        inverse = 1.0 / columns[k][k : k + 1]
         pivot = columns[k]
         for j in range(PANEL):
             if j != k:
@@ -634,7 +623,7 @@
     in_hbm = pl.BlockSpec(memory_space=pltpu.HBM)
     rim_blocks = RIM * layers + 2
     field_scratch = pltpu.VMEM((4, GROUP, strip_depth), jnp.float32)
-    params = pltpu.CompilerParams(vmem_limit_bytes=INNER_GRANT)
+    params = pltpu.CompilerParams(vmem_limit_bytes=60 * 2**20)
 
     def whole(array):
         return pl.BlockSpec(array.shape, lambda g: (0,) * array.ndim)
@@ -689,7 +678,7 @@
         compiler_params=params,
         cost_estimate=cost,
     )(tile_rank[None], perf_count, flat_perm, *fields, cells)
-    flat_press, flat_sat, partial_rates = pl.pallas_call(
+    press_rows, sat_rows, partial_rates = pl.pallas_call(
         functools.partial(edge_kernel, (local_count, layers, strip_width, tile_count)),
         grid=(local_count // GROUP,),
         in_specs=[smem, whole(low_rows), whole(high_rows)]
@@ -697,16 +686,17 @@
         + [smem, whole(cells), whole(wells), whole(press)]
         + state_specs,
         out_specs=[
-            block, block, pl.BlockSpec((local_count, well_count), lambda g: (0, 0))
+            stacked(rows), stacked(rows),
+            pl.BlockSpec((tile_count, local_count, well_count), lambda g: (0, 0, 0)),
         ],
         out_shape=[
-            f32(*flat_perm.shape), f32(*flat_perm.shape), f32(local_count, well_count)
+            f32(rows, local_count, strip_depth), f32(rows, local_count, strip_depth),
+            f32(tile_count, local_count, well_count),
         ],
         scratch_shapes=[
             pltpu.VMEM((sum(map(len, added.values())), GROUP, strip_depth), jnp.float32),
             pltpu.VMEM((3, local_count, slots), jnp.float32),
             shared_scratch,
-            pltpu.VMEM((rows, GROUP, strip_depth), jnp.float32),
             place_scratch,
         ],
         compiler_params=params,
@@ -714,7 +704,18 @@
     )(
         tile_rank[None], low_rows, high_rows, *fields, perf_count, cells, wells, press, *state
     )
-    own_rates = sum_over(partial_rates, "tile")
+    flat_press, flat_sat = pl.pallas_call(
+        functools.partial(output_kernel, layers, strip_width),
+        grid=(local_count // GROUP,),
+        in_specs=[stacked(rows)] * 2,
+        out_specs=[block] * 2,
+        out_shape=[f32(*flat_perm.shape)] * 2,
+        compiler_params=params,
+        cost_estimate=pl.CostEstimate(
+            flops=10**9, bytes_accessed=16 * flat_perm.size, transcendentals=0
+        ),
+    )(press_rows, sat_rows)
+    own_rates = jnp.sum(lax.all_to_all(partial_rates, "tile", 0, 0), 0)
     rates_all = lax.all_gather(own_rates, "member", axis=0, tiled=True)
     new_flat, well_rates = pl.pallas_call(
         functools.partial(update_kernel, (local_count, layers, strip_width)),
@@ -726,7 +727,7 @@
             pltpu.VMEM(flat_perm.shape, jnp.float32),
             pltpu.SemaphoreType.DMA((2,)),
         ],
-        compiler_params=pltpu.CompilerParams(vmem_limit_bytes=UPDATE_GRANT),
+        compiler_params=pltpu.CompilerParams(vmem_limit_bytes=60 * 2**20),
         cost_estimate=pl.CostEstimate(
             flops=12 * members**3, bytes_accessed=16 * flat_perm.size, transcendentals=0
         ),

time: 69.8 us -> 68.7 us (0.984)
  blocking collectives: 22.3 us -> 5.87 us
  starting transfers between devices: 6.19 us -> 12.8 us
  waiting for transfers between devices: 1.23 us -> 7.82 us
  Pallas kernels: 24.3 us -> 26.4 us
    all_gather x3 -> x0, blocking collectives: 16.2 us -> none  [sum_over(): array = jnp.sum(lax.all_gather(array, axis, axis_index_groups=groups), 0)]
    all_to_all x0 -> x1, waiting for transfers between devices: none -> 6.59 us  [per_device(): own_rates = jnp.sum(lax.all_to_all(partial_rates, 'tile', 0, 0), 0)]
    all_to_all x0 -> x1, starting transfers between devices: none -> 6.57 us  [per_device(): own_rates = jnp.sum(lax.all_to_all(partial_rates, 'tile', 0, 0), 0)]
    pallas_call x0 -> x1, Pallas kernels: none -> 2.64 us  [per_device(): pl.pallas_call(functools.partial(output_kernel, layers, strip_width), gri...]
  transfers between devices with their start and end apart: 3 -> 4, of which waited for: 1 -> 2; matrix products, arithmetic and copies ran while one was open for 0% -> 0% of each run, Pallas kernels for 21% -> 25%
where the time goes in v8:
time: 68.7 us; the launch traced here: 68.3 us
  Pallas kernels  26.4 us (38%)
  between operations  14.7 us (21%)
  starting transfers between devices  12.8 us (19%)
  waiting for transfers between devices  7.82 us (11%)
  blocking collectives  5.87 us (9%)
  local copies, waits for them, and re-layouts  0.77 us (1%)
    pallas_call x1, Pallas kernels, per_device(): pl.pallas_call(functools.partial(edge_kernel, (local_count, layers, strip...  7.35 us
    pallas_call x1, Pallas kernels, per_device(): pl.pallas_call(functools.partial(update_kernel, (local_count, layers, str...  7.18 us
    pallas_call x1, Pallas kernels, per_device(): pl.pallas_call(functools.partial(inner_kernel, (layers, strip_width)), gr...  6.92 us
    all_to_all x1, waiting for transfers between devices, per_device(): own_rates = jnp.sum(lax.all_to_all(partial_rates, 'tile', 0, 0), 0)  6.59 us
    all_to_all x1, starting transfers between devices, per_device(): own_rates = jnp.sum(lax.all_to_all(partial_rates, 'tile', 0, 0), 0)  6.57 us
    all_gather x1, blocking collectives, per_device(): rates_all = lax.all_gather(own_rates, 'member', axis=0, tiled=True)  5.87 us
    ppermute x1, starting transfers between devices, send_both(): lax.ppermute(up_rows, axis, forward)  4.86 us
    pallas_call x1, Pallas kernels, per_device(): pl.pallas_call(functools.partial(output_kernel, layers, strip_width), gri...  2.64 us
  transfers between devices with their start and end apart: 4, of which 2 were waited for; matrix products, arithmetic and copies ran while one was open for 0% of the time, Pallas kernels for 25%

profile of v8, /device:TPU:0, one launch (start us, length us, event | category | flops | bytes accessed | tf_op | source)
XLA Modules:
  0.0 68.3 jit_solution(14629706752162497270)
XLA Ops:
  7.2 0.0 all-gather.2.cloned.1.call-start
  7.2 2.3 %shard_map.147 = (bf16[14,32,256]{2,1,0:T(8,128)(2,1)}, bf16[14,32,256]{2,1,0:T(8,128)(2,1)}, bf16[32,32,256]{2,1,0:T(8,128)(2,1)}) custom-call(f32[2048,128]{1,0:T(8,128)} %bitcast.33, f32[32,256]{1,0:T(8,128)} %bitcast.37, f32[32,256]{1,0:T(8,128)} %bitcast.40, f32[32,256]{1,0:T(8,128)} %bitcast.43, f32[32,256]{1,0:T(8,128)} %bitcast.46), custom_call_target="tpu_custom_call" | custom-call | flops 1048576 | bytes 2097152 | tf_op jit(solution)/shard_map/pallas_call | solution.py:637
  9.5 0.0 all-gather.2.cloned.1.call-update
  9.5 4.9 %collective-permute-start = (bf16[448,256]{1,0:T(8,128)(2,1)}, bf16[448,256]{1,0:T(8,128)(2,1)S(1)}, u32[]{:S(2)}, u32[]{:S(2)}) collective-permute-start(bf16[448,256]{1,0:T(8,128)(2,1)} %bitcast.53), channel_id=1, source_target_pairs={{0,4},{4,8},{8,12},{12,16},{16,20},{20,24},{24,28},{1,5},{5,9},{9,... | collective-permute-start | bytes 688136 | tf_op jit(solution)/shard_map/ppermute | solution.py:71
  14.4 1.3 %collective-permute-start.1 = (bf16[448,256]{1,0:T(8,128)(2,1)}, bf16[448,256]{1,0:T(8,128)(2,1)S(1)}, u32[]{:S(2)}, u32[]{:S(2)}) collective-permute-start(bf16[448,256]{1,0:T(8,128)(2,1)} %bitcast.52), channel_id=1, source_target_pairs={{4,0},{8,4},{12,8},{16,12},{20,16},{24,20},{28,24},{5,1},{9,5},{13... | collective-permute-start | bytes 688136 | tf_op jit(solution)/shard_map/ppermute | solution.py:71
  16.3 6.9 %shard_map.148 = (f32[8,32,256]{2,1,0:T(8,128)}, f32[24,32,256]{2,1,0:T(8,128)}, f32[24,32,256]{2,1,0:T(8,128)}, f32[18,32,256]{2,1,0:T(8,128)}, f32[16,32,256]{...) custom-call(s32[1]{0:T(128)} %bitcast.rank_ref, ...), custom_call_target="tpu_custom_call" | custom-call | flops 10000000000 | bytes 6291456 | tf_op jit(solution)/shard_map/pallas_call | solution.py:667
  23.2 1.2 %collective-permute-done.low_ref = bf16[448,256]{1,0:T(8,128)(2,1)S(1)} collective-permute-done((bf16[448,256]{1,0:T(8,128)(2,1)}, bf16[448,256]{1,0:T(8,128)(2,1)S(1)}, u32[]{:S(2)}, u32[]{:S(2)}) %collective-permute-start) | collective-permute-done | bytes 229408 | tf_op jit(solution)/shard_map/ppermute | solution.py:71
  24.5 0.0 copy-start.1
  24.5 0.0 collective-permute-done.1.high_ref
  24.5 0.0 copy-start.2
  24.5 0.7 %copy-done.1 = bf16[448,256]{1,0:T(8,128)(2,1)} copy-done((bf16[448,256]{1,0:T(8,128)(2,1)}, bf16[448,256]{1,0:T(8,128)(2,1)S(1)}, u32[]{:S(2)}) %copy-start.1) | copy-done | bytes 229400
  25.2 0.1 copy-done.2
  25.2 7.3 %shard_map.149 = (f32[32,32,256]{2,1,0:T(8,128)}, f32[32,32,256]{2,1,0:T(8,128)}, f32[8,32,256]{2,1,0:T(8,128)}) custom-call(s32[1]{0:T(128)} %bitcast.rank_ref, bf16[448,256]{1,0:T(8,128)(2,1)} %copy-done.1, bf16[448,256]{1,0:T(8,128)(2,1)} %copy-done.2, f32[32,256]{1,0:T(8,128)} %bitcast.39, f32[32,256]{1,0:T(8,128)} %bitcast.42, f32[32,256]{1,0:T(8,128)} %bitcast.45, ...), custom_call_target="tpu_custom_call" | custom-call | flops 10000000000 | bytes 6291456 | tf_op jit(solution)/shard_map/pallas_call | solution.py:681
  32.6 6.6 %all-to-all-start = ((f32[8,32,256]{2,1,0:T(8,128)}), f32[8,32,256]{2,1,0:T(8,128)S(1)}, u32[]{:S(2)}, u32[]{:S(2)}) async-start(f32[8,32,256]{2,1,0:T(8,128)} %get-tuple-element.34), calls=%async_computation | async-start | bytes 524288 | tf_op jit(solution)/shard_map/all_to_all | solution.py:718
  39.1 2.6 %shard_map.151 = (f32[2048,128]{1,0:T(8,128)}, f32[2048,128]{1,0:T(8,128)}) custom-call(f32[32,32,256]{2,1,0:T(8,128)} %get-tuple-element.37.refs_0_, f32[32,32,256]{2,1,0:T(8,128)} %get-tuple-element.38.refs_1_), custom_call_target="tpu_custom_call" | custom-call | flops 1000000000 | bytes 4194304 | tf_op jit(solution)/shard_map/pallas_call | solution.py:707
  41.8 6.6 %all-to-all-done = f32[8,32,256]{2,1,0:T(8,128)S(1)} async-done(((f32[8,32,256]{2,1,0:T(8,128)}), f32[8,32,256]{2,1,0:T(8,128)S(1)}, u32[]{:S(2)}, u32[]{:S(2)}) %all-to-all-start) | async-done | bytes 262176 | tf_op jit(solution)/shard_map/all_to_all | solution.py:718
  48.4 0.0 copy-start
  48.4 5.9 %all_gather.6.rates_ref = f32[128,256]{1,0:T(8,128)} all-gather(f32[32,256]{1,0:T(8,128)S(1)} %reduce_sum.9.own_ref), channel_id=1, replica_groups=mesh['tile'=8,'member'=4] {'member'}, dimensions={0}, use_global_device_ids=true | all-gather | bytes 163840 | tf_op jit(solution)/shard_map/all_gather | solution.py:719
  54.3 0.0 all-gather.2.cloned.1.call-done.anomaly_ref
  54.3 0.0 copy-done
  54.3 7.2 %shard_map.150 = (f32[2048,128]{1,0:T(8,128)}, f32[32,32]{1,0:T(8,128)}) custom-call(s32[1]{0:T(128)} %bitcast.rank_ref, f32[128,256]{1,0:T(8,128)} %all_gather.6.rates_ref, f32[32,256]{1,0:T(8,128)} %copy-done, f32[32,256]{1,0:T(8,128)} %noise_ref.1, f32[1,256]{1,0:T(1,128)} %bitcast.49, f32[1,256]{1,0:T(1,128)} %bitcast.50, ...), custom_call_target="tpu_custom_call" | custom-call | flops 25165824 | bytes 4194304 | tf_op jit(solution)/shard_map/pallas_call | solution.py:720
  (1 shorter events, 0.0 us)
Async XLA Ops:
  7.2 47.1 %all-gather.2.cloned.1.call-start = ((), (), s32[]{:S(2)}) async-start(), calls=%async_computation.1 | async-start | bytes 2621440 | tf_op jit(solution)/shard_map/all_gather | solution.py:654
  9.5 14.9 %collective-permute-start = (bf16[448,256]{1,0:T(8,128)(2,1)}, bf16[448,256]{1,0:T(8,128)(2,1)S(1)}, u32[]{:S(2)}, u32[]{:S(2)}) collective-permute-start(bf16[448,256]{1,0:T(8,128)(2,1)} %bitcast.53), channel_id=1, source_target_pairs={{0,4},{4,8},{8,12},{12,16},{16,20},{20,24},{24,28},{1,5},{5,9},{9,... | collective-permute-start | bytes 688136 | tf_op jit(solution)/shard_map/ppermute | solution.py:71
  14.4 10.1 %collective-permute-start.1 = (bf16[448,256]{1,0:T(8,128)(2,1)}, bf16[448,256]{1,0:T(8,128)(2,1)S(1)}, u32[]{:S(2)}, u32[]{:S(2)}) collective-permute-start(bf16[448,256]{1,0:T(8,128)(2,1)} %bitcast.52), channel_id=1, source_target_pairs={{4,0},{8,4},{12,8},{16,12},{20,16},{24,20},{28,24},{5,1},{9,5},{13... | collective-permute-start | bytes 688136 | tf_op jit(solution)/shard_map/ppermute | solution.py:71
  24.5 0.7 %copy-start.1 = (bf16[448,256]{1,0:T(8,128)(2,1)}, bf16[448,256]{1,0:T(8,128)(2,1)S(1)}, u32[]{:S(2)}) copy-start(bf16[448,256]{1,0:T(8,128)(2,1)S(1)} %collective-permute-done.low_ref) | copy-start | bytes 688132
  24.5 0.8 %copy-start.2 = (bf16[448,256]{1,0:T(8,128)(2,1)}, bf16[448,256]{1,0:T(8,128)(2,1)S(1)}, u32[]{:S(2)}) copy-start(bf16[448,256]{1,0:T(8,128)(2,1)S(1)} %collective-permute-done.1.high_ref) | copy-start | bytes 688132
  32.6 15.8 %all-to-all-start = ((f32[8,32,256]{2,1,0:T(8,128)}), f32[8,32,256]{2,1,0:T(8,128)S(1)}, u32[]{:S(2)}, u32[]{:S(2)}) async-start(f32[8,32,256]{2,1,0:T(8,128)} %get-tuple-element.34), calls=%async_computation | async-start | bytes 524288 | tf_op jit(solution)/shard_map/all_to_all | solution.py:718
  48.4 5.9 %copy-start = (f32[32,256]{1,0:T(8,128)}, f32[32,256]{1,0:T(8,128)S(1)}, u32[]{:S(2)}) copy-start(f32[32,256]{1,0:T(8,128)S(1)} %reduce_sum.9.own_ref) | copy-start | bytes 98308
Sparse Core Ops, SparseCore 0:
  9.6 25.2 all-gather.1

commit v9 on v8

--- a/solution.py
+++ b/solution.py
@@ -127,6 +127,7 @@
 
 
 WORK = ("half", "face_x", "face_y", "face_z", "inverse", "first", "last")
+EDGE_NAMES = ("p0", "base", "sat", "frac", "frac_ahead")
 FIELD_NAMES = ("p0", "sat", "storage", "base", "ahead", "behind", "frac", "frac_ahead")
 
 
@@ -274,10 +275,10 @@
     return (part[:GROUP] + part[GROUP : 2 * GROUP]) + part[2 * GROUP :]
 
 
-def put_fields(dest_ref, field_refs):
+def put_fields(dest_ref, field_refs, names):
     fields = derived_fields(*(ref[...] for ref in field_refs))
     rows, depth = field_refs[0].shape
-    for n, name in enumerate(FIELD_NAMES):
+    for n, name in enumerate(names):
         for row in range(rows):
             dest_ref[n * rows + row] = jnp.broadcast_to(fields[name][row : row + 1, :], (8, depth))
 
@@ -295,7 +296,7 @@
 
     @pl.when(pl.program_id(0) == 0)
     def _():
-        put_fields(shared_ref, field_refs)
+        put_fields(shared_ref, field_refs, FIELD_NAMES)
         put_places(place_ref, cell_ref, range(rows), depth)
 
     def field(name, r, layer):
@@ -388,12 +389,12 @@
 
     @pl.when(group == 0)
     def _():
-        put_fields(shared_ref, field_refs)
+        put_fields(shared_ref, field_refs, EDGE_NAMES)
         put_places(place_ref, cell_ref, moved, depth)
 
     def field(name, r, layer):
         if 0 <= r < width:
-            tile = shared_ref[FIELD_NAMES.index(name) * rows + layer * width + r]
+            tile = shared_ref[EDGE_NAMES.index(name) * rows + layer * width + r]
             return jnp.concatenate([tile] * (GROUP // 8), axis=0)
         part, at = (rims[0], r + RIM) if r < 0 else (rims[1], r - width)
         at = layer * RIM + at
@@ -544,7 +545,7 @@
 
 def update_kernel(
     dims, rank_ref, rates_ref, own_ref, noise_ref, observed_ref, var_ref, anomaly_ref, perm_ref,
-    out_ref, held_ref, anomaly_buf, perm_buf, sems,
+    out_ref, held_ref, anomaly_buf, perm_buf, out_buf, sems,
 ):
     local_count, layers, width = dims
     rows = layers * width
@@ -576,6 +577,7 @@
     weights = solve_blocks(gram_matrix, cross_matrix).T.astype(jnp.bfloat16)
     for copy in copies:
         copy.wait()
+    sent = []
     for layer in range(layers):
         updates = []
         for x in range(width):
@@ -590,8 +592,17 @@
             updates.append(jnp.dot(weights, every, preferred_element_type=jnp.float32))
         for h in range(halves):
             rows_of_x = [update[:, h * LANES : (h + 1) * LANES] for update in updates]
-            for where_tile, tile in members_apart(rows_of_x, layer, h, layers, halves):
-                out_ref[where_tile, :] = perm_buf[where_tile, :] + tile
+            tiles = members_apart(rows_of_x, layer, h, layers, halves)
+            for m, (where_tile, tile) in enumerate(tiles):
+                out_buf[m, layer, h * 8 : (h + 1) * 8, :] = perm_buf[where_tile, :] + tile
+        sent.append(
+            pltpu.make_async_copy(
+                out_buf.at[:, layer], out_ref.at[:, layer], sems.at[2 + layer]
+            )
+        )
+        sent[-1].start()
+    for copy in sent:
+        copy.wait()
 
 
 def per_device(
@@ -717,15 +728,17 @@
     )(press_rows, sat_rows)
     own_rates = jnp.sum(lax.all_to_all(partial_rates, "tile", 0, 0), 0)
     rates_all = lax.all_gather(own_rates, "member", axis=0, tiled=True)
+    out_dims = (local_count, layers, rows * (strip_depth // LANES) // layers, LANES)
     new_flat, well_rates = pl.pallas_call(
         functools.partial(update_kernel, (local_count, layers, strip_width)),
-        out_shape=(f32(*flat_perm.shape), f32(local_count, well_share)),
+        out_shape=(f32(*out_dims), f32(local_count, well_share)),
         in_specs=[smem] + [vmem] * 5 + [in_hbm] * 2,
-        out_specs=(vmem, vmem),
+        out_specs=(in_hbm, vmem),
         scratch_shapes=[
             pltpu.VMEM(anomaly_all.shape, jnp.bfloat16),
             pltpu.VMEM(flat_perm.shape, jnp.float32),
-            pltpu.SemaphoreType.DMA((2,)),
+            pltpu.VMEM(out_dims, jnp.float32),
+            pltpu.SemaphoreType.DMA((2 + layers,)),
         ],
         compiler_params=pltpu.CompilerParams(vmem_limit_bytes=60 * 2**20),
         cost_estimate=pl.CostEstimate(

time: 68.7 us -> 69.1 us (level)
  no operation moved by 1% of the time
where the time goes in v9:
time: 69.1 us; the launch traced here: 68.7 us
  Pallas kernels  26.7 us (39%)
  between operations  14.7 us (21%)
  starting transfers between devices  12.8 us (19%)
  waiting for transfers between devices  7.82 us (11%)
  blocking collectives  5.87 us (8%)
  local copies, waits for them, and re-layouts  0.77 us (1%)
    pallas_call x1, Pallas kernels, per_device(): pl.pallas_call(functools.partial(update_kernel, (local_count, layers, str...  7.59 us
    pallas_call x1, Pallas kernels, per_device(): pl.pallas_call(functools.partial(edge_kernel, (local_count, layers, strip...  7.31 us
    pallas_call x1, Pallas kernels, per_device(): pl.pallas_call(functools.partial(inner_kernel, (layers, strip_width)), gr...  6.92 us
    all_to_all x1, waiting for transfers between devices, per_device(): own_rates = jnp.sum(lax.all_to_all(partial_rates, 'tile', 0, 0), 0)  6.59 us
    all_to_all x1, starting transfers between devices, per_device(): own_rates = jnp.sum(lax.all_to_all(partial_rates, 'tile', 0, 0), 0)  6.57 us
    all_gather x1, blocking collectives, per_device(): rates_all = lax.all_gather(own_rates, 'member', axis=0, tiled=True)  5.87 us
    ppermute x1, starting transfers between devices, send_both(): lax.ppermute(up_rows, axis, forward)  4.86 us
    pallas_call x1, Pallas kernels, per_device(): pl.pallas_call(functools.partial(output_kernel, layers, strip_width), gri...  2.64 us
  transfers between devices with their start and end apart: 4, of which 2 were waited for; matrix products, arithmetic and copies ran while one was open for 0% of the time, Pallas kernels for 25%

profile of v9, /device:TPU:0, one launch (start us, length us, event | category | flops | bytes accessed | tf_op | source)
XLA Modules:
  0.0 68.7 jit_solution(13045357765039804359)
XLA Ops:
  7.2 0.0 all-gather.2.cloned.1.call-start
  7.2 2.3 %shard_map.147 = (bf16[14,32,256]{2,1,0:T(8,128)(2,1)}, bf16[14,32,256]{2,1,0:T(8,128)(2,1)}, bf16[32,32,256]{2,1,0:T(8,128)(2,1)}) custom-call(f32[2048,128]{1,0:T(8,128)} %bitcast.33, f32[32,256]{1,0:T(8,128)} %bitcast.37, f32[32,256]{1,0:T(8,128)} %bitcast.40, f32[32,256]{1,0:T(8,128)} %bitcast.43, f32[32,256]{1,0:T(8,128)} %bitcast.46), custom_call_target="tpu_custom_call" | custom-call | flops 1048576 | bytes 2097152 | tf_op jit(solution)/shard_map/pallas_call | solution.py:648
  9.5 0.0 all-gather.2.cloned.1.call-update
  9.5 4.9 %collective-permute-start = (bf16[448,256]{1,0:T(8,128)(2,1)}, bf16[448,256]{1,0:T(8,128)(2,1)S(1)}, u32[]{:S(2)}, u32[]{:S(2)}) collective-permute-start(bf16[448,256]{1,0:T(8,128)(2,1)} %bitcast.53), channel_id=1, source_target_pairs={{0,4},{4,8},{8,12},{12,16},{16,20},{20,24},{24,28},{1,5},{5,9},{9,... | collective-permute-start | bytes 688136 | tf_op jit(solution)/shard_map/ppermute | solution.py:71
  14.4 1.3 %collective-permute-start.1 = (bf16[448,256]{1,0:T(8,128)(2,1)}, bf16[448,256]{1,0:T(8,128)(2,1)S(1)}, u32[]{:S(2)}, u32[]{:S(2)}) collective-permute-start(bf16[448,256]{1,0:T(8,128)(2,1)} %bitcast.52), channel_id=1, source_target_pairs={{4,0},{8,4},{12,8},{16,12},{20,16},{24,20},{28,24},{5,1},{9,5},{13... | collective-permute-start | bytes 688136 | tf_op jit(solution)/shard_map/ppermute | solution.py:71
  16.3 6.9 %shard_map.148 = (f32[8,32,256]{2,1,0:T(8,128)}, f32[24,32,256]{2,1,0:T(8,128)}, f32[24,32,256]{2,1,0:T(8,128)}, f32[18,32,256]{2,1,0:T(8,128)}, f32[16,32,256]{...) custom-call(s32[1]{0:T(128)} %bitcast.rank_ref, ...), custom_call_target="tpu_custom_call" | custom-call | flops 10000000000 | bytes 6291456 | tf_op jit(solution)/shard_map/pallas_call | solution.py:678
  23.2 1.2 %collective-permute-done.low_ref = bf16[448,256]{1,0:T(8,128)(2,1)S(1)} collective-permute-done((bf16[448,256]{1,0:T(8,128)(2,1)}, bf16[448,256]{1,0:T(8,128)(2,1)S(1)}, u32[]{:S(2)}, u32[]{:S(2)}) %collective-permute-start) | collective-permute-done | bytes 229408 | tf_op jit(solution)/shard_map/ppermute | solution.py:71
  24.5 0.0 copy-start.1
  24.5 0.0 collective-permute-done.1.high_ref
  24.5 0.0 copy-start.2
  24.5 0.7 %copy-done.1 = bf16[448,256]{1,0:T(8,128)(2,1)} copy-done((bf16[448,256]{1,0:T(8,128)(2,1)}, bf16[448,256]{1,0:T(8,128)(2,1)S(1)}, u32[]{:S(2)}) %copy-start.1) | copy-done | bytes 229400
  25.2 0.1 copy-done.2
  25.2 7.3 %shard_map.149 = (f32[32,32,256]{2,1,0:T(8,128)}, f32[32,32,256]{2,1,0:T(8,128)}, f32[8,32,256]{2,1,0:T(8,128)}) custom-call(s32[1]{0:T(128)} %bitcast.rank_ref, bf16[448,256]{1,0:T(8,128)(2,1)} %copy-done.1, bf16[448,256]{1,0:T(8,128)(2,1)} %copy-done.2, f32[32,256]{1,0:T(8,128)} %bitcast.39, f32[32,256]{1,0:T(8,128)} %bitcast.42, f32[32,256]{1,0:T(8,128)} %bitcast.45, ...), custom_call_target="tpu_custom_call" | custom-call | flops 10000000000 | bytes 6291456 | tf_op jit(solution)/shard_map/pallas_call | solution.py:692
  32.5 6.6 %all-to-all-start = ((f32[8,32,256]{2,1,0:T(8,128)}), f32[8,32,256]{2,1,0:T(8,128)S(1)}, u32[]{:S(2)}, u32[]{:S(2)}) async-start(f32[8,32,256]{2,1,0:T(8,128)} %get-tuple-element.34), calls=%async_computation | async-start | bytes 524288 | tf_op jit(solution)/shard_map/all_to_all | solution.py:729
  39.1 2.6 %shard_map.151 = (f32[2048,128]{1,0:T(8,128)}, f32[2048,128]{1,0:T(8,128)}) custom-call(f32[32,32,256]{2,1,0:T(8,128)} %get-tuple-element.37.refs_0_, f32[32,32,256]{2,1,0:T(8,128)} %get-tuple-element.38.refs_1_), custom_call_target="tpu_custom_call" | custom-call | flops 1000000000 | bytes 4194304 | tf_op jit(solution)/shard_map/pallas_call | solution.py:718
  41.7 6.6 %all-to-all-done = f32[8,32,256]{2,1,0:T(8,128)S(1)} async-done(((f32[8,32,256]{2,1,0:T(8,128)}), f32[8,32,256]{2,1,0:T(8,128)S(1)}, u32[]{:S(2)}, u32[]{:S(2)}) %all-to-all-start) | async-done | bytes 262176 | tf_op jit(solution)/shard_map/all_to_all | solution.py:729
  48.4 0.0 copy-start
  48.4 5.9 %all_gather.6.rates_ref = f32[128,256]{1,0:T(8,128)} all-gather(f32[32,256]{1,0:T(8,128)S(1)} %reduce_sum.9.own_ref), channel_id=1, replica_groups=mesh['tile'=8,'member'=4] {'member'}, dimensions={0}, use_global_device_ids=true | all-gather | bytes 163840 | tf_op jit(solution)/shard_map/all_gather | solution.py:730
  54.2 0.0 all-gather.2.cloned.1.call-done.anomaly_ref
  54.2 0.0 copy-done
  54.2 7.6 %shard_map.150 = (f32[32,4,16,128]{3,2,1,0:T(8,128)}, f32[32,32]{1,0:T(8,128)}) custom-call(s32[1]{0:T(128)} %bitcast.rank_ref, f32[128,256]{1,0:T(8,128)} %all_gather.6.rates_ref, f32[32,256]{1,0:T(8,128)} %copy-done, f32[32,256]{1,0:T(8,128)} %noise_ref.1, f32[1,256]{1,0:T(1,128)} %bitcast.49, f32[1,256]{1,0:T(1,128)} %bitcast.50, ...), custom_call_target="tpu_custom_call" | custom-call | flops 25165824 | bytes 4194304 | tf_op jit(solution)/shard_map/pallas_call | solution.py:732
  (1 shorter events, 0.0 us)
Async XLA Ops:
  7.2 47.1 %all-gather.2.cloned.1.call-start = ((), (), s32[]{:S(2)}) async-start(), calls=%async_computation.1 | async-start | bytes 2621440 | tf_op jit(solution)/shard_map/all_gather | solution.py:665
  9.5 14.9 %collective-permute-start = (bf16[448,256]{1,0:T(8,128)(2,1)}, bf16[448,256]{1,0:T(8,128)(2,1)S(1)}, u32[]{:S(2)}, u32[]{:S(2)}) collective-permute-start(bf16[448,256]{1,0:T(8,128)(2,1)} %bitcast.53), channel_id=1, source_target_pairs={{0,4},{4,8},{8,12},{12,16},{16,20},{20,24},{24,28},{1,5},{5,9},{9,... | collective-permute-start | bytes 688136 | tf_op jit(solution)/shard_map/ppermute | solution.py:71
  14.4 10.1 %collective-permute-start.1 = (bf16[448,256]{1,0:T(8,128)(2,1)}, bf16[448,256]{1,0:T(8,128)(2,1)S(1)}, u32[]{:S(2)}, u32[]{:S(2)}) collective-permute-start(bf16[448,256]{1,0:T(8,128)(2,1)} %bitcast.52), channel_id=1, source_target_pairs={{4,0},{8,4},{12,8},{16,12},{20,16},{24,20},{28,24},{5,1},{9,5},{13... | collective-permute-start | bytes 688136 | tf_op jit(solution)/shard_map/ppermute | solution.py:71
  24.5 0.7 %copy-start.1 = (bf16[448,256]{1,0:T(8,128)(2,1)}, bf16[448,256]{1,0:T(8,128)(2,1)S(1)}, u32[]{:S(2)}) copy-start(bf16[448,256]{1,0:T(8,128)(2,1)S(1)} %collective-permute-done.low_ref) | copy-start | bytes 688132
  24.5 0.8 %copy-start.2 = (bf16[448,256]{1,0:T(8,128)(2,1)}, bf16[448,256]{1,0:T(8,128)(2,1)S(1)}, u32[]{:S(2)}) copy-start(bf16[448,256]{1,0:T(8,128)(2,1)S(1)} %collective-permute-done.1.high_ref) | copy-start | bytes 688132
  32.5 15.8 %all-to-all-start = ((f32[8,32,256]{2,1,0:T(8,128)}), f32[8,32,256]{2,1,0:T(8,128)S(1)}, u32[]{:S(2)}, u32[]{:S(2)}) async-start(f32[8,32,256]{2,1,0:T(8,128)} %get-tuple-element.34), calls=%async_computation | async-start | bytes 524288 | tf_op jit(solution)/shard_map/all_to_all | solution.py:729
  48.4 5.9 %copy-start = (f32[32,256]{1,0:T(8,128)}, f32[32,256]{1,0:T(8,128)S(1)}, u32[]{:S(2)}) copy-start(f32[32,256]{1,0:T(8,128)S(1)} %reduce_sum.9.own_ref) | copy-start | bytes 98308
Sparse Core Ops, SparseCore 0:
  9.6 25.2 all-gather.1

commit v10 on v8

--- a/solution.py
+++ b/solution.py
@@ -366,8 +366,28 @@
     kept, added = state_slots(layers, width)
     field_refs, count_ref, cell_ref, well_ref, bhp_ref = refs[:4], refs[4], refs[5], refs[6], refs[7]
     refs = refs[8:]
-    states, refs = dict(zip(kept, refs)), refs[len(kept) :]
-    perf_ref, press_ref, moved_ref, rates_ref = refs[:4]
+    sources, refs = refs[: len(kept) + 1], refs[len(kept) + 1 :]
+    sems, buffers, refs = refs[-1], refs[-2 - len(kept) : -1], refs[: -2 - len(kept)]
+    states = dict(zip(kept, buffers))
+    copies = {
+        kind: pltpu.make_async_copy(source, buffer, sems.at[n])
+        for n, (kind, source, buffer) in enumerate(zip([*kept, "perf"], sources, buffers))
+    }
+    perf_ref, refs = buffers[-1], [None, *refs]
+    at_group = pl.ds(pl.multiple_of(group * GROUP, GROUP), GROUP)
+
+    @pl.when(group == 0)
+    def _():
+        for copy in copies.values():
+            copy.start()
+
+    def arrive(*kinds):
+        @pl.when(group == 0)
+        def _():
+            for kind in kinds:
+                copies[kind].wait()
+
+    _, press_ref, moved_ref, rates_ref = refs[:4]
     added_ref, gathered_ref, shared_ref, place_ref = refs[4:]
     rim_rows = RIM * layers * local_count
     has_low = (rank_ref[0] > 0).astype(jnp.float32)
@@ -404,7 +424,7 @@
     def load(kind, r, layer):
         if (r, layer) in added.get(kind, {}):
             return added_ref[added[kind][r, layer]]
-        return states[kind][kept[kind][r, layer]]
+        return states[kind][kept[kind][r, layer], at_group, :]
 
     def store(kind, r, layer, values_in):
         added_ref[added[kind][r, layer]] = values_in
@@ -415,6 +435,7 @@
             at = (i * layers + layer) * local_count + group * GROUP
             values = ref[pl.ds(pl.multiple_of(at, GROUP), GROUP), :].astype(jnp.float32)
             store("half", r, layer, 0.5 * jnp.exp(-values))
+    arrive("half")
     for r in (-3, -2, -1, width - 1, width, width + 1):
         for layer in range(layers):
             face = reciprocal(load("half", r, layer) + load("half", r + 1, layer))
@@ -432,11 +453,12 @@
             bottom = reciprocal(bottom)
             store("first", r, layer, top * bottom)
             store("inverse", r, layer, bottom)
+    arrive(*(kind for kind in copies if kind != "half"))
     for r, face_row, towards in ((0, -1, -1), (width - 1, width - 1, width)):
         for layer in range(layers):
             face = load("face_x", face_row, layer)
-            top = states["first"][kept["first"][r, layer]]
-            bottom = states["inverse"][kept["inverse"][r, layer]]
+            top = states["first"][kept["first"][r, layer], at_group, :]
+            bottom = states["inverse"][kept["inverse"][r, layer], at_group, :]
             bottom = reciprocal(bottom + face)
             store("first", r, layer, (top + face * field("p0", towards, layer)) * bottom)
             store("inverse", r, layer, bottom)
@@ -460,8 +482,10 @@
             values_of.append((1, load("last", r, layer)))
         find(found, values_of, place_ref[i * depth : (i + 1) * depth, :])
     for n in range(3):
-        total = perf_ref[n] if found[n] is None else perf_ref[n] + joined(found[n])
-        gathered_ref[n, pl.ds(pl.multiple_of(group * GROUP, GROUP), GROUP), :] = total
+        total = perf_ref[n, at_group, :]
+        if found[n] is not None:
+            total = total + joined(found[n])
+        gathered_ref[n, at_group, :] = total
 
     @pl.when(group == local_count // GROUP - 1)
     def _():
@@ -684,7 +708,7 @@
         in_specs=[smem, whole(low_rows), whole(high_rows)]
         + [whole(array) for array in fields]
         + [smem, whole(cells), whole(wells), whole(press)]
-        + state_specs,
+        + [in_hbm] * len(state),
         out_specs=[
             stacked(rows), stacked(rows),
             pl.BlockSpec((tile_count, local_count, well_count), lambda g: (0, 0, 0)),
@@ -698,6 +722,8 @@
             pltpu.VMEM((3, local_count, slots), jnp.float32),
             shared_scratch,
             place_scratch,
+            *(pltpu.VMEM(array.shape, jnp.float32) for array in state),
+            pltpu.SemaphoreType.DMA((len(state),)),
         ],
         compiler_params=params,
         cost_estimate=cost,

time: 68.7 us -> 69.1 us (level)
  no operation moved by 1% of the time
where the time goes in v10:
time: 69.1 us; the launch traced here: 68.7 us
  Pallas kernels  26.7 us (39%)
  between operations  14.7 us (21%)
  starting transfers between devices  12.8 us (19%)
  waiting for transfers between devices  7.8 us (11%)
  blocking collectives  5.87 us (8%)
  local copies, waits for them, and re-layouts  0.77 us (1%)
    pallas_call x1, Pallas kernels, per_device(): pl.pallas_call(functools.partial(edge_kernel, (local_count, layers, strip...  7.7 us
    pallas_call x1, Pallas kernels, per_device(): pl.pallas_call(functools.partial(update_kernel, (local_count, layers, str...  7.18 us
    pallas_call x1, Pallas kernels, per_device(): pl.pallas_call(functools.partial(inner_kernel, (layers, strip_width)), gr...  6.92 us
    all_to_all x1, starting transfers between devices, per_device(): own_rates = jnp.sum(lax.all_to_all(partial_rates, 'tile', 0, 0), 0)  6.58 us
    all_to_all x1, waiting for transfers between devices, per_device(): own_rates = jnp.sum(lax.all_to_all(partial_rates, 'tile', 0, 0), 0)  6.57 us
    all_gather x1, blocking collectives, per_device(): rates_all = lax.all_gather(own_rates, 'member', axis=0, tiled=True)  5.87 us
    ppermute x1, starting transfers between devices, send_both(): lax.ppermute(up_rows, axis, forward)  4.86 us
    pallas_call x1, Pallas kernels, per_device(): pl.pallas_call(functools.partial(output_kernel, layers, strip_width), gri...  2.64 us
  transfers between devices with their start and end apart: 4, of which 2 were waited for; matrix products, arithmetic and copies ran while one was open for 0% of the time, Pallas kernels for 25%

profile of v10, /device:TPU:0, one launch (start us, length us, event | category | flops | bytes accessed | tf_op | source)
XLA Modules:
  0.0 68.7 jit_solution(4275017733451933127)
XLA Ops:
  7.2 0.0 all-gather.2.cloned.1.call-start
  7.2 2.3 %shard_map.147 = (bf16[14,32,256]{2,1,0:T(8,128)(2,1)}, bf16[14,32,256]{2,1,0:T(8,128)(2,1)}, bf16[32,32,256]{2,1,0:T(8,128)(2,1)}) custom-call(f32[2048,128]{1,0:T(8,128)} %bitcast.33, f32[32,256]{1,0:T(8,128)} %bitcast.37, f32[32,256]{1,0:T(8,128)} %bitcast.40, f32[32,256]{1,0:T(8,128)} %bitcast.43, f32[32,256]{1,0:T(8,128)} %bitcast.46), custom_call_target="tpu_custom_call" | custom-call | flops 1048576 | bytes 2097152 | tf_op jit(solution)/shard_map/pallas_call | solution.py:661
  9.5 0.0 all-gather.2.cloned.1.call-update
  9.5 4.9 %collective-permute-start = (bf16[448,256]{1,0:T(8,128)(2,1)}, bf16[448,256]{1,0:T(8,128)(2,1)S(1)}, u32[]{:S(2)}, u32[]{:S(2)}) collective-permute-start(bf16[448,256]{1,0:T(8,128)(2,1)} %bitcast.53), channel_id=1, source_target_pairs={{0,4},{4,8},{8,12},{12,16},{16,20},{20,24},{24,28},{1,5},{5,9},{9,... | collective-permute-start | bytes 688136 | tf_op jit(solution)/shard_map/ppermute | solution.py:71
  14.4 1.3 %collective-permute-start.1 = (bf16[448,256]{1,0:T(8,128)(2,1)}, bf16[448,256]{1,0:T(8,128)(2,1)S(1)}, u32[]{:S(2)}, u32[]{:S(2)}) collective-permute-start(bf16[448,256]{1,0:T(8,128)(2,1)} %bitcast.52), channel_id=1, source_target_pairs={{4,0},{8,4},{12,8},{16,12},{20,16},{24,20},{28,24},{5,1},{9,5},{13... | collective-permute-start | bytes 688136 | tf_op jit(solution)/shard_map/ppermute | solution.py:71
  16.3 6.9 %shard_map.148 = (f32[8,32,256]{2,1,0:T(8,128)}, f32[24,32,256]{2,1,0:T(8,128)}, f32[24,32,256]{2,1,0:T(8,128)}, f32[18,32,256]{2,1,0:T(8,128)}, f32[16,32,256]{...) custom-call(s32[1]{0:T(128)} %bitcast.rank_ref, ...), custom_call_target="tpu_custom_call" | custom-call | flops 10000000000 | bytes 6291456 | tf_op jit(solution)/shard_map/pallas_call | solution.py:691
  23.2 1.2 %collective-permute-done.low_ref = bf16[448,256]{1,0:T(8,128)(2,1)S(1)} collective-permute-done((bf16[448,256]{1,0:T(8,128)(2,1)}, bf16[448,256]{1,0:T(8,128)(2,1)S(1)}, u32[]{:S(2)}, u32[]{:S(2)}) %collective-permute-start) | collective-permute-done | bytes 229408 | tf_op jit(solution)/shard_map/ppermute | solution.py:71
  24.5 0.0 copy-start.1
  24.5 0.0 collective-permute-done.1.high_ref
  24.5 0.0 copy-start.2
  24.5 0.7 %copy-done.1 = bf16[448,256]{1,0:T(8,128)(2,1)} copy-done((bf16[448,256]{1,0:T(8,128)(2,1)}, bf16[448,256]{1,0:T(8,128)(2,1)S(1)}, u32[]{:S(2)}) %copy-start.1) | copy-done | bytes 229400
  25.2 0.1 copy-done.2
  25.2 7.7 %shard_map.149 = (f32[32,32,256]{2,1,0:T(8,128)}, f32[32,32,256]{2,1,0:T(8,128)}, f32[8,32,256]{2,1,0:T(8,128)}) custom-call(s32[1]{0:T(128)} %bitcast.rank_ref, bf16[448,256]{1,0:T(8,128)(2,1)} %copy-done.1, bf16[448,256]{1,0:T(8,128)(2,1)} %copy-done.2, f32[32,256]{1,0:T(8,128)} %bitcast.39, f32[32,256]{1,0:T(8,128)} %bitcast.42, f32[32,256]{1,0:T(8,128)} %bitcast.45, ...), custom_call_target="tpu_custom_call" | custom-call | flops 10000000000 | bytes 6291456 | tf_op jit(solution)/shard_map/pallas_call | solution.py:705
  32.9 6.6 %all-to-all-start = ((f32[8,32,256]{2,1,0:T(8,128)}), f32[8,32,256]{2,1,0:T(8,128)S(1)}, u32[]{:S(2)}, u32[]{:S(2)}) async-start(f32[8,32,256]{2,1,0:T(8,128)} %get-tuple-element.34), calls=%async_computation | async-start | bytes 524288 | tf_op jit(solution)/shard_map/all_to_all | solution.py:744
  39.5 2.6 %shard_map.151 = (f32[2048,128]{1,0:T(8,128)}, f32[2048,128]{1,0:T(8,128)}) custom-call(f32[32,32,256]{2,1,0:T(8,128)} %get-tuple-element.37.refs_0_, f32[32,32,256]{2,1,0:T(8,128)} %get-tuple-element.38.refs_1_), custom_call_target="tpu_custom_call" | custom-call | flops 1000000000 | bytes 4194304 | tf_op jit(solution)/shard_map/pallas_call | solution.py:733
  42.1 6.6 %all-to-all-done = f32[8,32,256]{2,1,0:T(8,128)S(1)} async-done(((f32[8,32,256]{2,1,0:T(8,128)}), f32[8,32,256]{2,1,0:T(8,128)S(1)}, u32[]{:S(2)}, u32[]{:S(2)}) %all-to-all-start) | async-done | bytes 262176 | tf_op jit(solution)/shard_map/all_to_all | solution.py:744
  48.7 0.0 copy-start
  48.8 5.9 %all_gather.6.rates_ref = f32[128,256]{1,0:T(8,128)} all-gather(f32[32,256]{1,0:T(8,128)S(1)} %reduce_sum.9.own_ref), channel_id=1, replica_groups=mesh['tile'=8,'member'=4] {'member'}, dimensions={0}, use_global_device_ids=true | all-gather | bytes 163840 | tf_op jit(solution)/shard_map/all_gather | solution.py:745
  54.6 0.0 all-gather.2.cloned.1.call-done.anomaly_ref
  54.6 0.0 copy-done
  54.6 7.2 %shard_map.150 = (f32[2048,128]{1,0:T(8,128)}, f32[32,32]{1,0:T(8,128)}) custom-call(s32[1]{0:T(128)} %bitcast.rank_ref, f32[128,256]{1,0:T(8,128)} %all_gather.6.rates_ref, f32[32,256]{1,0:T(8,128)} %copy-done, f32[32,256]{1,0:T(8,128)} %noise_ref.1, f32[1,256]{1,0:T(1,128)} %bitcast.49, f32[1,256]{1,0:T(1,128)} %bitcast.50, ...), custom_call_target="tpu_custom_call" | custom-call | flops 25165824 | bytes 4194304 | tf_op jit(solution)/shard_map/pallas_call | solution.py:746
  (1 shorter events, 0.0 us)
Async XLA Ops:
  7.2 47.5 %all-gather.2.cloned.1.call-start = ((), (), s32[]{:S(2)}) async-start(), calls=%async_computation.1 | async-start | bytes 2621440 | tf_op jit(solution)/shard_map/all_gather | solution.py:678
  9.5 14.9 %collective-permute-start = (bf16[448,256]{1,0:T(8,128)(2,1)}, bf16[448,256]{1,0:T(8,128)(2,1)S(1)}, u32[]{:S(2)}, u32[]{:S(2)}) collective-permute-start(bf16[448,256]{1,0:T(8,128)(2,1)} %bitcast.53), channel_id=1, source_target_pairs={{0,4},{4,8},{8,12},{12,16},{16,20},{20,24},{24,28},{1,5},{5,9},{9,... | collective-permute-start | bytes 688136 | tf_op jit(solution)/shard_map/ppermute | solution.py:71
  14.4 10.1 %collective-permute-start.1 = (bf16[448,256]{1,0:T(8,128)(2,1)}, bf16[448,256]{1,0:T(8,128)(2,1)S(1)}, u32[]{:S(2)}, u32[]{:S(2)}) collective-permute-start(bf16[448,256]{1,0:T(8,128)(2,1)} %bitcast.52), channel_id=1, source_target_pairs={{4,0},{8,4},{12,8},{16,12},{20,16},{24,20},{28,24},{5,1},{9,5},{13... | collective-permute-start | bytes 688136 | tf_op jit(solution)/shard_map/ppermute | solution.py:71
  24.5 0.7 %copy-start.1 = (bf16[448,256]{1,0:T(8,128)(2,1)}, bf16[448,256]{1,0:T(8,128)(2,1)S(1)}, u32[]{:S(2)}) copy-start(bf16[448,256]{1,0:T(8,128)(2,1)S(1)} %collective-permute-done.low_ref) | copy-start | bytes 688132
  24.5 0.8 %copy-start.2 = (bf16[448,256]{1,0:T(8,128)(2,1)}, bf16[448,256]{1,0:T(8,128)(2,1)S(1)}, u32[]{:S(2)}) copy-start(bf16[448,256]{1,0:T(8,128)(2,1)S(1)} %collective-permute-done.1.high_ref) | copy-start | bytes 688132
  32.9 15.8 %all-to-all-start = ((f32[8,32,256]{2,1,0:T(8,128)}), f32[8,32,256]{2,1,0:T(8,128)S(1)}, u32[]{:S(2)}, u32[]{:S(2)}) async-start(f32[8,32,256]{2,1,0:T(8,128)} %get-tuple-element.34), calls=%async_computation | async-start | bytes 524288 | tf_op jit(solution)/shard_map/all_to_all | solution.py:744
  48.7 5.9 %copy-start = (f32[32,256]{1,0:T(8,128)}, f32[32,256]{1,0:T(8,128)S(1)}, u32[]{:S(2)}) copy-start(f32[32,256]{1,0:T(8,128)S(1)} %reduce_sum.9.own_ref) | copy-start | bytes 98308
Sparse Core Ops, SparseCore 0:
  9.6 25.2 all-gather.1

commit v11 on v8

--- a/solution.py
+++ b/solution.py
@@ -76,9 +76,9 @@
     return guess * (2.0 - values_in * guess)
 
 
-def pieces(values_in):
+def pieces(values_in, count=3):
     parts = []
-    for _ in range(3):
+    for _ in range(count):
         parts.append(values_in.astype(jnp.bfloat16))
         values_in = values_in - parts[-1].astype(jnp.float32)
     return jnp.concatenate(parts, axis=0)
@@ -127,6 +127,7 @@
 
 
 WORK = ("half", "face_x", "face_y", "face_z", "inverse", "first", "last")
+EDGE_NAMES = ("p0", "base", "sat", "frac", "frac_ahead")
 FIELD_NAMES = ("p0", "sat", "storage", "base", "ahead", "behind", "frac", "frac_ahead")
 
 
@@ -263,21 +264,21 @@
 
 
 def find(found, values_of, place):
-    every = jnp.concatenate([pieces(values) for _, values in values_of], axis=0)
+    every = jnp.concatenate([pieces(values, 2) for _, values in values_of], axis=0)
     sums = jnp.dot(every, place, preferred_element_type=jnp.float32)
     for i, (n, _) in enumerate(values_of):
-        part = sums[i * 3 * GROUP : (i + 1) * 3 * GROUP]
+        part = sums[i * 2 * GROUP : (i + 1) * 2 * GROUP]
         found[n] = part if found[n] is None else found[n] + part
 
 
 def joined(part):
-    return (part[:GROUP] + part[GROUP : 2 * GROUP]) + part[2 * GROUP :]
-
-
-def put_fields(dest_ref, field_refs):
+    return part[:GROUP] + part[GROUP:]
+
+
+def put_fields(dest_ref, field_refs, names):
     fields = derived_fields(*(ref[...] for ref in field_refs))
     rows, depth = field_refs[0].shape
-    for n, name in enumerate(FIELD_NAMES):
+    for n, name in enumerate(names):
         for row in range(rows):
             dest_ref[n * rows + row] = jnp.broadcast_to(fields[name][row : row + 1, :], (8, depth))
 
@@ -295,7 +296,7 @@
 
     @pl.when(pl.program_id(0) == 0)
     def _():
-        put_fields(shared_ref, field_refs)
+        put_fields(shared_ref, field_refs, FIELD_NAMES)
         put_places(place_ref, cell_ref, range(rows), depth)
 
     def field(name, r, layer):
@@ -388,12 +389,12 @@
 
     @pl.when(group == 0)
     def _():
-        put_fields(shared_ref, field_refs)
+        put_fields(shared_ref, field_refs, EDGE_NAMES)
         put_places(place_ref, cell_ref, moved, depth)
 
     def field(name, r, layer):
         if 0 <= r < width:
-            tile = shared_ref[FIELD_NAMES.index(name) * rows + layer * width + r]
+            tile = shared_ref[EDGE_NAMES.index(name) * rows + layer * width + r]
             return jnp.concatenate([tile] * (GROUP // 8), axis=0)
         part, at = (rims[0], r + RIM) if r < 0 else (rims[1], r - width)
         at = layer * RIM + at

time: 68.7 us -> 68.6 us (level)
  transfers between devices with their start and end apart: 4 -> 4, of which waited for: 2 -> 2; matrix products, arithmetic and copies ran while one was open for 0% -> 0% of each run, Pallas kernels for 25% -> 24%
where the time goes in v11:
time: 68.6 us; the launch traced here: 68.2 us
  Pallas kernels  26 us (38%)
  between operations  14.7 us (21%)
  starting transfers between devices  12.8 us (19%)
  waiting for transfers between devices  8.02 us (12%)
  blocking collectives  5.87 us (9%)
  local copies, waits for them, and re-layouts  0.77 us (1%)
    pallas_call x1, Pallas kernels, per_device(): pl.pallas_call(functools.partial(edge_kernel, (local_count, layers, strip...  7.22 us
    pallas_call x1, Pallas kernels, per_device(): pl.pallas_call(functools.partial(update_kernel, (local_count, layers, str...  7.18 us
    pallas_call x1, Pallas kernels, per_device(): pl.pallas_call(functools.partial(inner_kernel, (layers, strip_width)), gr...  6.71 us
    all_to_all x1, waiting for transfers between devices, per_device(): own_rates = jnp.sum(lax.all_to_all(partial_rates, 'tile', 0, 0), 0)  6.59 us
    all_to_all x1, starting transfers between devices, per_device(): own_rates = jnp.sum(lax.all_to_all(partial_rates, 'tile', 0, 0), 0)  6.57 us
    all_gather x1, blocking collectives, per_device(): rates_all = lax.all_gather(own_rates, 'member', axis=0, tiled=True)  5.87 us
    ppermute x1, starting transfers between devices, send_both(): lax.ppermute(up_rows, axis, forward)  4.86 us
    pallas_call x1, Pallas kernels, per_device(): pl.pallas_call(functools.partial(output_kernel, layers, strip_width), gri...  2.64 us
  transfers between devices with their start and end apart: 4, of which 2 were waited for; matrix products, arithmetic and copies ran while one was open for 0% of the time, Pallas kernels for 24%

profile of v11, /device:TPU:0, one launch (start us, length us, event | category | flops | bytes accessed | tf_op | source)
XLA Modules:
  0.0 68.2 jit_solution(61024314386757690)
XLA Ops:
  7.2 0.0 all-gather.2.cloned.1.call-start
  7.2 2.3 %shard_map.147 = (bf16[14,32,256]{2,1,0:T(8,128)(2,1)}, bf16[14,32,256]{2,1,0:T(8,128)(2,1)}, bf16[32,32,256]{2,1,0:T(8,128)(2,1)}) custom-call(f32[2048,128]{1,0:T(8,128)} %bitcast.33, f32[32,256]{1,0:T(8,128)} %bitcast.37, f32[32,256]{1,0:T(8,128)} %bitcast.40, f32[32,256]{1,0:T(8,128)} %bitcast.43, f32[32,256]{1,0:T(8,128)} %bitcast.46), custom_call_target="tpu_custom_call" | custom-call | flops 1048576 | bytes 2097152 | tf_op jit(solution)/shard_map/pallas_call | solution.py:638
  9.5 0.0 all-gather.2.cloned.1.call-update
  9.5 4.9 %collective-permute-start = (bf16[448,256]{1,0:T(8,128)(2,1)}, bf16[448,256]{1,0:T(8,128)(2,1)S(1)}, u32[]{:S(2)}, u32[]{:S(2)}) collective-permute-start(bf16[448,256]{1,0:T(8,128)(2,1)} %bitcast.53), channel_id=1, source_target_pairs={{0,4},{4,8},{8,12},{12,16},{16,20},{20,24},{24,28},{1,5},{5,9},{9,... | collective-permute-start | bytes 688136 | tf_op jit(solution)/shard_map/ppermute | solution.py:71
  14.4 1.3 %collective-permute-start.1 = (bf16[448,256]{1,0:T(8,128)(2,1)}, bf16[448,256]{1,0:T(8,128)(2,1)S(1)}, u32[]{:S(2)}, u32[]{:S(2)}) collective-permute-start(bf16[448,256]{1,0:T(8,128)(2,1)} %bitcast.52), channel_id=1, source_target_pairs={{4,0},{8,4},{12,8},{16,12},{20,16},{24,20},{28,24},{5,1},{9,5},{13... | collective-permute-start | bytes 688136 | tf_op jit(solution)/shard_map/ppermute | solution.py:71
  16.3 6.7 %shard_map.148 = (f32[8,32,256]{2,1,0:T(8,128)}, f32[24,32,256]{2,1,0:T(8,128)}, f32[24,32,256]{2,1,0:T(8,128)}, f32[18,32,256]{2,1,0:T(8,128)}, f32[16,32,256]{...) custom-call(s32[1]{0:T(128)} %bitcast.rank_ref, ...), custom_call_target="tpu_custom_call" | custom-call | flops 10000000000 | bytes 6291456 | tf_op jit(solution)/shard_map/pallas_call | solution.py:668
  23.0 1.4 %collective-permute-done.low_ref = bf16[448,256]{1,0:T(8,128)(2,1)S(1)} collective-permute-done((bf16[448,256]{1,0:T(8,128)(2,1)}, bf16[448,256]{1,0:T(8,128)(2,1)S(1)}, u32[]{:S(2)}, u32[]{:S(2)}) %collective-permute-start) | collective-permute-done | bytes 229408 | tf_op jit(solution)/shard_map/ppermute | solution.py:71
  24.5 0.0 copy-start.1
  24.5 0.0 collective-permute-done.1.high_ref
  24.5 0.0 copy-start.2
  24.5 0.7 %copy-done.1 = bf16[448,256]{1,0:T(8,128)(2,1)} copy-done((bf16[448,256]{1,0:T(8,128)(2,1)}, bf16[448,256]{1,0:T(8,128)(2,1)S(1)}, u32[]{:S(2)}) %copy-start.1) | copy-done | bytes 229400
  25.2 0.1 copy-done.2
  25.2 7.2 %shard_map.149 = (f32[32,32,256]{2,1,0:T(8,128)}, f32[32,32,256]{2,1,0:T(8,128)}, f32[8,32,256]{2,1,0:T(8,128)}) custom-call(s32[1]{0:T(128)} %bitcast.rank_ref, bf16[448,256]{1,0:T(8,128)(2,1)} %copy-done.1, bf16[448,256]{1,0:T(8,128)(2,1)} %copy-done.2, f32[32,256]{1,0:T(8,128)} %bitcast.39, f32[32,256]{1,0:T(8,128)} %bitcast.42, f32[32,256]{1,0:T(8,128)} %bitcast.45, ...), custom_call_target="tpu_custom_call" | custom-call | flops 10000000000 | bytes 6291456 | tf_op jit(solution)/shard_map/pallas_call | solution.py:682
  32.4 6.6 %all-to-all-start = ((f32[8,32,256]{2,1,0:T(8,128)}), f32[8,32,256]{2,1,0:T(8,128)S(1)}, u32[]{:S(2)}, u32[]{:S(2)}) async-start(f32[8,32,256]{2,1,0:T(8,128)} %get-tuple-element.34), calls=%async_computation | async-start | bytes 524288 | tf_op jit(solution)/shard_map/all_to_all | solution.py:719
  39.0 2.6 %shard_map.151 = (f32[2048,128]{1,0:T(8,128)}, f32[2048,128]{1,0:T(8,128)}) custom-call(f32[32,32,256]{2,1,0:T(8,128)} %get-tuple-element.37.refs_0_, f32[32,32,256]{2,1,0:T(8,128)} %get-tuple-element.38.refs_1_), custom_call_target="tpu_custom_call" | custom-call | flops 1000000000 | bytes 4194304 | tf_op jit(solution)/shard_map/pallas_call | solution.py:708
  41.6 6.6 %all-to-all-done = f32[8,32,256]{2,1,0:T(8,128)S(1)} async-done(((f32[8,32,256]{2,1,0:T(8,128)}), f32[8,32,256]{2,1,0:T(8,128)S(1)}, u32[]{:S(2)}, u32[]{:S(2)}) %all-to-all-start) | async-done | bytes 262176 | tf_op jit(solution)/shard_map/all_to_all | solution.py:719
  48.3 0.0 copy-start
  48.3 5.9 %all_gather.6.rates_ref = f32[128,256]{1,0:T(8,128)} all-gather(f32[32,256]{1,0:T(8,128)S(1)} %reduce_sum.9.own_ref), channel_id=1, replica_groups=mesh['tile'=8,'member'=4] {'member'}, dimensions={0}, use_global_device_ids=true | all-gather | bytes 163840 | tf_op jit(solution)/shard_map/all_gather | solution.py:720
  54.1 0.0 all-gather.2.cloned.1.call-done.anomaly_ref
  54.1 0.0 copy-done
  54.1 7.2 %shard_map.150 = (f32[2048,128]{1,0:T(8,128)}, f32[32,32]{1,0:T(8,128)}) custom-call(s32[1]{0:T(128)} %bitcast.rank_ref, f32[128,256]{1,0:T(8,128)} %all_gather.6.rates_ref, f32[32,256]{1,0:T(8,128)} %copy-done, f32[32,256]{1,0:T(8,128)} %noise_ref.1, f32[1,256]{1,0:T(1,128)} %bitcast.49, f32[1,256]{1,0:T(1,128)} %bitcast.50, ...), custom_call_target="tpu_custom_call" | custom-call | flops 25165824 | bytes 4194304 | tf_op jit(solution)/shard_map/pallas_call | solution.py:721
  (1 shorter events, 0.0 us)
Async XLA Ops:
  7.2 47.0 %all-gather.2.cloned.1.call-start = ((), (), s32[]{:S(2)}) async-start(), calls=%async_computation.1 | async-start | bytes 2621440 | tf_op jit(solution)/shard_map/all_gather | solution.py:655
  9.5 14.9 %collective-permute-start = (bf16[448,256]{1,0:T(8,128)(2,1)}, bf16[448,256]{1,0:T(8,128)(2,1)S(1)}, u32[]{:S(2)}, u32[]{:S(2)}) collective-permute-start(bf16[448,256]{1,0:T(8,128)(2,1)} %bitcast.53), channel_id=1, source_target_pairs={{0,4},{4,8},{8,12},{12,16},{16,20},{20,24},{24,28},{1,5},{5,9},{9,... | collective-permute-start | bytes 688136 | tf_op jit(solution)/shard_map/ppermute | solution.py:71
  14.4 10.1 %collective-permute-start.1 = (bf16[448,256]{1,0:T(8,128)(2,1)}, bf16[448,256]{1,0:T(8,128)(2,1)S(1)}, u32[]{:S(2)}, u32[]{:S(2)}) collective-permute-start(bf16[448,256]{1,0:T(8,128)(2,1)} %bitcast.52), channel_id=1, source_target_pairs={{4,0},{8,4},{12,8},{16,12},{20,16},{24,20},{28,24},{5,1},{9,5},{13... | collective-permute-start | bytes 688136 | tf_op jit(solution)/shard_map/ppermute | solution.py:71
  24.5 0.7 %copy-start.1 = (bf16[448,256]{1,0:T(8,128)(2,1)}, bf16[448,256]{1,0:T(8,128)(2,1)S(1)}, u32[]{:S(2)}) copy-start(bf16[448,256]{1,0:T(8,128)(2,1)S(1)} %collective-permute-done.low_ref) | copy-start | bytes 688132
  24.5 0.8 %copy-start.2 = (bf16[448,256]{1,0:T(8,128)(2,1)}, bf16[448,256]{1,0:T(8,128)(2,1)S(1)}, u32[]{:S(2)}) copy-start(bf16[448,256]{1,0:T(8,128)(2,1)S(1)} %collective-permute-done.1.high_ref) | copy-start | bytes 688132
  32.4 15.8 %all-to-all-start = ((f32[8,32,256]{2,1,0:T(8,128)}), f32[8,32,256]{2,1,0:T(8,128)S(1)}, u32[]{:S(2)}, u32[]{:S(2)}) async-start(f32[8,32,256]{2,1,0:T(8,128)} %get-tuple-element.34), calls=%async_computation | async-start | bytes 524288 | tf_op jit(solution)/shard_map/all_to_all | solution.py:719
  48.3 5.9 %copy-start = (f32[32,256]{1,0:T(8,128)}, f32[32,256]{1,0:T(8,128)S(1)}, u32[]{:S(2)}) copy-start(f32[32,256]{1,0:T(8,128)S(1)} %reduce_sum.9.own_ref) | copy-start | bytes 98308
Sparse Core Ops, SparseCore 0:
  9.6 25.2 all-gather.1
